TPU v7x, 32 devices: a whole 2x2x4 slice. The times are simulated.
32 devices in a mesh: ctx: 8 (over y, x, core), fsdp: 4 (over z).
Axes of the slice: x: 2, y: 2, z: 4, core: 2. Of those that a mesh axis runs over, the one named last changes fastest.
Arguments:
- tokens: bfloat16 [4, 1024, 1536], P('fsdp', 'ctx'), may hold values from -6 to 6
- cotangent: bfloat16 [4, 1024, 1536], P('fsdp', 'ctx'), may hold values from -6 to 6
- block_position: int32 [16], replicated, may hold values from 0 to 15, as said below
- w_query: bfloat16 [1536, 1536], P(('ctx', 'fsdp')), may hold values from -0.15625 to 0.15625
- key_weight: bfloat16 [1536, 256], P(('ctx', 'fsdp')), may hold values from -0.15625 to 0.15625
- value_weight: bfloat16 [1536, 256], P(('ctx', 'fsdp')), may hold values from -0.15625 to 0.15625
- w_output: bfloat16 [1536, 1536], P(('ctx', 'fsdp')), may hold values from -2.5 to 2.5
- w_gate: bfloat16 [8960, 1536], P(('ctx', 'fsdp')), may hold values from -0.15625 to 0.15625
- w_up: bfloat16 [8960, 1536], P(('ctx', 'fsdp')), may hold values from -0.15625 to 0.15625
- w_down: bfloat16 [8960, 1536], P(('ctx', 'fsdp')), may hold values from -0.0625 to 0.0625
- projection_bias: bfloat16 [2048], replicated, may hold values from -3 to 3
- norm_gains: bfloat16 [2, 1536], replicated, may hold values from 0.5 to 1.5
- momentum_query: float32 [1536, 1536], P(('ctx', 'fsdp')), may hold values from -112 to 112
- key_momentum: float32 [1536, 256], P(('ctx', 'fsdp')), may hold values from -112 to 112
- value_momentum: float32 [1536, 256], P(('ctx', 'fsdp')), may hold values from -112 to 112
- momentum_output: float32 [1536, 1536], P(('ctx', 'fsdp')), may hold values from -112 to 112
- momentum_gate: float32 [8960, 1536], P(('ctx', 'fsdp')), may hold values from -112 to 112
- momentum_up: float32 [8960, 1536], P(('ctx', 'fsdp')), may hold values from -112 to 112
- momentum_down: float32 [8960, 1536], P(('ctx', 'fsdp')), may hold values from -112 to 112
- bias_momentum: float32 [2048], replicated, may hold values from -112 to 112
- momentum_gains: float32 [2, 1536], replicated, may hold values from -112 to 112
Outputs:
- out_tokens: bfloat16 [4, 1024, 1536], P('fsdp', 'ctx')
- grad_tokens: float32 [4, 1024, 1536], P('fsdp', 'ctx')
- grad_query: float32 [1536, 1536], P(('ctx', 'fsdp'))
- grad_key: float32 [1536, 256], P(('ctx', 'fsdp'))
- grad_value: float32 [1536, 256], P(('ctx', 'fsdp'))
- grad_output: float32 [1536, 1536], P(('ctx', 'fsdp'))
- grad_gate: float32 [8960, 1536], P(('ctx', 'fsdp'))
- grad_up: float32 [8960, 1536], P(('ctx', 'fsdp'))
- grad_down: float32 [8960, 1536], P(('ctx', 'fsdp'))
- moment_query: float32 [1536, 1536], P(('ctx', 'fsdp'))
- moment_key: float32 [1536, 256], P(('ctx', 'fsdp'))
- moment_value: float32 [1536, 256], P(('ctx', 'fsdp'))
- moment_output: float32 [1536, 1536], P(('ctx', 'fsdp'))
- moment_gate: float32 [8960, 1536], P(('ctx', 'fsdp'))
- moment_up: float32 [8960, 1536], P(('ctx', 'fsdp'))
- moment_down: float32 [8960, 1536], P(('ctx', 'fsdp'))
- update_query: float32 [1536, 1536], P(('ctx', 'fsdp'))
- update_key: float32 [1536, 256], P(('ctx', 'fsdp'))
- update_value: float32 [1536, 256], P(('ctx', 'fsdp'))
- update_output: float32 [1536, 1536], P(('ctx', 'fsdp'))
- update_gate: float32 [8960, 1536], P(('ctx', 'fsdp'))
- update_up: float32 [8960, 1536], P(('ctx', 'fsdp'))
- update_down: float32 [8960, 1536], P(('ctx', 'fsdp'))
- grad_bias: float32 [2048], replicated
- moment_bias: float32 [2048], replicated
- update_bias: float32 [2048], replicated
- grad_gains: float32 [2, 1536], replicated
- moment_gains: float32 [2, 1536], replicated
- update_gains: float32 [2, 1536], replicated
Inputs may be any that keep to these rules, and one draw needn't show every extreme that they name: `block_position`: A permutation of the blocks 0 to 15; entries 2 c and 2 c + 1, the two blocks of ctx index c, sum to 15.
All inputs are finite; a program needn't handle non-finite values.
Results may differ from a plain program's by a relative error of at most 0.02.
Values may be sent and summed in bfloat16 or wider, within the bound.
No kernel may reach another device: no remote copies, remote signals or barrier semaphores. Data moves between devices by JAX's collectives and lax.ppermute only.
A program may use at most 320 MiB of HBM per device.

v0:
```python
import math

import jax
import jax.numpy as jnp
import numpy as np
from jax import lax
from jax.sharding import PartitionSpec as P

QUERY_HEADS = 12
KEY_VALUE_HEADS = 2
HEAD_DIM = 128
NS_ITERS = 2


NORM_EPSILON = 1e-06
ROPE_BASE = 1000000.0
POLY_ONE = 3.4445
POLY_THREE = -4.775
POLY_FIVE = 2.0315
MOMENTUM = 0.95
STEP_SCALE = 0.06
VECTOR_STEP = 0.1
MASK_FILL = -1e30


def matmul(left, right):
    return jnp.dot(left, right, preferred_element_type=jnp.float32)


def matmul_nt(left, right):
    return lax.dot_general(
        left, right, (((1,), (1,)), ((), ())), preferred_element_type=jnp.float32
    )


def matmul_tn(left, right):
    return lax.dot_general(
        left, right, (((0,), (0,)), ((), ())), preferred_element_type=jnp.float32
    )


def rope_tables(positions, head_size):
    half_width = head_size // 2
    ratios = jnp.arange(half_width, dtype=jnp.float32) * (2.0 / head_size)
    frequency = jnp.exp(-math.log(ROPE_BASE) * ratios)
    angles = positions.astype(jnp.float32)[:, None] * frequency[None, :]
    return (jnp.cos(angles), jnp.sin(angles))


def apply_rotary(values, cosine_lookup, sine_lookup):
    half_width = values.shape[-1] // 2
    front_half = values[..., :half_width]
    back_half = values[..., half_width:]
    cosine_rows = cosine_lookup[:, None, :]
    sine_rows = sine_lookup[:, None, :]
    return jnp.concatenate(
        [
            front_half * cosine_rows - back_half * sine_rows,
            back_half * cosine_rows + front_half * sine_rows,
        ],
        axis=-1,
    )


def norm_scale(values):
    return lax.rsqrt(jnp.mean(values * values, axis=-1, keepdims=True) + NORM_EPSILON)


def norm_back(values, scale_rows, gain, grad_normed):
    weighted = grad_normed * gain
    inner_mean = jnp.mean(weighted * values, axis=-1, keepdims=True)
    grad_values = (
        scale_rows * weighted - values * (scale_rows * scale_rows * scale_rows) * inner_mean
    )
    grad_gain = jnp.sum(grad_normed * values * scale_rows, axis=0)
    return (grad_values, grad_gain)


def vector_step(old_state, gradient):
    fresh_state = MOMENTUM * old_state + gradient
    inverse_rms = lax.rsqrt(
        jnp.mean(fresh_state * fresh_state, axis=-1, keepdims=True) + NORM_EPSILON
    )
    return (fresh_state, -VECTOR_STEP * fresh_state * inverse_rms)


def shards(
    tokens,
    cotangent,
    block_position,
    w_query,
    key_weight,
    value_weight,
    w_output,
    w_gate,
    w_up,
    w_down,
    projection_bias,
    norm_gains,
    momentum_query,
    key_momentum,
    value_momentum,
    momentum_output,
    momentum_gate,
    momentum_up,
    momentum_down,
    bias_momentum,
    momentum_gains,
):
    shard_rows = tokens.shape[1]
    model_width = tokens.shape[2]
    ctx_count = lax.axis_size("ctx")
    ctx_rank = lax.axis_index("ctx")
    all_count = lax.axis_size(("ctx", "fsdp"))
    seq_length = shard_rows * ctx_count
    half_block = shard_rows // 2
    query_width = QUERY_HEADS * HEAD_DIM
    key_value_width = KEY_VALUE_HEADS * HEAD_DIM
    heads_per_group = QUERY_HEADS // KEY_VALUE_HEADS
    grouped_rows = heads_per_group * shard_rows
    score_scale = 1.0 / math.sqrt(HEAD_DIM)
    ff_rows = w_gate.shape[0]
    all_positions = (
        block_position[:, None] * half_block + jnp.arange(half_block, dtype=jnp.int32)[None, :]
    ).reshape(seq_length)
    own_positions = lax.dynamic_slice_in_dim(all_positions, ctx_rank * shard_rows, shard_rows)
    cosine_lookup, sine_lookup = rope_tables(own_positions, HEAD_DIM)
    row_positions = jnp.tile(own_positions, heads_per_group)
    inputs = tokens[0].astype(jnp.float32)
    grad_out = cotangent[0].astype(jnp.float32)
    grad_mid = cotangent[0]
    gain_one = norm_gains[0].astype(jnp.float32)
    gain_two = norm_gains[1].astype(jnp.float32)
    bias_values = projection_bias.astype(jnp.float32)
    full_query, full_key, full_value, full_output = (
        lax.all_gather(w_query, ("ctx", "fsdp"), axis=0, tiled=True),
        lax.all_gather(key_weight, ("ctx", "fsdp"), axis=0, tiled=True),
        lax.all_gather(value_weight, ("ctx", "fsdp"), axis=0, tiled=True),
        lax.all_gather(w_output, ("ctx", "fsdp"), axis=0, tiled=True),
    )
    scale_one = norm_scale(inputs)
    normed_one = (inputs * scale_one * gain_one).astype(jnp.bfloat16)
    query_proj = matmul(normed_one, full_query) + bias_values[:query_width]
    key_projected = (
        matmul(normed_one, full_key) + bias_values[query_width : query_width + key_value_width]
    )
    value_lowered = (
        matmul(normed_one, full_value) + bias_values[query_width + key_value_width :]
    ).astype(jnp.bfloat16)
    rotated_queries = apply_rotary(
        query_proj.reshape(shard_rows, QUERY_HEADS, HEAD_DIM), cosine_lookup, sine_lookup
    ).astype(jnp.bfloat16)
    rotated_keys = (
        apply_rotary(
            key_projected.reshape(shard_rows, KEY_VALUE_HEADS, HEAD_DIM), cosine_lookup, sine_lookup
        )
        .astype(jnp.bfloat16)
        .reshape(shard_rows, key_value_width)
    )
    gathered_keys, gathered_values = (
        lax.all_gather(rotated_keys, "ctx", axis=0, tiled=True),
        lax.all_gather(value_lowered, "ctx", axis=0, tiled=True),
    )
    current_key_block = math.gcd(seq_length, 1024)
    block_sum_total = seq_length // current_key_block
    key_block_list = gathered_keys.reshape(
        block_sum_total, current_key_block, KEY_VALUE_HEADS, HEAD_DIM
    )
    value_block_list = gathered_values.reshape(
        block_sum_total, current_key_block, KEY_VALUE_HEADS, HEAD_DIM
    )
    position_blocks = all_positions.reshape(block_sum_total, current_key_block)
    grouped_queries = (
        rotated_queries.reshape(shard_rows, KEY_VALUE_HEADS, heads_per_group, HEAD_DIM)
        .transpose(1, 2, 0, 3)
        .reshape(KEY_VALUE_HEADS, grouped_rows, HEAD_DIM)
    )

    def block_scores(key_piece, position_piece):
        raw_scores = (
            jnp.einsum(
                "hqd,khd->hqk", grouped_queries, key_piece, preferred_element_type=jnp.float32
            )
            * score_scale
        )
        visible = (position_piece[None, :] <= row_positions[:, None])[None]
        return (jnp.where(visible, raw_scores, MASK_FILL), visible)

    def stats_step(running, inputs_block):
        row_peak, row_total = running
        key_piece, position_piece = inputs_block
        scores, visible = block_scores(key_piece, position_piece)
        new_peak = jnp.maximum(row_peak, jnp.max(scores, axis=-1))
        exp_scores = jnp.where(visible, jnp.exp(scores - new_peak[..., None]), 0.0)
        row_total = row_total * jnp.exp(row_peak - new_peak) + jnp.sum(exp_scores, axis=-1)
        return ((new_peak, row_total), None)

    initial_peak = jnp.full((KEY_VALUE_HEADS, grouped_rows), MASK_FILL, jnp.float32)
    initial_total = jnp.zeros((KEY_VALUE_HEADS, grouped_rows), jnp.float32)
    (row_peak, row_total), unused_stats = lax.scan(
        stats_step, (initial_peak, initial_total), (key_block_list, position_blocks)
    )
    log_total = row_peak + jnp.log(row_total)

    def output_step(combined_heads, inputs_block):
        key_piece, value_piece, position_piece = inputs_block
        scores, visible = block_scores(key_piece, position_piece)
        soft_block = jnp.exp(scores - log_total[..., None])
        combined_heads = combined_heads + jnp.einsum(
            "hqk,khd->hqd",
            soft_block.astype(jnp.bfloat16),
            value_piece,
            preferred_element_type=jnp.float32,
        )
        return (combined_heads, None)

    blank_heads = jnp.zeros((KEY_VALUE_HEADS, grouped_rows, HEAD_DIM), jnp.float32)
    combined_heads, unused_out = lax.scan(
        output_step, blank_heads, (key_block_list, value_block_list, position_blocks)
    )
    attended = (
        combined_heads.reshape(KEY_VALUE_HEADS, heads_per_group, shard_rows, HEAD_DIM)
        .transpose(2, 0, 1, 3)
        .reshape(shard_rows, query_width)
        .astype(jnp.bfloat16)
    )
    hidden_one = inputs + matmul(attended, full_output)
    scale_two = norm_scale(hidden_one)
    normed_two = (hidden_one * scale_two * gain_two).astype(jnp.bfloat16)
    gate_full, up_full, down_full = (
        lax.all_gather(w_gate, ("ctx", "fsdp"), axis=0, tiled=True),
        lax.all_gather(w_up, ("ctx", "fsdp"), axis=0, tiled=True),
        lax.all_gather(w_down, ("ctx", "fsdp"), axis=0, tiled=True),
    )
    gate_values = matmul_nt(normed_two, gate_full)
    up_values = matmul_nt(normed_two, up_full)
    sigmoid_gate = jax.nn.sigmoid(gate_values)
    active = gate_values * sigmoid_gate
    hidden_store = (active * up_values).astype(jnp.bfloat16)
    branch_out = matmul(hidden_store, down_full)
    grad_hidden = matmul_nt(grad_mid, down_full)
    up_store = (grad_hidden * active).astype(jnp.bfloat16)
    gate_store = (
        grad_hidden * up_values * (sigmoid_gate * (1.0 + gate_values * (1.0 - sigmoid_gate)))
    ).astype(jnp.bfloat16)
    grad_normed_two = matmul(gate_store, gate_full) + matmul(up_store, up_full)
    out_tokens = (hidden_one + branch_out).astype(jnp.bfloat16)
    grad_hidden_one, grad_gain_two = norm_back(hidden_one, scale_two, gain_two, grad_normed_two)
    grad_hidden_one = grad_hidden_one + grad_out
    grad_branch = grad_hidden_one.astype(jnp.bfloat16)
    attended_gradient = matmul_nt(grad_branch, full_output).astype(jnp.bfloat16)
    grad_grouped = (
        attended_gradient.reshape(shard_rows, KEY_VALUE_HEADS, heads_per_group, HEAD_DIM)
        .transpose(1, 2, 0, 3)
        .reshape(KEY_VALUE_HEADS, grouped_rows, HEAD_DIM)
    )
    row_inner = jnp.sum(grad_grouped.astype(jnp.float32) * combined_heads, axis=-1)

    def grad_step(running, inputs_block):
        key_piece, value_piece, position_piece = inputs_block
        scores, visible = block_scores(key_piece, position_piece)
        soft_block = jnp.exp(scores - log_total[..., None])
        grad_soft = jnp.einsum(
            "hqd,khd->hqk", grad_grouped, value_piece, preferred_element_type=jnp.float32
        )
        value_part = jnp.einsum(
            "hqk,hqd->khd",
            soft_block.astype(jnp.bfloat16),
            grad_grouped,
            preferred_element_type=jnp.float32,
        )
        score_grad = (soft_block * (grad_soft - row_inner[..., None])).astype(jnp.bfloat16)
        running = running + jnp.einsum(
            "hqk,khd->hqd", score_grad, key_piece, preferred_element_type=jnp.float32
        )
        key_part = jnp.einsum(
            "hqk,hqd->khd", score_grad, grouped_queries, preferred_element_type=jnp.float32
        )
        return (running, (key_part, value_part))

    rotated_query_gradient, (key_parts, value_parts) = lax.scan(
        grad_step, blank_heads, (key_block_list, value_block_list, position_blocks)
    )
    rotated_query_gradient = rotated_query_gradient * score_scale
    key_grad_all = key_parts.reshape(seq_length, key_value_width) * score_scale
    value_grad_all = value_parts.reshape(seq_length, key_value_width)
    rotated_key_gradient, value_grad_sum = (
        lax.psum_scatter(
            key_grad_all.astype(jnp.bfloat16), "ctx", scatter_dimension=0, tiled=True
        ).astype(jnp.float32),
        lax.psum_scatter(
            value_grad_all.astype(jnp.bfloat16), "ctx", scatter_dimension=0, tiled=True
        ).astype(jnp.float32),
    )
    query_grad_heads = (
        rotated_query_gradient.reshape(KEY_VALUE_HEADS, heads_per_group, shard_rows, HEAD_DIM)
        .transpose(2, 0, 1, 3)
        .reshape(shard_rows, QUERY_HEADS, HEAD_DIM)
    )
    query_grad_low = (
        apply_rotary(query_grad_heads, cosine_lookup, -sine_lookup)
        .astype(jnp.bfloat16)
        .reshape(shard_rows, query_width)
    )
    key_grad_low = (
        apply_rotary(
            rotated_key_gradient.reshape(shard_rows, KEY_VALUE_HEADS, HEAD_DIM),
            cosine_lookup,
            -sine_lookup,
        )
        .astype(jnp.bfloat16)
        .reshape(shard_rows, key_value_width)
    )
    value_grad_low = value_grad_sum.astype(jnp.bfloat16)
    grad_normed_one = (
        matmul_nt(query_grad_low, full_query)
        + matmul_nt(key_grad_low, full_key)
        + matmul_nt(value_grad_low, full_value)
    )
    grad_inputs, grad_gain_one = norm_back(inputs, scale_one, gain_one, grad_normed_one)
    grad_tokens = (grad_inputs + grad_hidden_one)[None]
    bias_term = jnp.concatenate(
        [
            jnp.sum(query_grad_low, axis=0, dtype=jnp.float32),
            jnp.sum(key_grad_low, axis=0, dtype=jnp.float32),
            jnp.sum(value_grad_low, axis=0, dtype=jnp.float32),
        ]
    )
    gain_term = jnp.stack([grad_gain_one, grad_gain_two])
    grad_bias, grad_gains = lax.psum((bias_term, gain_term), ("ctx", "fsdp"))
    attention_grads = lax.psum_scatter(
        jnp.concatenate(
            [
                matmul_tn(normed_one, query_grad_low),
                matmul_tn(normed_one, key_grad_low),
                matmul_tn(normed_one, value_grad_low),
                matmul_tn(attended, grad_branch),
            ],
            axis=1,
        ),
        ("ctx", "fsdp"),
        scatter_dimension=0,
        tiled=True,
    )
    grad_query = attention_grads[:, :query_width]
    grad_key = attention_grads[:, query_width : query_width + key_value_width]
    grad_value = attention_grads[
        :, query_width + key_value_width : query_width + 2 * key_value_width
    ]
    grad_output = attention_grads[:, query_width + 2 * key_value_width :]
    gate_cols, up_cols, hidden_cols = (
        lax.all_to_all(gate_store, ("ctx", "fsdp"), split_axis=1, concat_axis=0, tiled=True),
        lax.all_to_all(up_store, ("ctx", "fsdp"), split_axis=1, concat_axis=0, tiled=True),
        lax.all_to_all(hidden_store, ("ctx", "fsdp"), split_axis=1, concat_axis=0, tiled=True),
    )
    normed_piece = lax.all_gather(normed_two, ("ctx", "fsdp"), axis=0, tiled=True)
    grad_piece = lax.all_gather(grad_mid, ("ctx", "fsdp"), axis=0, tiled=True)
    grad_gate = matmul_tn(gate_cols, normed_piece)
    grad_up = matmul_tn(up_cols, normed_piece)
    grad_down = matmul_tn(hidden_cols, grad_piece)
    matrix_pairs = (
        (grad_query, momentum_query),
        (grad_key, key_momentum),
        (grad_value, value_momentum),
        (grad_output, momentum_output),
        (grad_gate, momentum_gate),
        (grad_up, momentum_up),
        (grad_down, momentum_down),
    )
    moments = [MOMENTUM * old_state + gradient for gradient, old_state in matrix_pairs]
    owners = [matrix_index * ctx_count // 7 for matrix_index in range(7)]
    padded = jnp.stack(
        [
            jnp.pad(
                moment.astype(jnp.bfloat16),
                ((0, ff_rows - moment.shape[0]), (0, model_width - moment.shape[1])),
            )
            for moment in moments
        ]
    )
    owner_table = jnp.asarray(
        (np.arange(ctx_count)[:, None] == np.array(owners)[None, :]).astype(np.float32),
        jnp.bfloat16,
    )
    outgoing = jnp.einsum(
        "cm,mrd->crd", owner_table, padded, preferred_element_type=jnp.float32
    ).astype(jnp.bfloat16)
    arrived = lax.all_to_all(outgoing, "ctx", split_axis=0, concat_axis=0, tiled=True)
    current = arrived.reshape(ctx_count * ff_rows, model_width)
    for iteration in range(NS_ITERS):
        gram_matrix = lax.psum(matmul_tn(current, current).astype(jnp.bfloat16), "fsdp").astype(
            jnp.float32
        )
        if iteration == 0:
            factor = 1.0 / (jnp.sqrt(jnp.trace(gram_matrix)) + 1e-07)
        else:
            factor = 1.0
        gram_matrix = gram_matrix * (factor * factor)
        gram_low = gram_matrix.astype(jnp.bfloat16)
        polynomial = (POLY_THREE * gram_matrix + POLY_FIVE * matmul(gram_low, gram_low)).astype(
            jnp.bfloat16
        )
        current = (
            factor * (POLY_ONE * current.astype(jnp.float32) + matmul(current, polynomial))
        ).astype(jnp.bfloat16)
    returned = lax.all_to_all(
        current.reshape(ctx_count, ff_rows, model_width),
        "ctx",
        split_axis=0,
        concat_axis=0,
        tiled=True,
    )
    updates = []
    for matrix_index in range(7):
        rows_local, col_count = moments[matrix_index].shape
        owned_piece = returned[owners[matrix_index], :rows_local, :col_count].astype(jnp.float32)
        whole_rows = rows_local * all_count
        updates.append(-STEP_SCALE * math.sqrt(max(whole_rows, col_count)) * owned_piece)
    moment_bias, update_bias = vector_step(bias_momentum, grad_bias)
    moment_gains, update_gains = vector_step(momentum_gains, grad_gains)
    return (
        out_tokens[None],
        grad_tokens,
        grad_query,
        grad_key,
        grad_value,
        grad_output,
        grad_gate,
        grad_up,
        grad_down,
        moments[0],
        moments[1],
        moments[2],
        moments[3],
        moments[4],
        moments[5],
        moments[6],
        updates[0],
        updates[1],
        updates[2],
        updates[3],
        updates[4],
        updates[5],
        updates[6],
        grad_bias,
        moment_bias,
        update_bias,
        grad_gains,
        moment_gains,
        update_gains,
    )


def solution(mesh):
    return jax.shard_map(
        shards,
        mesh=mesh,
        in_specs=(
            P("fsdp", "ctx", None),
            P("fsdp", "ctx", None),
            P(),
            P(("ctx", "fsdp"), None),
            P(("ctx", "fsdp"), None),
            P(("ctx", "fsdp"), None),
            P(("ctx", "fsdp"), None),
            P(("ctx", "fsdp"), None),
            P(("ctx", "fsdp"), None),
            P(("ctx", "fsdp"), None),
            P(),
            P(),
            P(("ctx", "fsdp"), None),
            P(("ctx", "fsdp"), None),
            P(("ctx", "fsdp"), None),
            P(("ctx", "fsdp"), None),
            P(("ctx", "fsdp"), None),
            P(("ctx", "fsdp"), None),
            P(("ctx", "fsdp"), None),
            P(),
            P(),
        ),
        out_specs=(
            P("fsdp", "ctx", None),
            P("fsdp", "ctx", None),
            P(("ctx", "fsdp"), None),
            P(("ctx", "fsdp"), None),
            P(("ctx", "fsdp"), None),
            P(("ctx", "fsdp"), None),
            P(("ctx", "fsdp"), None),
            P(("ctx", "fsdp"), None),
            P(("ctx", "fsdp"), None),
            P(("ctx", "fsdp"), None),
            P(("ctx", "fsdp"), None),
            P(("ctx", "fsdp"), None),
            P(("ctx", "fsdp"), None),
            P(("ctx", "fsdp"), None),
            P(("ctx", "fsdp"), None),
            P(("ctx", "fsdp"), None),
            P(("ctx", "fsdp"), None),
            P(("ctx", "fsdp"), None),
            P(("ctx", "fsdp"), None),
            P(("ctx", "fsdp"), None),
            P(("ctx", "fsdp"), None),
            P(("ctx", "fsdp"), None),
            P(("ctx", "fsdp"), None),
            P(),
            P(),
            P(),
            P(),
            P(),
            P(),
        ),
        check_vma=False,
    )
```

profile of v0, /device:TPU:0, one launch (start us, length us, event | category | flops | bytes accessed | tf_op | source)
XLA Modules:
  0.0 1972.5 jit_solution(4340414847793262689)
XLA Ops:
  14.6 81.1 %all_gather.34 = bf16[1536,256]{1,0:T(8,128)(2,1)S(1)} all-gather(bf16[48,256]{1,0:T(8,128)(2,1)} %param.26), channel_id=1, replica_groups=mesh['ctx'=8,'fsdp'=4] {'ctx','fsdp'}, dimensions={0}, use_global_device_ids=true | all-gather | bytes 811008 | tf_op jit(solution)/shard_map/all_gather | solution.py:137
  109.2 77.6 %all_gather.36 = bf16[1536,256]{1,0:T(8,128)(2,1)S(1)} all-gather(bf16[48,256]{1,0:T(8,128)(2,1)S(1)} %copy-done.50), channel_id=1, replica_groups=mesh['ctx'=8,'fsdp'=4] {'ctx','fsdp'}, dimensions={0}, use_global_device_ids=true | all-gather | bytes 811008 | tf_op jit(solution)/shard_map/all_gather | solution.py:138
  188.1 15.3 all_gather.37
  219.1 102.1 %all-gather.13.cloned.1.call-done = bf16[8960,1536]{1,0:T(8,128)(2,1)} async-done(((bf16[280,1536]{1,0:T(8,128)(2,1)}), bf16[8960,1536]{1,0:T(8,128)(2,1)}) %all-gather.13.cloned.1.call-update) | async-done | bytes 27525136 | tf_op jit(solution)/shard_map/all_gather | solution.py:231
  321.1 16.2 fusion.83
  337.3 150.6 %all-gather.15.cloned.1.call-done = bf16[8960,1536]{1,0:T(8,128)(2,1)} async-done(((bf16[280,1536]{1,0:T(8,128)(2,1)}), bf16[8960,1536]{1,0:T(8,128)(2,1)}) %all-gather.15.cloned.1.call-update) | async-done | bytes 27525136 | tf_op jit(solution)/shard_map/all_gather | solution.py:232
  488.0 16.4 fusion.84
  504.4 150.4 %all-gather.17.cloned.1.call-done = bf16[8960,1536]{1,0:T(8,128)(2,1)} async-done(((bf16[280,1536]{1,0:T(8,128)(2,1)}), bf16[8960,1536]{1,0:T(8,128)(2,1)}) %all-gather.17.cloned.1.call-update) | async-done | bytes 27525136 | tf_op jit(solution)/shard_map/all_gather | solution.py:233
  654.8 17.7 multiply_convert_fusion.2
  724.5 19.4 reduce-scatter.10.cloned.1.call-done
  747.2 34.9 %reduce-scatter.12.cloned.1.call-done = bf16[128,256]{1,0:T(8,128)(2,1)} async-done(((bf16[1024,256]{1,0:T(8,128)(2,1)}), bf16[128,256]{1,0:T(8,128)(2,1)}) %reduce-scatter.12.cloned.1.call-update) | async-done | bytes 65552
  783.4 14.9 pad_maximum_fusion
  798.3 21.7 %copy.176 = f32[1536,3584]{1,0:T(8,128)} copy(f32[1536,3584]{0,1:T(8,128)} %pad_maximum_fusion) | data formatting | bytes 44040192
  833.2 47.5 %all-to-all-done = bf16[128,32,280]{0,2,1:T(8,128)(2,1)} async-done(((bf16[128,32,280]{0,2,1:T(8,128)(2,1)}), bf16[128,32,280]{0,2,1:T(8,128)(2,1)}, u32[]{:S(2)}, u32[]{:S(2)}) %all-to-all-start) | async-done | bytes 2293792 | tf_op jit(solution)/shard_map/all_to_all | solution.py:352
  887.8 98.6 %all-to-all-done.1 = bf16[128,32,280]{0,2,1:T(8,128)(2,1)} async-done(((bf16[128,32,280]{0,2,1:T(8,128)(2,1)}), bf16[128,32,280]{0,2,1:T(8,128)(2,1)}, u32[]{:S(2)}, u32[]{:S(2)}) %all-to-all-start.1) | async-done | bytes 2293792 | tf_op jit(solution)/shard_map/all_to_all | solution.py:353
  993.0 121.5 %reduce-scatter.14.cloned.1.call-done = f32[48,3584]{1,0:T(8,128)} async-done(((f32[1536,3584]{1,0:T(8,128)}), f32[48,3584]{1,0:T(8,128)}) %reduce-scatter.14.cloned.1.call-update) | async-done | bytes 688144 | tf_op jit(solution)/shard_map/reduce_scatter | solution.py:331
  1122.1 91.4 %all-gather.19.cloned.1.call-done = bf16[4096,1536]{1,0:T(8,128)(2,1)} async-done(((bf16[128,1536]{1,0:T(8,128)(2,1)}), bf16[4096,1536]{1,0:T(8,128)(2,1)}) %all-gather.19.cloned.1.call-update) | async-done | bytes 12582928 | tf_op jit(solution)/shard_map/all_gather | solution.py:356
  1232.3 78.3 %all-gather.21.cloned.1.call-done = bf16[1,4096,1536]{2,1,0:T(8,128)(2,1)} async-done(((bf16[1,128,1536]{2,1,0:T(8,128)(2,1)}), bf16[1,4096,1536]{2,1,0:T(8,128)(2,1)}) %all-gather.21.cloned.1.call-update) | async-done | bytes 12582928 | tf_op jit(solution)/shard_map/all_gather | solution.py:357
  1328.5 80.6 %all_to_all.67 = bf16[8,280,1536]{2,1,0:T(8,128)(2,1)S(1)} all-to-all(bf16[8,280,1536]{2,1,0:T(8,128)(2,1)S(1)} %copy.163), channel_id=1, replica_groups=mesh['ctx'=8,'fsdp'=4] {'ctx'}, dimensions={0} | all-to-all | bytes 13762560 | tf_op jit(solution)/shard_map/all_to_all | solution.py:388
  1425.1 169.4 %all-reduce.8.cloned.1.call-done = bf16[1536,1536]{1,0:T(8,128)(2,1)} async-done(((bf16[1536,1536]{1,0:T(8,128)(2,1)}), bf16[1536,1536]{1,0:T(8,128)(2,1)}) %all-reduce.8.cloned.1.call-update) | async-done | bytes 4718608 | tf_op jit(solution)/shard_map/psum | solution.py:391
  1626.0 13.3 convolution_convert_fusion
  1639.3 171.1 %all-reduce.10.cloned.1.call-done = bf16[1536,1536]{1,0:T(8,128)(2,1)} async-done(((bf16[1536,1536]{1,0:T(8,128)(2,1)}), bf16[1536,1536]{1,0:T(8,128)(2,1)}) %all-reduce.10.cloned.1.call-update) | async-done | bytes 4718608 | tf_op jit(solution)/shard_map/psum | solution.py:391
  1810.5 28.9 %add_convert_fusion = bf16[2240,1536]{1,0:T(8,128)(2,1)} fusion(bf16[2240,1536]{1,0:T(8,128)(2,1)} %copy-done.64, bf16[1536,1536]{1,0:T(8,128)(2,1)} %all-reduce.10.cloned.1.call-done), kind=kOutput, calls=%fused_computation.1 | convolution fusion | flops 17842962432 | bytes 18481152 | tf_op jit(solution)/shard_map/dot_general | solution.py:27
  1862.2 91.7 %all-reduce.4 = (f32[2048]{0:T(1024)S(1)}, f32[2,1536]{1,0:T(2,128)S(1)}) all-reduce(f32[2048]{0:T(1024)S(1)} %pad_maximum_fusion.3, f32[2,1536]{1,0:T(2,128)S(1)} %pad_maximum_fusion.2), channel_id=1, replica_groups=mesh['ctx'=8,'fsdp'=4] {'ctx','fsdp'}, use_global_device_ids=true, to_apply=%region_16.17 | all-reduce | flops 5120 | bytes 40960 | tf_op jit(solution)/shard_map/psum | solution.py:330
  (281 shorter events, 244.7 us)
Async XLA Ops:
  7.2 196.7 %all-gather.9.cloned.1.call-start = ((), (), s32[]{:S(2)}) async-start(), calls=%async_computation.8 | async-start | bytes 4866048 | tf_op jit(solution)/shard_map/all_gather | solution.py:136
  8.0 207.5 %all-gather.11.cloned.1.call-start = ((), (), s32[]{:S(2)}) async-start(), calls=%async_computation.9 | async-start | bytes 4866048 | tf_op jit(solution)/shard_map/all_gather | solution.py:139
  8.7 312.4 %all-gather.13.cloned.1.call-start = ((), (), s32[]{:S(2)}) async-start(), calls=%async_computation.10 | async-start | bytes 28385280 | tf_op jit(solution)/shard_map/all_gather | solution.py:231
  9.4 478.5 %all-gather.15.cloned.1.call-start = ((), (), s32[]{:S(2)}) async-start(), calls=%async_computation.11 | async-start | bytes 28385280 | tf_op jit(solution)/shard_map/all_gather | solution.py:232
  10.0 644.7 %all-gather.17.cloned.1.call-start = ((), (), s32[]{:S(2)}) async-start(), calls=%async_computation.12 | async-start | bytes 28385280 | tf_op jit(solution)/shard_map/all_gather | solution.py:233
  10.6 733.3 %reduce-scatter.10.cloned.1.call-start = ((), (), s32[]{:S(2)}) async-start(), calls=%async_computation.17 | async-start | bytes 589824
  12.2 769.9 %copy-start.38 = (f32[1536]{0:T(1024)}, f32[1536]{0:T(1024)S(1)}, u32[]{:S(2)}) copy-start(f32[1536]{0:T(1024)S(1)} %get-tuple-element.173) | copy-start | bytes 18436
  13.9 768.2 %copy-start.51 = (f32[128]{0:T(128)}, f32[128]{0:T(128)S(1)}, u32[]{:S(2)}) copy-start(f32[128]{0:T(128)S(1)} %get-tuple-element.238) | copy-start | bytes 1540
  218.9 477.9 %copy-start.2 = (f32[128,1536]{1,0:T(8,128)}, f32[128,1536]{1,0:T(8,128)S(1)}, u32[]{:S(2)}) copy-start(f32[128,1536]{1,0:T(8,128)S(1)} %get-tuple-element.246) | copy-start | bytes 2359300
  219.0 268.9 %copy-start.10 = (bf16[128,1536]{1,0:T(8,128)(2,1)}, bf16[128,1536]{1,0:T(8,128)(2,1)S(1)}, u32[]{:S(2)}) copy-start(bf16[128,1536]{1,0:T(8,128)(2,1)S(1)} %multiply_convert_fusion.5) | copy-start | bytes 1179652
  711.4 70.6 %reduce-scatter.12.cloned.1.call-start = ((), (), s32[]{:S(2)}) async-start(), calls=%async_computation.18 | async-start | bytes 589824
  724.5 390.1 %reduce-scatter.14.cloned.1.call-start = ((), (), s32[]{:S(2)}) async-start(), calls=%async_computation.19 | async-start | bytes 22708224 | tf_op jit(solution)/shard_map/reduce_scatter | solution.py:331
  820.1 393.4 %all-gather.19.cloned.1.call-start = ((), (), s32[]{:S(2)}) async-start(), calls=%async_computation.13 | async-start | bytes 12976128 | tf_op jit(solution)/shard_map/all_gather | solution.py:356
  820.8 489.8 %all-gather.21.cloned.1.call-start = ((), (), s32[]{:S(2)}) async-start(), calls=%async_computation.16 | async-start | bytes 12976128 | tf_op jit(solution)/shard_map/all_gather | solution.py:357
  824.2 56.6 %all-to-all-start = ((bf16[128,32,280]{0,2,1:T(8,128)(2,1)}), bf16[128,32,280]{0,2,1:T(8,128)(2,1)}, u32[]{:S(2)}, u32[]{:S(2)}) async-start(bf16[128,32,280]{0,2,1:T(8,128)(2,1)} %bitcast.232), calls=%async_computation | async-start | bytes 4587520 | tf_op jit(solution)/shard_map/all_to_all | solution.py:352
  880.8 233.8 %copy-start.44 = (f32[48,256]{1,0:T(8,128)S(1)}, f32[48,256]{1,0:T(8,128)}, u32[]{:S(2)}) copy-start(f32[48,256]{1,0:T(8,128)} %param.36) | copy-start | bytes 147460
  880.8 233.8 %copy-start.45 = (f32[48,256]{1,0:T(8,128)S(1)}, f32[48,256]{1,0:T(8,128)}, u32[]{:S(2)}) copy-start(f32[48,256]{1,0:T(8,128)} %param.35) | copy-start | bytes 147460
  880.8 235.3 %copy-start.41 = (f32[48,1536]{1,0:T(8,128)S(1)}, f32[48,1536]{1,0:T(8,128)}, u32[]{:S(2)}) copy-start(f32[48,1536]{1,0:T(8,128)} %param.37) | copy-start | bytes 884740
  880.8 235.3 %copy-start.42 = (f32[48,1536]{1,0:T(8,128)S(1)}, f32[48,1536]{1,0:T(8,128)}, u32[]{:S(2)}) copy-start(f32[48,1536]{1,0:T(8,128)} %param.34) | copy-start | bytes 884740
  880.8 105.5 %all-to-all-start.1 = ((bf16[128,32,280]{0,2,1:T(8,128)(2,1)}), bf16[128,32,280]{0,2,1:T(8,128)(2,1)}, u32[]{:S(2)}, u32[]{:S(2)}) async-start(bf16[128,32,280]{0,2,1:T(8,128)(2,1)} %bitcast.231), calls=%async_computation.1 | async-start | bytes 4587520 | tf_op jit(solution)/shard_map/all_to_all | solution.py:353
  986.3 324.2 %all-to-all-start.2 = ((bf16[128,32,280]{0,2,1:T(8,128)(2,1)}), bf16[128,32,280]{0,2,1:T(8,128)(2,1)S(1)}, u32[]{:S(2)}, u32[]{:S(2)}) async-start(bf16[128,32,280]{0,2,1:T(8,128)(2,1)} %bitcast.230), calls=%async_computation.2 | async-start | bytes 4587520 | tf_op jit(solution)/shard_map/all_to_all | solution.py:354
  992.6 601.9 %all-reduce.8.cloned.1.call-start = ((), (), s32[]{:S(2)}) async-start(), calls=%async_computation.14 | async-start | bytes 9437184 | tf_op jit(solution)/shard_map/psum | solution.py:391
  1425.1 385.4 %all-reduce.10.cloned.1.call-start = ((), (), s32[]{:S(2)}) async-start(), calls=%async_computation.15 | async-start | bytes 9437184 | tf_op jit(solution)/shard_map/psum | solution.py:391
  1839.4 118.5 %all-to-all-start.4 = ((bf16[8,280,1536]{2,1,0:T(8,128)(2,1)}), bf16[8,280,1536]{2,1,0:T(8,128)(2,1)}, u32[]{:S(2)}, u32[]{:S(2)}) async-start(bf16[8,280,1536]{2,1,0:T(8,128)(2,1)} %bitcast.234), calls=%async_computation.4 | async-start | bytes 13762560 | tf_op jit(solution)/shard_map/all_to_all | solution.py:406
  (63 other events, 1641.4 us)
Sparse Core Ops, SparseCore 0:
  10.9 68.9 all-gather.8
  82.7 64.2 all-gather.10
  149.8 171.3 all-gather.12
  323.8 164.0 all-gather.14
  490.6 164.0 all-gather.16
  711.6 32.3 reduce-scatter.9
  747.9 34.1 reduce-scatter.11
  820.2 294.3 reduce-scatter.13
  1118.0 95.4 all-gather.18
  1216.2 94.2 all-gather.20
  1425.2 169.2 all-reduce.7
  1639.5 170.9 all-reduce.9
where the time goes:
time: 1980 us; the launch traced here: 1970 us
  waiting for transfers between devices  1240 us (63%)
  blocking collectives  355 us (18%)
  matrix products  242 us (12%)
  local copies, waits for them, and re-layouts  53.8 us (3%)
  other arithmetic  43.6 us (2%)
  starting transfers between devices  21.6 us (1%)
    psum x2, waiting for transfers between devices, shards(): lax.psum(matmul_tn(current, current).astype(jnp.bfloat16), 'fsdp')  340 us
    all_gather x1, waiting for transfers between devices, shards(): lax.all_gather(w_up, ('ctx', 'fsdp'), axis=0, tiled=True)  151 us
    all_gather x1, waiting for transfers between devices, shards(): lax.all_gather(w_down, ('ctx', 'fsdp'), axis=0, tiled=True)  150 us
    reduce_scatter x1, waiting for transfers between devices, shards(): lax.psum_scatter(jnp.concatenate([matmul_tn(normed_one, query_grad_low),...  122 us
    all_gather x1, waiting for transfers between devices, shards(): lax.all_gather(w_gate, ('ctx', 'fsdp'), axis=0, tiled=True)  102 us
    all_to_all x1, waiting for transfers between devices, shards(): lax.all_to_all(up_store, ('ctx', 'fsdp'), split_axis=1, concat_axis=0, ti...  98.6 us
    dot_general x10, matrix products, matmul(): return jnp.dot(left, right, preferred_element_type=jnp.float32)  98.1 us
    psum x1, blocking collectives, shards(): grad_bias, grad_gains = lax.psum((bias_term, gain_term), ('ctx', 'fsdp'))  91.7 us
  transfers between devices with their start and end apart: 16, of which 12 were waited for; matrix products, arithmetic and copies ran while one was open for 6% of the time, Pallas kernels for 0%

commit v1 on v0

v1 whole, which is shorter than its diff:
```python
import math

import jax
import jax.numpy as jnp
import numpy as np
from jax import lax
from jax.sharding import PartitionSpec as P

QUERY_HEADS = 12
KEY_VALUE_HEADS = 2
HEAD_DIM = 128
CORES = 2

NORM_EPSILON = 1e-06
ROPE_BASE = 1000000.0
POLY_ONE = 3.4445
POLY_THREE = -4.775
POLY_FIVE = 2.0315
MOMENTUM = 0.95
STEP_SCALE = 0.06
VECTOR_STEP = 0.1
MASK_FILL = -1e30

F32 = jnp.float32
BF16 = jnp.bfloat16


def matmul(left, right):
    return jnp.dot(left, right, preferred_element_type=F32)


def matmul_nt(left, right):
    return lax.dot_general(left, right, (((1,), (1,)), ((), ())), preferred_element_type=F32)


def matmul_tn(left, right):
    return lax.dot_general(left, right, (((0,), (0,)), ((), ())), preferred_element_type=F32)


def after(value, *others):
    return lax.optimization_barrier((value,) + others)[0]


class Grid:
    def __init__(self, ctx_count, z_count):
        plane = ctx_count // CORES
        x_count = math.isqrt(plane)
        while plane % x_count:
            x_count -= 1
        self.x_count, self.y_count, self.z_count = x_count, plane // x_count, z_count

    def place(self):
        ctx = lax.axis_index("ctx")
        return (
            ctx // (CORES * self.x_count),
            (ctx // CORES) % self.x_count,
            ctx % CORES,
            lax.axis_index("fsdp"),
        )

    def shift(self, value, dy=0, dx=0, dc=0, dz=0, keep=None):
        y_count, x_count, z_count = self.y_count, self.x_count, self.z_count
        dy, dx, dc, dz = dy % y_count, dx % x_count, dc % CORES, dz % z_count
        if not (dy or dx or dc):
            if not dz:
                return value
            return lax.ppermute(value, "fsdp", [(z, (z + dz) % z_count) for z in range(z_count)])
        pairs = []
        for y in range(y_count):
            for x in range(x_count):
                for c in range(CORES):
                    to_y, to_x, to_c = (y + dy) % y_count, (x + dx) % x_count, (c + dc) % CORES
                    if keep is None or keep(to_y, to_x):
                        pairs.append(
                            ((y * x_count + x) * CORES + c, (to_y * x_count + to_x) * CORES + to_c)
                        )
        assert not dz
        return lax.ppermute(value, "ctx", pairs)

    def plane_gather(self, block):
        half = block.shape[0] // 2
        first, second = block[:half], block[half:]
        first = jnp.concatenate(
            [first] + [self.shift(first, dx=j) for j in range(1, self.x_count)]
        )
        second = jnp.concatenate(
            [second] + [self.shift(second, dy=j) for j in range(1, self.y_count)]
        )
        return jnp.concatenate(
            [first]
            + [self.shift(first, dy=j) for j in range(1, self.y_count)]
            + [second]
            + [self.shift(second, dx=j) for j in range(1, self.x_count)]
        )

    def plane_order(self, rows):
        half = rows // 2
        jy, jx, row = [], [], []
        for y in range(self.y_count):
            for x in range(self.x_count):
                for r in range(half):
                    jy.append(y), jx.append(x), row.append(r)
        for x in range(self.x_count):
            for y in range(self.y_count):
                for r in range(half, rows):
                    jy.append(y), jx.append(x), row.append(r)
        return np.array(jy), np.array(jx), np.array(row)

    def gather(self, block):
        slots = [block]
        for _ in range(1, self.z_count):
            slots.append(self.shift(slots[-1], dz=1))
        return [self.plane_gather(slot) for slot in slots]

    def plane_reduce(self, part):
        def step(rows, count, axis):
            size = rows.shape[0] // count
            total = rows[:size].astype(F32)
            for j in range(1, count):
                piece = rows[j * size : (j + 1) * size].astype(BF16)
                total = total + self.shift(piece, **{axis: -j}).astype(F32)
            return total

        half = part.shape[0] // 2
        first = step(step(part[:half], self.y_count, "dy"), self.x_count, "dx")
        second = step(step(part[half:], self.x_count, "dx"), self.y_count, "dy")
        return jnp.concatenate([first, second])

    def z_sum(self, parts):
        total = parts[0].astype(F32)
        for j in range(1, self.z_count):
            total = total + self.shift(parts[j].astype(BF16), dz=-j).astype(F32)
        return total

    def reduce(self, parts):
        return self.z_sum([self.plane_reduce(part) for part in parts])


def rope_tables(positions, head_size):
    half_width = head_size // 2
    ratios = jnp.arange(half_width, dtype=F32) * (2.0 / head_size)
    frequency = jnp.exp(-math.log(ROPE_BASE) * ratios)
    angles = positions.astype(F32)[:, None] * frequency[None, :]
    return (jnp.cos(angles), jnp.sin(angles))


def apply_rotary(values, cosine_lookup, sine_lookup):
    half_width = values.shape[-1] // 2
    front_half = values[..., :half_width]
    back_half = values[..., half_width:]
    cosine_rows = cosine_lookup[:, None, :]
    sine_rows = sine_lookup[:, None, :]
    return jnp.concatenate(
        [
            front_half * cosine_rows - back_half * sine_rows,
            back_half * cosine_rows + front_half * sine_rows,
        ],
        axis=-1,
    )


def norm_scale(values):
    return lax.rsqrt(jnp.mean(values * values, axis=-1, keepdims=True) + NORM_EPSILON)


def norm_back(values, scale_rows, gain, grad_normed):
    weighted = grad_normed * gain
    inner_mean = jnp.mean(weighted * values, axis=-1, keepdims=True)
    grad_values = (
        scale_rows * weighted - values * (scale_rows * scale_rows * scale_rows) * inner_mean
    )
    grad_gain = jnp.sum(grad_normed * values * scale_rows, axis=0)
    return (grad_values, grad_gain)


def vector_step(old_state, gradient):
    fresh_state = MOMENTUM * old_state + gradient
    inverse_rms = lax.rsqrt(
        jnp.mean(fresh_state * fresh_state, axis=-1, keepdims=True) + NORM_EPSILON
    )
    return (fresh_state, -VECTOR_STEP * fresh_state * inverse_rms)


def polynomials(gram):
    factor = 1.0 / (jnp.sqrt(jnp.trace(gram)) + 1e-07)
    gram_one = gram * (factor * factor)
    low_one = gram_one.astype(BF16)
    poly_one = (POLY_THREE * gram_one + POLY_FIVE * matmul(low_one, low_one)).astype(BF16)
    mixed = matmul(low_one, poly_one)
    gram_two = (
        (POLY_ONE * POLY_ONE) * gram_one
        + (2.0 * POLY_ONE) * mixed
        + matmul(poly_one, mixed.astype(BF16))
    )
    low_two = gram_two.astype(BF16)
    poly_two = (POLY_THREE * gram_two + POLY_FIVE * matmul(low_two, low_two)).astype(BF16)
    return factor, poly_one, poly_two


def advance(start, factor, poly_one, poly_two):
    middle = (factor * (POLY_ONE * start.astype(F32) + matmul(start, poly_one))).astype(BF16)
    return (POLY_ONE * middle.astype(F32) + matmul(middle, poly_two)).astype(BF16)


def shards(
    tokens,
    cotangent,
    block_position,
    w_query,
    key_weight,
    value_weight,
    w_output,
    w_gate,
    w_up,
    w_down,
    projection_bias,
    norm_gains,
    momentum_query,
    key_momentum,
    value_momentum,
    momentum_output,
    momentum_gate,
    momentum_up,
    momentum_down,
    bias_momentum,
    momentum_gains,
):
    shard_rows = tokens.shape[1]
    width = tokens.shape[2]
    ctx_count = lax.axis_size("ctx")
    z_count = lax.axis_size("fsdp")
    grid = Grid(ctx_count, z_count)
    y_count, x_count = grid.y_count, grid.x_count
    plane = y_count * x_count
    place_y, place_x, place_c, place_z = grid.place()
    ctx_rank = lax.axis_index("ctx")
    all_count = ctx_count * z_count
    half_block = shard_rows // 2
    query_width = QUERY_HEADS * HEAD_DIM
    key_value_width = KEY_VALUE_HEADS * HEAD_DIM
    heads_per_group = QUERY_HEADS // KEY_VALUE_HEADS
    grouped_rows = heads_per_group * shard_rows
    score_scale = 1.0 / math.sqrt(HEAD_DIM)
    weight_rows = w_query.shape[0]
    ff_rows = w_gate.shape[0]

    weight_block = jnp.concatenate([w_query, key_weight, value_weight, w_output], axis=1)
    weight_chunks = grid.gather(weight_block)
    weight_parts = []
    for chunk in weight_chunks:
        weight_parts += [chunk, grid.shift(chunk, dc=1)]
    full_weights = jnp.concatenate(weight_parts)
    qkv_width = query_width + 2 * key_value_width
    full_qkv = full_weights[:, :qkv_width]
    full_output = full_weights[:, qkv_width:]
    jy, jx, row = grid.plane_order(weight_rows)
    source_y = (place_y - jnp.asarray(jy)) % y_count
    source_x = (place_x - jnp.asarray(jx)) % x_count
    pieces = []
    for jz in range(z_count):
        for jc in range(CORES):
            device = ((source_y * x_count + source_x) * CORES + (place_c - jc) % CORES) * z_count
            pieces.append((device + (place_z - jz) % z_count) * weight_rows + jnp.asarray(row))
    relative_rows = jnp.concatenate(pieces)
    reorder = (jnp.arange(width, dtype=jnp.int32)[:, None] == relative_rows[None, :]).astype(BF16)

    inputs = tokens[0].astype(F32)
    grad_mid = cotangent[0]
    grad_out = grad_mid.astype(F32)
    gain_one = norm_gains[0].astype(F32)
    gain_two = norm_gains[1].astype(F32)
    bias_values = projection_bias.astype(F32)

    ff_block = jnp.concatenate([w_gate, w_up, w_down])
    ff_other = grid.shift(ff_block, dc=1)
    gate_pair = jnp.concatenate([w_gate, ff_other[:ff_rows]])
    up_pair = jnp.concatenate([w_up, ff_other[ff_rows : 2 * ff_rows]])
    down_pair = jnp.concatenate([w_down, ff_other[2 * ff_rows :]])

    own_positions = (
        lax.dynamic_slice_in_dim(block_position, 2 * ctx_rank, 2)[:, None] * half_block
        + jnp.arange(half_block, dtype=jnp.int32)[None, :]
    ).reshape(shard_rows)
    cosine_lookup, sine_lookup = rope_tables(own_positions, HEAD_DIM)
    row_positions = jnp.tile(own_positions, heads_per_group)
    scale_one = norm_scale(inputs)
    normed_one = (inputs * scale_one * gain_one).astype(BF16)
    normed_relative = matmul(normed_one, reorder).astype(BF16)
    projected = matmul(normed_relative, full_qkv) + bias_values
    value_lowered = projected[:, query_width + key_value_width :].astype(BF16)
    rotated_queries = apply_rotary(
        projected[:, :query_width].reshape(shard_rows, QUERY_HEADS, HEAD_DIM),
        cosine_lookup,
        sine_lookup,
    ).astype(BF16)
    rotated_keys = (
        apply_rotary(
            projected[:, query_width : query_width + key_value_width].reshape(
                shard_rows, KEY_VALUE_HEADS, HEAD_DIM
            ),
            cosine_lookup,
            sine_lookup,
        )
        .astype(BF16)
        .reshape(shard_rows, key_value_width)
    )
    key_value = jnp.concatenate([rotated_keys, value_lowered], axis=1)
    key_value = jnp.concatenate([key_value, grid.shift(key_value, dc=1)])
    places = [(jy_, jx_) for jy_ in range(y_count) for jx_ in range(x_count)]
    gathered = jnp.concatenate([grid.shift(key_value, dy=a, dx=b) for a, b in places])
    key_ctx = jnp.stack(
        [
            (((place_y - a) % y_count) * x_count + (place_x - b) % x_count) * CORES
            + (place_c - j) % CORES
            for a, b in places
            for j in range(CORES)
        ]
    )
    key_positions = (
        jnp.take(block_position.reshape(ctx_count, 2), key_ctx, axis=0)[:, :, None] * half_block
        + jnp.arange(half_block, dtype=jnp.int32)[None, None, :]
    ).reshape(shard_rows * ctx_count)
    seq_length = shard_rows * ctx_count
    all_keys = gathered[:, :key_value_width].reshape(seq_length, KEY_VALUE_HEADS, HEAD_DIM)
    all_values = gathered[:, key_value_width:].reshape(seq_length, KEY_VALUE_HEADS, HEAD_DIM)

    grad_chunks = grid.gather(after(grad_mid, weight_chunks[-1]))

    grouped_queries = (
        rotated_queries.reshape(shard_rows, KEY_VALUE_HEADS, heads_per_group, HEAD_DIM)
        .transpose(1, 2, 0, 3)
        .reshape(KEY_VALUE_HEADS, grouped_rows, HEAD_DIM)
    )
    visible = (key_positions[None, :] <= row_positions[:, None])[None]

    def attention_scores():
        raw = (
            jnp.einsum("hqd,khd->hqk", grouped_queries, all_keys, preferred_element_type=F32)
            * score_scale
        )
        return jnp.where(visible, raw, MASK_FILL)

    scores = attention_scores()
    row_peak = jnp.max(scores, axis=-1)
    log_total = row_peak + jnp.log(jnp.sum(jnp.exp(scores - row_peak[..., None]), axis=-1))
    soft = jnp.exp(scores - log_total[..., None])
    combined_heads = jnp.einsum(
        "hqk,khd->hqd", soft.astype(BF16), all_values, preferred_element_type=F32
    )
    attended = (
        combined_heads.reshape(KEY_VALUE_HEADS, heads_per_group, shard_rows, HEAD_DIM)
        .transpose(2, 0, 1, 3)
        .reshape(shard_rows, query_width)
        .astype(BF16)
    )
    attended_relative = matmul(attended, reorder).astype(BF16)
    hidden_one = inputs + matmul(attended_relative, full_output)
    scale_two = norm_scale(hidden_one)
    normed_two = (hidden_one * scale_two * gain_two).astype(BF16)

    normed_chunks = grid.gather(normed_two)
    hidden_parts, gate_parts, up_parts = [], [], []
    out_parts, normed_grad_parts = [], []
    for normed_chunk, grad_chunk in zip(normed_chunks, grad_chunks):
        gate_values = matmul_nt(normed_chunk, gate_pair)
        up_values = matmul_nt(normed_chunk, up_pair)
        grad_hidden = matmul_nt(grad_chunk, down_pair)
        sigmoid_gate = jax.nn.sigmoid(gate_values)
        active = gate_values * sigmoid_gate
        hidden = (active * up_values).astype(BF16)
        up_low = (grad_hidden * active).astype(BF16)
        gate_low = (
            grad_hidden * up_values * (sigmoid_gate * (1.0 + gate_values * (1.0 - sigmoid_gate)))
        ).astype(BF16)
        hidden_parts.append(hidden)
        gate_parts.append(gate_low)
        up_parts.append(up_low)
        out_parts.append(matmul(hidden, down_pair).astype(BF16))
        normed_grad_parts.append(
            (matmul(gate_low, gate_pair) + matmul(up_low, up_pair)).astype(BF16)
        )
    normed_all = jnp.concatenate(normed_chunks)
    grad_all = jnp.concatenate(grad_chunks)

    def own_rows(pair):
        other = grid.shift(pair[ff_rows:].astype(BF16), dc=1)
        return pair[:ff_rows] + other.astype(F32)

    grad_gate = own_rows(matmul_tn(jnp.concatenate(gate_parts), normed_all))
    grad_up = own_rows(matmul_tn(jnp.concatenate(up_parts), normed_all))
    grad_down = own_rows(matmul_tn(jnp.concatenate(hidden_parts), grad_all))
    moment_gate = MOMENTUM * momentum_gate + grad_gate
    moment_up = MOMENTUM * momentum_up + grad_up
    moment_down = MOMENTUM * momentum_down + grad_down

    ff_start = jnp.stack([m.astype(BF16) for m in (moment_gate, moment_up, moment_down)])
    ff_count = ff_start.shape[0]

    def weight_at(a, b):
        column = ((place_y + a) % y_count) * x_count + (place_x + b) % x_count
        return lax.dynamic_index_in_dim(
            ff_start, jnp.minimum(column, ff_count - 1), axis=0, keepdims=False
        )

    def has_weight(y, x):
        return y * x_count + x < ff_count

    current = jnp.concatenate(
        [grid.shift(weight_at(a, b), dy=a, dx=b, keep=has_weight) for a, b in places]
    )
    gram_part = matmul_tn(current, current).astype(BF16)
    half_rows = width // CORES
    kept = lax.dynamic_slice_in_dim(gram_part, place_c * half_rows, half_rows)
    sent = lax.dynamic_slice_in_dim(gram_part, (1 - place_c) * half_rows, half_rows)
    gram_half = (kept.astype(F32) + grid.shift(sent, dc=1).astype(F32)).astype(BF16)
    z_rows = half_rows // z_count
    gram_own = grid.z_sum(
        [
            lax.dynamic_slice_in_dim(gram_half, ((place_z - j) % z_count) * z_rows, z_rows)
            for j in range(z_count)
        ]
    ).astype(BF16)
    gram_half = jnp.zeros((half_rows, width), BF16)
    piece = gram_own
    for j in range(z_count):
        gram_half = lax.dynamic_update_slice_in_dim(
            gram_half, piece, ((place_z - j) % z_count) * z_rows, axis=0
        )
        if j + 1 < z_count:
            piece = grid.shift(piece, dz=1)
    gram_other = grid.shift(gram_half, dc=1)
    gram = jnp.where(
        place_c == 0,
        jnp.concatenate([gram_half, gram_other]),
        jnp.concatenate([gram_other, gram_half]),
    )
    moved = advance(current, *polynomials(gram.astype(F32)))
    back = jnp.stack(
        [
            grid.shift(moved[k * ff_rows : (k + 1) * ff_rows], dy=-a, dx=-b)
            for k, (a, b) in enumerate(places)
        ]
    )

    def ff_update(index):
        a = (index // x_count - place_y) % y_count
        b = (index % x_count - place_x) % x_count
        rows = lax.dynamic_index_in_dim(back, a * x_count + b, axis=0, keepdims=False)
        scale = -STEP_SCALE * math.sqrt(max(ff_rows * all_count, width))
        return scale * rows.astype(F32)

    update_gate, update_up, update_down = ff_update(0), ff_update(1), ff_update(2)

    grad_normed_two = grid.reduce(normed_grad_parts)
    grad_hidden_one, grad_gain_two = norm_back(hidden_one, scale_two, gain_two, grad_normed_two)
    grad_hidden_one = grad_hidden_one + grad_out
    grad_branch = grad_hidden_one.astype(BF16)
    attended_gradient = matmul_nt(
        matmul_nt(grad_branch, full_output).astype(BF16), reorder
    ).astype(BF16)
    grad_grouped = (
        attended_gradient.reshape(shard_rows, KEY_VALUE_HEADS, heads_per_group, HEAD_DIM)
        .transpose(1, 2, 0, 3)
        .reshape(KEY_VALUE_HEADS, grouped_rows, HEAD_DIM)
    )
    row_inner = jnp.sum(grad_grouped.astype(F32) * combined_heads, axis=-1)
    soft = jnp.exp(attention_scores() - log_total[..., None])
    grad_soft = jnp.einsum("hqd,khd->hqk", grad_grouped, all_values, preferred_element_type=F32)
    value_part = jnp.einsum(
        "hqk,hqd->khd", soft.astype(BF16), grad_grouped, preferred_element_type=F32
    )
    score_grad = (soft * (grad_soft - row_inner[..., None])).astype(BF16)
    query_part = jnp.einsum("hqk,khd->hqd", score_grad, all_keys, preferred_element_type=F32)
    key_part = jnp.einsum("hqk,hqd->khd", score_grad, grouped_queries, preferred_element_type=F32)
    key_value_grad = jnp.concatenate(
        [
            key_part.reshape(seq_length, key_value_width) * score_scale,
            value_part.reshape(seq_length, key_value_width),
        ],
        axis=1,
    ).astype(BF16)
    pair_rows = CORES * shard_rows
    pair_grad = sum(
        grid.shift(key_value_grad[k * pair_rows : (k + 1) * pair_rows], dy=-a, dx=-b).astype(F32)
        for k, (a, b) in enumerate(places)
    )
    key_value_sum = pair_grad[:shard_rows] + grid.shift(
        pair_grad[shard_rows:].astype(BF16), dc=1
    ).astype(F32)
    query_grad_heads = (
        (query_part * score_scale)
        .reshape(KEY_VALUE_HEADS, heads_per_group, shard_rows, HEAD_DIM)
        .transpose(2, 0, 1, 3)
        .reshape(shard_rows, QUERY_HEADS, HEAD_DIM)
    )
    query_grad_low = (
        apply_rotary(query_grad_heads, cosine_lookup, -sine_lookup)
        .astype(BF16)
        .reshape(shard_rows, query_width)
    )
    key_grad_low = (
        apply_rotary(
            key_value_sum[:, :key_value_width].reshape(shard_rows, KEY_VALUE_HEADS, HEAD_DIM),
            cosine_lookup,
            -sine_lookup,
        )
        .astype(BF16)
        .reshape(shard_rows, key_value_width)
    )
    value_grad_low = key_value_sum[:, key_value_width:].astype(BF16)
    qkv_grad_low = jnp.concatenate([query_grad_low, key_grad_low, value_grad_low], axis=1)

    weight_part = jnp.concatenate(
        [
            matmul_tn(normed_relative, qkv_grad_low).astype(BF16),
            matmul_tn(attended_relative, grad_branch).astype(BF16),
        ],
        axis=1,
    ).reshape(z_count, CORES, plane * weight_rows, qkv_width + width)
    other = grid.shift(weight_part[:, 1], dc=1)
    weight_sum = weight_part[:, 0].astype(F32) + other.astype(F32)
    attention_grads = grid.reduce([weight_sum[j].astype(BF16) for j in range(z_count)])
    grad_query = attention_grads[:, :query_width]
    grad_key = attention_grads[:, query_width : query_width + key_value_width]
    grad_value = attention_grads[:, query_width + key_value_width : qkv_width]
    grad_output = attention_grads[:, qkv_width:]

    normed_grad = matmul_nt(qkv_grad_low, full_qkv)
    high = normed_grad.astype(BF16)
    low = (normed_grad - high.astype(F32)).astype(BF16)
    grad_normed_one = matmul_nt(high, reorder) + matmul_nt(low, reorder)
    grad_inputs, grad_gain_one = norm_back(inputs, scale_one, gain_one, grad_normed_one)
    grad_tokens = (grad_inputs + grad_hidden_one)[None]
    vectors = lax.psum(
        jnp.concatenate(
            [jnp.sum(qkv_grad_low, axis=0, dtype=F32), grad_gain_one, grad_gain_two]
        ),
        ("ctx", "fsdp"),
    )
    grad_bias = vectors[:qkv_width]
    grad_gains = vectors[qkv_width:].reshape(2, width)
    moment_bias, update_bias = vector_step(bias_momentum, grad_bias)
    moment_gains, update_gains = vector_step(momentum_gains, grad_gains)

    moment_query = MOMENTUM * momentum_query + grad_query
    moment_key = MOMENTUM * key_momentum + grad_key
    moment_value = MOMENTUM * value_momentum + grad_value
    moment_output = MOMENTUM * momentum_output + grad_output
    query_key = jnp.concatenate([moment_query, moment_key], axis=1).astype(BF16)
    output_value = jnp.concatenate([moment_output, moment_value], axis=1).astype(BF16)
    mine = jnp.where(place_c == 0, query_key, output_value)
    theirs = jnp.where(place_c == 0, output_value, query_key)
    pair_start = jnp.concatenate([mine, grid.shift(theirs, dc=1)])
    start_all = jnp.concatenate(grid.gather(pair_start))
    large, small = start_all[:, :width], start_all[:, width:]
    large_new = advance(pair_start[:, :width], *polynomials(matmul_tn(large, large)))
    small_new = advance(pair_start[:, width:], *polynomials(matmul_tn(small, small)))
    pair_new = jnp.concatenate([large_new, small_new], axis=1)
    mine_new = pair_new[:weight_rows]
    theirs_new = grid.shift(pair_new[weight_rows:], dc=1)
    query_key_new = jnp.where(place_c == 0, mine_new, theirs_new).astype(F32)
    output_value_new = jnp.where(place_c == 0, theirs_new, mine_new).astype(F32)
    scale = -STEP_SCALE * math.sqrt(max(weight_rows * all_count, width))
    kv_scale = -STEP_SCALE * math.sqrt(max(weight_rows * all_count, key_value_width))
    update_query = scale * query_key_new[:, :width]
    update_key = kv_scale * query_key_new[:, width:]
    update_output = scale * output_value_new[:, :width]
    update_value = kv_scale * output_value_new[:, width:]

    out_tokens = (hidden_one + grid.reduce(out_parts)).astype(BF16)[None]
    return (
        out_tokens,
        grad_tokens,
        grad_query,
        grad_key,
        grad_value,
        grad_output,
        grad_gate,
        grad_up,
        grad_down,
        moment_query,
        moment_key,
        moment_value,
        moment_output,
        moment_gate,
        moment_up,
        moment_down,
        update_query,
        update_key,
        update_value,
        update_output,
        update_gate,
        update_up,
        update_down,
        grad_bias,
        moment_bias,
        update_bias,
        grad_gains,
        moment_gains,
        update_gains,
    )


def solution(mesh):
    tokens = P("fsdp", "ctx", None)
    rows = P(("ctx", "fsdp"), None)
    return jax.shard_map(
        shards,
        mesh=mesh,
        in_specs=(tokens, tokens, P()) + (rows,) * 7 + (P(), P()) + (rows,) * 7 + (P(), P()),
        out_specs=(tokens, tokens) + (rows,) * 21 + (P(),) * 6,
        check_vma=False,
    )
```

time: 1980 us -> 1110 us (0.56)
  waiting for transfers between devices: 1240 us -> 389 us
  blocking collectives: 355 us -> 65.8 us
  starting transfers between devices: 21.6 us -> 195 us
  local copies, waits for them, and re-layouts: 53.8 us -> 99.2 us
  matrix products: 242 us -> 279 us
    all_gather x7 -> x0, waiting for transfers between devices: 573 us -> none  [the longest x1 151 us: shards(): lax.all_gather(w_up, ('ctx', 'fsdp'), axis=0, tiled=True)]
    ppermute x0 -> x166, waiting for transfers between devices: none -> 389 us  [the longest x139 351 us: shift(): return lax.ppermute(value, 'ctx', pairs)]
    psum x2 -> x0, waiting for transfers between devices: 340 us -> none  [shards(): lax.psum(matmul_tn(current, current).astype(jnp.bfloat16), 'fsdp')]
    ppermute x0 -> x166, starting transfers between devices: none -> 195 us  [the longest x139 143 us: shift(): return lax.ppermute(value, 'ctx', pairs)]
    all_gather x4 -> x0, blocking collectives: 183 us -> none  [the longest x1 81.1 us: shards(): lax.all_gather(key_weight, ('ctx', 'fsdp'), axis=0, tiled=True)]
    all_to_all x4 -> x0, waiting for transfers between devices: 146 us -> none  [the longest x1 98.6 us: shards(): lax.all_to_all(up_store, ('ctx', 'fsdp'), split_axis=1, concat_axis=0, ti...]
    reduce_scatter x1 -> x0, waiting for transfers between devices: 122 us -> none  [shards(): lax.psum_scatter(jnp.concatenate([matmul_tn(normed_one, query_grad_low),...]
    dot_general x17 -> x37, matrix products: 117 us -> 206 us  [the longest x31 191 us: matmul(): return jnp.dot(left, right, preferred_element_type=F32)]
  transfers between devices with their start and end apart: 16 -> 166, of which waited for: 12 -> 91; matrix products, arithmetic and copies ran while one was open for 6% -> 30% of each run, Pallas kernels for 0% -> 0%
where the time goes in v1:
time: 1110 us; the launch traced here: 1100 us
  waiting for transfers between devices  389 us (35%)
  matrix products  279 us (25%)
  starting transfers between devices  195 us (18%)
  local copies, waits for them, and re-layouts  99.2 us (9%)
  blocking collectives  65.8 us (6%)
  other arithmetic  62.7 us (6%)
    ppermute x139, waiting for transfers between devices, shift(): return lax.ppermute(value, 'ctx', pairs)  351 us
    dot_general x31, matrix products, matmul(): return jnp.dot(left, right, preferred_element_type=F32)  191 us
    ppermute x139, starting transfers between devices, shift(): return lax.ppermute(value, 'ctx', pairs)  143 us
    unnamed x316, local copies, waits for them, and re-layouts  71.5 us
    psum x1, blocking collectives, shards(): lax.psum(jnp.concatenate([jnp.sum(qkv_grad_low, axis=0, dtype=F32), grad_...  65.8 us
    ppermute x27, starting transfers between devices, shift(): lax.ppermute(value, 'fsdp', [(z, (z + dz) % z_count) for z in range(z_cou...  52.1 us
    dot_general x8, matrix products, matmul_tn(): lax.dot_general(left, right, (((0,), (0,)), ((), ())), preferred_element_...  39.7 us
    ppermute x27, waiting for transfers between devices, shift(): lax.ppermute(value, 'fsdp', [(z, (z + dz) % z_count) for z in range(z_cou...  38.7 us
  transfers between devices with their start and end apart: 166, of which 91 were waited for; matrix products, arithmetic and copies ran while one was open for 30% of the time, Pallas kernels for 0%

profile of v1, /device:TPU:0, one launch (start us, length us, event | category | flops | bytes accessed | tf_op | source)
XLA Modules:
  0.0 1098.4 jit_solution(3594479417605652293)
XLA Ops:
  58.7 11.3 %collective-permute-done.8 = bf16[24,3584]{1,0:T(8,128)(2,1)S(1)} collective-permute-done((bf16[24,3584]{1,0:T(8,128)(2,1)S(1)}, bf16[24,3584]{1,0:T(8,128)(2,1)S(1)}, u32[]{:S(2)}, u32[]{:S(2)}) %collective-permute-start.8) | collective-permute-done | bytes 172064 | tf_op jit(solution)/shard_map/ppermute | solution.py:78
  70.7 8.6 collective-permute-done.9
  107.8 8.4 collective-permute-done.19
  191.5 11.5 %collective-permute-done.25 = bf16[256,512]{1,0:T(8,128)(2,1)S(1)} collective-permute-done((bf16[256,512]{1,0:T(8,128)(2,1)S(1)}, bf16[256,512]{1,0:T(8,128)(2,1)S(1)}, u32[]{:S(2)}, u32[]{:S(2)}) %collective-permute-start.25) | collective-permute-done | bytes 262176 | tf_op jit(solution)/shard_map/ppermute | solution.py:78
  278.6 7.7 collective-permute-done.32
  339.9 10.9 collective-permute-done.97
  493.2 10.2 collective-permute-start.103
  509.3 10.9 collective-permute-done.103
  580.8 8.8 convolution_convert_fusion
  612.7 65.8 %psum.7 = f32[5120]{0:T(1024)} all-reduce(f32[5120]{0:T(1024)} %pad_maximum_fusion.60), channel_id=1, replica_groups=mesh['ctx'=8,'fsdp'=4] {'ctx','fsdp'}, use_global_device_ids=true, to_apply=%region_13.14 | all-reduce | flops 5120 | bytes 40960 | tf_op jit(solution)/shard_map/psum | solution.py:534
  756.7 9.2 collective-permute-done.122
  788.8 7.6 collective-permute-done.135
  819.4 16.8 %fusion.5 = bf16[1536,1536]{1,0:T(8,128)(2,1)} fusion(f32[]{:T(128)S(6)} %mul.932, bf16[768,1536]{1,0:T(8,128)(2,1)S(1)} %constant_dynamic-update-slice_fusion.181, bf16[768,1536]{1,0:T(8,128)(2,1)} %collective-permute-done.162, pred[]{:T(512)S(6)} %eq.102), kind=kOutput, calls=%fused_computation.15 | convolution fusion | flops 7311458304 | bytes 9437189 | tf_op jit(solution)/shard_map/dot_general | solution.py:29
  836.2 11.2 %fusion.208 = f32[1120,1536]{1,0:T(8,128)} fusion(bf16[1536,1536]{1,0:T(8,128)(2,1)} %fusion.5, bf16[280,1536]{1,0:T(8,128)(2,1)} %collective-permute-done.154, bf16[280,1536]{1,0:T(8,128)(2,1)} %collective-permute-done.153, bf16[280,1536]{1,0:T(8,128)(2,1)} %collective-permute-done.152, bf16[280,1536]{1,0:T(8,128)(2,1)S(1)} %copy-done.40), kind=kOutput, calls=%fused_computation.709 | convolution fusion | flops 5298585600 | bytes 15040512 | tf_op jit(solution)/shard_map/dot_general | solution.py:29
  847.4 14.2 %fusion.39 = f32[1536,1536]{1,0:T(8,128)} fusion(bf16[1536,1536]{1,0:T(8,128)(2,1)S(1)} %copy-done.83, f32[]{:T(128)S(6)} %mul.932, bf16[768,1536]{1,0:T(8,128)(2,1)} %collective-permute-done.162, bf16[768,1536]{1,0:T(8,128)(2,1)S(1)} %constant_dynamic-update-slice_fusion.181, pred[]{:T(512)S(6)} %eq.102), kind=kOutput, calls=%fused_computation.67 | convolution fusion | flops 7276068864 | bytes 18874372 | tf_op jit(solution)/shard_map/dot_general | solution.py:29
  861.7 17.1 %fusion.7 = f32[1536,1536]{1,0:T(8,128)} fusion(f32[1536,1536]{1,0:T(8,128)} %fusion.39, bf16[1536,1536]{1,0:T(8,128)(2,1)} %fusion.5, f32[]{:T(128)S(6)} %mul.932, bf16[768,1536]{1,0:T(8,128)(2,1)S(1)} %constant_dynamic-update-slice_fusion.181, bf16[768,1536]{1,0:T(8,128)(2,1)} %collective-permute-done.162, pred[]{:T(512)S(6)} %eq.102), kind=kOutput, calls=%fused_computation.17 | convolution fusion | flops 7285506048 | bytes 28311556 | tf_op jit(solution)/shard_map/dot_general | solution.py:29
  878.7 28.5 %fusion.14 = bf16[1120,1536]{1,0:T(8,128)(2,1)S(1)} fusion(f32[1120,1536]{1,0:T(8,128)} %fusion.208, f32[]{:T(128)S(6)} %div.70, f32[1536,1536]{1,0:T(8,128)} %fusion.7, bf16[280,1536]{1,0:T(8,128)(2,1)} %collective-permute-done.154, bf16[280,1536]{1,0:T(8,128)(2,1)} %collective-permute-done.153, bf16[280,1536]{1,0:T(8,128)(2,1)} %collective-permute-done.152, ...), kind=kOutput, calls=%fused_computation.32 | convolution fusion | flops 12592545792 | bytes 23199748 | tf_op jit(solution)/shard_map/dot_general | solution.py:29
  923.6 36.3 %collective-permute-done.144 = bf16[48,1792]{1,0:T(8,128)(2,1)S(1)} collective-permute-done((bf16[48,1792]{1,0:T(8,128)(2,1)S(1)}, bf16[48,1792]{1,0:T(8,128)(2,1)S(1)}, u32[]{:S(2)}, u32[]{:S(2)}) %collective-permute-start.144) | collective-permute-done | bytes 172064 | tf_op jit(solution)/shard_map/ppermute | solution.py:78
  968.7 17.2 %collective-permute-done.145 = bf16[96,1792]{1,0:T(8,128)(2,1)S(1)} collective-permute-done((bf16[96,1792]{1,0:T(8,128)(2,1)S(1)}, bf16[96,1792]{1,0:T(8,128)(2,1)S(1)}, u32[]{:S(2)}, u32[]{:S(2)}) %collective-permute-start.145) | collective-permute-done | bytes 344096 | tf_op jit(solution)/shard_map/ppermute | solution.py:78
  1005.1 11.2 %select_reduce_fusion = (f32[]{:T(128)}, f32[1536,1536]{1,0:T(8,128)}) fusion(bf16[1536,1792]{1,0:T(8,128)(2,1)S(1)} %constant_dynamic-update-slice_fusion.157), kind=kOutput, calls=%fused_computation.23 | convolution fusion | flops 7254835200 | bytes 14155780 | tf_op jit(solution)/shard_map/dot_general | solution.py:37
  1022.4 15.2 %add_convert_fusion.2 = bf16[1536,1536]{1,0:T(8,128)(2,1)S(1)} fusion(f32[1536,1536]{1,0:T(8,128)} %get-tuple-element.321, f32[]{:T(128)S(6)} %mul.893), kind=kOutput, calls=%fused_computation.22 | convolution fusion | flops 7264272384 | bytes 14155780 | tf_op jit(solution)/shard_map/dot_general | solution.py:29
  1037.6 12.2 %fusion.29 = f32[1536,1536]{1,0:T(8,128)} fusion(bf16[1536,1536]{1,0:T(8,128)(2,1)S(1)} %add_convert_fusion.2, f32[1536,1536]{1,0:T(8,128)} %get-tuple-element.321, f32[]{:T(128)S(6)} %mul.893), kind=kOutput, calls=%fused_computation.57 | convolution fusion | flops 7252475904 | bytes 23592964 | tf_op jit(solution)/shard_map/dot_general | solution.py:29
  1049.8 19.0 %add_add_fusion = f32[1536,1536]{1,0:T(8,128)} fusion(f32[1536,1536]{1,0:T(8,128)} %fusion.29, bf16[1536,1536]{1,0:T(8,128)(2,1)S(1)} %add_convert_fusion.2, f32[1536,1536]{1,0:T(8,128)} %get-tuple-element.321, f32[]{:T(128)S(6)} %mul.893), kind=kOutput, calls=%fused_computation.21 | convolution fusion | flops 7261913088 | bytes 33030148 | tf_op jit(solution)/shard_map/dot_general | solution.py:29
  1073.0 19.9 %fusion.65 = bf16[96,1536]{1,0:T(8,128)(2,1)} fusion(f32[1536,1536]{1,0:T(8,128)} %add_add_fusion, f32[96,1536]{1,0:T(8,128)} %fusion.200, f32[]{:T(128)S(6)} %div.68, bf16[48,1792]{1,0:T(8,128)(2,1)} %copy-done.6, bf16[48,1792]{1,0:T(8,128)(2,1)} %copy-done.4), kind=kOutput, calls=%fused_computation.95 | convolution fusion | flops 7715487744 | bytes 21038080 | tf_op jit(solution)/shard_map/dot_general | solution.py:29
  (916 shorter events, 701.8 us)
Async XLA Ops:
  12.7 129.9 %collective-permute-start.31 = (bf16[840,1536]{1,0:T(8,128)(2,1)}, bf16[840,1536]{1,0:T(8,128)(2,1)}, u32[]{:S(2)}, u32[]{:S(2)}) collective-permute-start(bf16[840,1536]{1,0:T(8,128)(2,1)} %pad_maximum_fusion.3), channel_id=1, source_target_pairs={{0,4},{4,0},{8,12},{12,8},{16,20},{20,16},{24,28},{28,24},{1,5},{5... | collective-permute-start | bytes 7741448 | tf_op jit(solution)/shard_map/ppermute | solution.py:78
  159.5 150.5 %collective-permute-start.94 = (bf16[128,1536]{1,0:T(8,128)(2,1)}, bf16[128,1536]{1,0:T(8,128)(2,1)}, u32[]{:S(2)}, u32[]{:S(2)}) collective-permute-start(bf16[128,1536]{1,0:T(8,128)(2,1)} %collective-permute-done.84), channel_id=1, source_target_pairs={{0,1},{1,2},{2,3},{3,0},{4,5},{5,6},{6,7},{7,4},{8,9},{9,10},{10,1... | collective-permute-start | bytes 1179656 | tf_op jit(solution)/shard_map/ppermute | solution.py:67
  180.0 40.9 %collective-permute-start.76 = (bf16[128,1536]{1,0:T(8,128)(2,1)}, bf16[128,1536]{1,0:T(8,128)(2,1)S(1)}, u32[]{:S(2)}, u32[]{:S(2)}) collective-permute-start(bf16[128,1536]{1,0:T(8,128)(2,1)} %pad_maximum_fusion.24), channel_id=1, source_target_pairs={{0,16},{4,20},{8,24},{12,28},{16,0},{20,4},{24,8},{28,12},{1,17},{... | collective-permute-start | bytes 1179656 | tf_op jit(solution)/shard_map/ppermute | solution.py:78
  244.0 142.2 %collective-permute-start.56 = (bf16[128,1536]{1,0:T(8,128)(2,1)S(1)}, bf16[128,1536]{1,0:T(8,128)(2,1)S(1)}, u32[]{:S(2)}, u32[]{:S(2)}) collective-permute-start(bf16[128,1536]{1,0:T(8,128)(2,1)S(1)} %collective-permute-done.46), channel_id=1, source_target_pairs={{0,1},{1,2},{2,3},{3,0},{4,5},{5,6},{6,7},{7,4},{8,9},{9,10},{10,1... | collective-permute-start | bytes 1179656 | tf_op jit(solution)/shard_map/ppermute | solution.py:67
  370.5 137.3 %collective-permute-start.83 = (bf16[128,1536]{1,0:T(8,128)(2,1)S(1)}, bf16[128,1536]{1,0:T(8,128)(2,1)S(1)}, u32[]{:S(2)}, u32[]{:S(2)}) collective-permute-start(bf16[128,1536]{1,0:T(8,128)(2,1)S(1)} %pad_maximum_fusion.26), channel_id=1, source_target_pairs={{0,3},{1,0},{2,1},{3,2},{4,7},{5,4},{6,5},{7,6},{8,11},{9,8},{10,9... | collective-permute-start | bytes 1179656 | tf_op jit(solution)/shard_map/ppermute | solution.py:67
  374.9 147.9 %collective-permute-start.45 = (bf16[128,1536]{1,0:T(8,128)(2,1)S(1)}, bf16[128,1536]{1,0:T(8,128)(2,1)S(1)}, u32[]{:S(2)}, u32[]{:S(2)}) collective-permute-start(bf16[128,1536]{1,0:T(8,128)(2,1)S(1)} %pad_maximum_fusion.15), channel_id=1, source_target_pairs={{0,3},{1,0},{2,1},{3,2},{4,7},{5,4},{6,5},{7,6},{8,11},{9,8},{10,9... | collective-permute-start | bytes 1179656 | tf_op jit(solution)/shard_map/ppermute | solution.py:67
  420.3 87.5 %collective-permute-start.93 = (bf16[128,1536]{1,0:T(8,128)(2,1)S(1)}, bf16[128,1536]{1,0:T(8,128)(2,1)S(1)}, u32[]{:S(2)}, u32[]{:S(2)}) collective-permute-start(bf16[128,1536]{1,0:T(8,128)(2,1)S(1)} %pad_maximum_fusion.29), channel_id=1, source_target_pairs={{0,2},{1,3},{2,0},{3,1},{4,6},{5,7},{6,4},{7,5},{8,10},{9,11},{10,... | collective-permute-start | bytes 1179656 | tf_op jit(solution)/shard_map/ppermute | solution.py:67
  488.5 34.3 %collective-permute-start.55 = (bf16[128,1536]{1,0:T(8,128)(2,1)S(1)}, bf16[128,1536]{1,0:T(8,128)(2,1)S(1)}, u32[]{:S(2)}, u32[]{:S(2)}) collective-permute-start(bf16[128,1536]{1,0:T(8,128)(2,1)S(1)} %pad_maximum_fusion.18), channel_id=1, source_target_pairs={{0,2},{1,3},{2,0},{3,1},{4,6},{5,7},{6,4},{7,5},{8,10},{9,11},{10,... | collective-permute-start | bytes 1179656 | tf_op jit(solution)/shard_map/ppermute | solution.py:67
  507.8 69.6 %collective-permute-start.154 = (bf16[280,1536]{1,0:T(8,128)(2,1)}, bf16[280,1536]{1,0:T(8,128)(2,1)}, u32[]{:S(2)}, u32[]{:S(2)}) collective-permute-start(bf16[280,1536]{1,0:T(8,128)(2,1)} %get-tuple-element.94), channel_id=1, source_target_pairs={{8,16},{12,20},{16,8},{20,12},{24,0},{28,4},{9,17},{13,21},{17,9},... | collective-permute-start | bytes 2580488 | tf_op jit(solution)/shard_map/ppermute | solution.py:78
  520.1 57.3 %collective-permute-start.153 = (bf16[280,1536]{1,0:T(8,128)(2,1)}, bf16[280,1536]{1,0:T(8,128)(2,1)}, u32[]{:S(2)}, u32[]{:S(2)}) collective-permute-start(bf16[280,1536]{1,0:T(8,128)(2,1)} %get-tuple-element.95), channel_id=1, source_target_pairs={{0,16},{4,20},{16,0},{20,4},{24,8},{28,12},{1,17},{5,21},{17,1},{2... | collective-permute-start | bytes 2580488 | tf_op jit(solution)/shard_map/ppermute | solution.py:78
  577.3 106.2 %collective-permute-start.108 = (bf16[4,192,3584]{2,1,0:T(8,128)(2,1)}, bf16[4,192,3584]{2,1,0:T(8,128)(2,1)}, u32[]{:S(2)}, u32[]{:S(2)}) collective-permute-start(bf16[4,192,3584]{2,1,0:T(8,128)(2,1)} %slice_bitcast_fusion), channel_id=1, source_target_pairs={{0,4},{4,0},{8,12},{12,8},{16,20},{20,16},{24,28},{28,24},{1,5},{5... | collective-permute-start | bytes 16515080 | tf_op jit(solution)/shard_map/ppermute | solution.py:78
  603.4 77.1 %collective-permute-start.158 = (bf16[192,1536]{1,0:T(8,128)(2,1)S(1)}, bf16[192,1536]{1,0:T(8,128)(2,1)S(1)}, u32[]{:S(2)}, u32[]{:S(2)}) collective-permute-start(bf16[192,1536]{1,0:T(8,128)(2,1)S(1)} %get-tuple-element.101), channel_id=1, source_target_pairs={{0,1},{1,2},{2,3},{3,0},{4,5},{5,6},{6,7},{7,4},{8,9},{9,10},{10,1... | collective-permute-start | bytes 1769480 | tf_op jit(solution)/shard_map/ppermute | solution.py:67
  603.5 77.1 %collective-permute-start.157 = (bf16[192,1536]{1,0:T(8,128)(2,1)S(1)}, bf16[192,1536]{1,0:T(8,128)(2,1)}, u32[]{:S(2)}, u32[]{:S(2)}) collective-permute-start(bf16[192,1536]{1,0:T(8,128)(2,1)S(1)} %get-tuple-element.102), channel_id=1, source_target_pairs={{0,2},{1,3},{2,0},{3,1},{4,6},{5,7},{6,4},{7,5},{8,10},{9,11},{10,... | collective-permute-start | bytes 1769480 | tf_op jit(solution)/shard_map/ppermute | solution.py:67
  607.4 74.0 %collective-permute-start.156 = (bf16[192,1536]{1,0:T(8,128)(2,1)S(1)}, bf16[192,1536]{1,0:T(8,128)(2,1)}, u32[]{:S(2)}, u32[]{:S(2)}) collective-permute-start(bf16[192,1536]{1,0:T(8,128)(2,1)S(1)} %get-tuple-element.100), channel_id=1, source_target_pairs={{0,3},{1,0},{2,1},{3,2},{4,7},{5,4},{6,5},{7,6},{8,11},{9,8},{10,9... | collective-permute-start | bytes 1769480 | tf_op jit(solution)/shard_map/ppermute | solution.py:67
  724.4 54.0 %collective-permute-start.161 = (bf16[192,1536]{1,0:T(8,128)(2,1)S(1)}, bf16[192,1536]{1,0:T(8,128)(2,1)S(1)}, u32[]{:S(2)}, u32[]{:S(2)}) collective-permute-start(bf16[192,1536]{1,0:T(8,128)(2,1)S(1)} %collective-permute-done.160), channel_id=1, source_target_pairs={{0,1},{1,2},{2,3},{3,0},{4,5},{5,6},{6,7},{7,4},{8,9},{9,10},{10,1... | collective-permute-start | bytes 1769480 | tf_op jit(solution)/shard_map/ppermute | solution.py:67
  778.4 35.0 %collective-permute-start.162 = (bf16[768,1536]{1,0:T(8,128)(2,1)S(1)}, bf16[768,1536]{1,0:T(8,128)(2,1)}, u32[]{:S(2)}, u32[]{:S(2)}) collective-permute-start(bf16[768,1536]{1,0:T(8,128)(2,1)S(1)} %constant_dynamic-update-slice_fusion.181), channel_id=1, source_target_pairs={{0,4},{4,0},{8,12},{12,8},{16,20},{20,16},{24,28},{28,24},{1,5},{5... | collective-permute-start | bytes 7077896 | tf_op jit(solution)/shard_map/ppermute | solution.py:78
  804.6 102.6 %collective-permute-start.138 = (bf16[96,1792]{1,0:T(8,128)(2,1)}, bf16[96,1792]{1,0:T(8,128)(2,1)}, u32[]{:S(2)}, u32[]{:S(2)}) collective-permute-start(bf16[96,1792]{1,0:T(8,128)(2,1)} %pad_maximum_fusion.46), channel_id=1, source_target_pairs={{0,16},{4,20},{8,24},{12,28},{16,0},{20,4},{24,8},{28,12},{1,17},{... | collective-permute-start | bytes 1032200 | tf_op jit(solution)/shard_map/ppermute | solution.py:78
  807.8 104.3 %collective-permute-start.140 = (bf16[96,1792]{1,0:T(8,128)(2,1)}, bf16[96,1792]{1,0:T(8,128)(2,1)}, u32[]{:S(2)}, u32[]{:S(2)}) collective-permute-start(bf16[96,1792]{1,0:T(8,128)(2,1)} %pad_maximum_fusion.47), channel_id=1, source_target_pairs={{0,8},{4,12},{8,0},{12,4},{16,24},{20,28},{24,16},{28,20},{1,9},{5... | collective-permute-start | bytes 1032200 | tf_op jit(solution)/shard_map/ppermute | solution.py:78
  813.3 172.6 %collective-permute-start.146 = (bf16[96,1792]{1,0:T(8,128)(2,1)}, bf16[96,1792]{1,0:T(8,128)(2,1)}, u32[]{:S(2)}, u32[]{:S(2)}) collective-permute-start(bf16[96,1792]{1,0:T(8,128)(2,1)} %collective-permute-done.141), channel_id=1, source_target_pairs={{0,1},{1,2},{2,3},{3,0},{4,5},{5,6},{6,7},{7,4},{8,9},{9,10},{10,1... | collective-permute-start | bytes 1032200 | tf_op jit(solution)/shard_map/ppermute | solution.py:67
  916.7 80.3 %collective-permute-start.165 = (bf16[280,1536]{1,0:T(8,128)(2,1)S(1)}, bf16[280,1536]{1,0:T(8,128)(2,1)S(1)}, u32[]{:S(2)}, u32[]{:S(2)}) collective-permute-start(bf16[280,1536]{1,0:T(8,128)(2,1)S(1)} %get-tuple-element.90), channel_id=1, source_target_pairs={{0,24},{4,28},{8,16},{12,20},{16,8},{20,12},{24,0},{28,4},{1,25},{... | collective-permute-start | bytes 2580488 | tf_op jit(solution)/shard_map/ppermute | solution.py:78
  918.0 79.1 %collective-permute-start.164 = (bf16[280,1536]{1,0:T(8,128)(2,1)S(1)}, bf16[280,1536]{1,0:T(8,128)(2,1)S(1)}, u32[]{:S(2)}, u32[]{:S(2)}) collective-permute-start(bf16[280,1536]{1,0:T(8,128)(2,1)S(1)} %get-tuple-element.91), channel_id=1, source_target_pairs={{0,16},{4,20},{8,24},{12,28},{16,0},{20,4},{24,8},{28,12},{1,17},{... | collective-permute-start | bytes 2580488 | tf_op jit(solution)/shard_map/ppermute | solution.py:78
  919.3 40.6 %collective-permute-start.144 = (bf16[48,1792]{1,0:T(8,128)(2,1)S(1)}, bf16[48,1792]{1,0:T(8,128)(2,1)S(1)}, u32[]{:S(2)}, u32[]{:S(2)}) collective-permute-start(bf16[48,1792]{1,0:T(8,128)(2,1)S(1)} %get-tuple-element.229), channel_id=1, source_target_pairs={{0,16},{4,20},{8,24},{12,28},{16,0},{20,4},{24,8},{28,12},{1,17},{... | collective-permute-start | bytes 516104 | tf_op jit(solution)/shard_map/ppermute | solution.py:78
  922.9 43.1 %collective-permute-start.143 = (bf16[96,1792]{1,0:T(8,128)(2,1)S(1)}, bf16[96,1792]{1,0:T(8,128)(2,1)S(1)}, u32[]{:S(2)}, u32[]{:S(2)}) collective-permute-start(bf16[96,1792]{1,0:T(8,128)(2,1)S(1)} %pad_maximum_fusion.48), channel_id=1, source_target_pairs={{0,16},{4,20},{8,24},{12,28},{16,0},{20,4},{24,8},{28,12},{1,17},{... | collective-permute-start | bytes 1032200 | tf_op jit(solution)/shard_map/ppermute | solution.py:78
  960.0 37.0 %collective-permute-start.163 = (bf16[280,1536]{1,0:T(8,128)(2,1)S(1)}, bf16[280,1536]{1,0:T(8,128)(2,1)S(1)}, u32[]{:S(2)}, u32[]{:S(2)}) collective-permute-start(bf16[280,1536]{1,0:T(8,128)(2,1)S(1)} %get-tuple-element.92), channel_id=1, source_target_pairs={{0,8},{4,12},{8,0},{12,4},{16,24},{20,28},{24,16},{28,20},{1,9},{5... | collective-permute-start | bytes 2580488 | tf_op jit(solution)/shard_map/ppermute | solution.py:78
  (232 other events, 3246.4 us)

commit v2 on v1

v2 whole, which is shorter than its diff:
```python
import functools
import math

import jax
import jax.numpy as jnp
import numpy as np
from jax import lax
from jax.experimental import pallas as pl
from jax.experimental.pallas import tpu as pltpu
from jax.sharding import PartitionSpec as P

QUERY_HEADS = 12
KEY_VALUE_HEADS = 2
HEAD_DIM = 128
CORES = 2
TILE = 256
VMEM_BYTES = 56 * 2**20

NORM_EPSILON = 1e-06
ROPE_BASE = 1000000.0
POLY_ONE = 3.4445
POLY_THREE = -4.775
POLY_FIVE = 2.0315
MOMENTUM = 0.95
STEP_SCALE = 0.06
VECTOR_STEP = 0.1
MASK_FILL = -1e30

F32 = jnp.float32
BF16 = jnp.bfloat16


def matmul(left, right):
    return jnp.dot(left, right, preferred_element_type=F32)


def matmul_nt(left, right):
    return lax.dot_general(left, right, (((1,), (1,)), ((), ())), preferred_element_type=F32)


def matmul_tn(left, right):
    return lax.dot_general(left, right, (((0,), (0,)), ((), ())), preferred_element_type=F32)


def after(value, *others):
    return lax.optimization_barrier((value,) + others)[0]


class Grid:
    def __init__(self, ctx_count, z_count):
        plane = ctx_count // CORES
        x_count = math.isqrt(plane)
        while plane % x_count:
            x_count -= 1
        self.x_count, self.y_count, self.z_count = x_count, plane // x_count, z_count

    def place(self):
        ctx = lax.axis_index("ctx")
        return (
            ctx // (CORES * self.x_count),
            (ctx // CORES) % self.x_count,
            ctx % CORES,
            lax.axis_index("fsdp"),
        )

    def shift(self, value, dy=0, dx=0, dc=0, dz=0, dpair=0, dhigh=0, keep=None):
        y_count, x_count, z_count = self.y_count, self.x_count, self.z_count
        if dz or dpair or dhigh:
            pairs = []
            for z in range(z_count):
                high, low = (z // 2 + dhigh) % (z_count // 2), (z % 2 + dpair) % 2
                pairs.append((z, (high * 2 + low + dz) % z_count))
            return lax.ppermute(value, "fsdp", pairs)
        dy, dx, dc = dy % y_count, dx % x_count, dc % CORES
        if not (dy or dx or dc):
            return value
        pairs = []
        for y in range(y_count):
            for x in range(x_count):
                for c in range(CORES):
                    to_y, to_x, to_c = (y + dy) % y_count, (x + dx) % x_count, (c + dc) % CORES
                    if keep is None or keep(to_y, to_x):
                        pairs.append(
                            ((y * x_count + x) * CORES + c, (to_y * x_count + to_x) * CORES + to_c)
                        )
        return lax.ppermute(value, "ctx", pairs)

    def plane_gather(self, block):
        half = block.shape[0] // 2
        first, second = block[:half], block[half:]
        first = jnp.concatenate(
            [first] + [self.shift(first, dx=j) for j in range(1, self.x_count)]
        )
        second = jnp.concatenate(
            [second] + [self.shift(second, dy=j) for j in range(1, self.y_count)]
        )
        return jnp.concatenate(
            [first]
            + [self.shift(first, dy=j) for j in range(1, self.y_count)]
            + [second]
            + [self.shift(second, dx=j) for j in range(1, self.x_count)]
        )

    def plane_order(self, rows):
        half = rows // 2
        jy, jx, row = [], [], []
        for y in range(self.y_count):
            for x in range(self.x_count):
                for r in range(half):
                    jy.append(y), jx.append(x), row.append(r)
        for x in range(self.x_count):
            for y in range(self.y_count):
                for r in range(half, rows):
                    jy.append(y), jx.append(x), row.append(r)
        return np.array(jy), np.array(jx), np.array(row)

    def z_slots(self, block):
        return [block] + [self.shift(block, dz=j) for j in range(1, self.z_count)]

    def gather(self, slots):
        size = self.z_count // 2
        return [
            self.plane_gather(jnp.concatenate(slots[k : k + size]))
            for k in range(0, self.z_count, size)
        ]

    def gather_order(self, rows):
        size = self.z_count // 2
        jy, jx, row = self.plane_order(size * rows)
        jz = [k + row // rows for k in range(0, self.z_count, size)]
        return jz, jy, jx, row % rows

    def plane_reduce(self, part):
        def step(rows, count, axis):
            size = rows.shape[0] // count
            total = rows[:size].astype(F32)
            for j in range(1, count):
                piece = rows[j * size : (j + 1) * size].astype(BF16)
                total = total + self.shift(piece, **{axis: -j}).astype(F32)
            return total

        half = part.shape[0] // 2
        first = step(step(part[:half], self.y_count, "dy"), self.x_count, "dx")
        second = step(step(part[half:], self.x_count, "dx"), self.y_count, "dy")
        return jnp.concatenate([first, second])

    def z_sum(self, parts):
        total = parts[0].astype(F32)
        for j in range(1, self.z_count):
            total = total + self.shift(parts[j].astype(BF16), dz=-j).astype(F32)
        return total

    def reduce_plane(self, parts):
        slots = []
        for part in parts:
            total = self.plane_reduce(part)
            size = self.z_count // len(parts)
            rows = total.shape[0] // size
            slots += [total[k * rows : (k + 1) * rows] for k in range(size)]
        return slots

    def token_gather(self, block):
        slots = [block] + [self.shift(block, dhigh=j) for j in range(1, self.z_count // 2)]
        return [self.plane_gather(slot) for slot in slots]

    def token_reduce(self, parts):
        terms = [self.plane_reduce(parts[0])]
        for j in range(1, len(parts)):
            piece = self.plane_reduce(parts[j]).astype(BF16)
            terms.append(self.shift(piece, dhigh=-j))
        return terms

    def total(self, value):
        for axis, count in (("ctx", self.y_count * self.x_count * CORES), ("fsdp", self.z_count)):
            step = 1
            while step < count:
                value = value + lax.ppermute(value, axis, [(k, k ^ step) for k in range(count)])
                step *= 2
        return value


def rope_tables(positions, head_size):
    half_width = head_size // 2
    ratios = jnp.arange(half_width, dtype=F32) * (2.0 / head_size)
    frequency = jnp.exp(-math.log(ROPE_BASE) * ratios)
    angles = positions.astype(F32)[:, None] * frequency[None, :]
    cosine, sine = jnp.cos(angles), jnp.sin(angles)
    return jnp.concatenate([cosine, cosine], axis=1), jnp.concatenate([-sine, sine], axis=1)


def norm_scale(values):
    return lax.rsqrt(jnp.mean(values * values, axis=-1, keepdims=True) + NORM_EPSILON)


def norm_back(values, scale_rows, gain, grad_normed):
    weighted = grad_normed * gain
    inner_mean = jnp.mean(weighted * values, axis=-1, keepdims=True)
    grad_values = (
        scale_rows * weighted - values * (scale_rows * scale_rows * scale_rows) * inner_mean
    )
    grad_gain = jnp.sum(grad_normed * values * scale_rows, axis=0, keepdims=True)
    return (grad_values, grad_gain)


def rotate(head, cosine, sine):
    return head * cosine + pltpu.roll(head, HEAD_DIM // 2, 1) * sine


def head_columns(head):
    return slice(head * HEAD_DIM, (head + 1) * HEAD_DIM)


def by_pieces(rows, piece_refs):
    total, start = 0.0, 0
    for ref in piece_refs:
        size = ref.shape[0]
        total = total + matmul(rows[:, start : start + size], ref[...])
        start += size
    return total


def by_pieces_nt(rows, piece_refs):
    return jnp.concatenate([matmul_nt(rows, ref[...]) for ref in piece_refs], axis=1)


def compute(kernel, outs, args, flops, scratch=()):
    return pl.pallas_call(
        kernel,
        out_shape=[jax.ShapeDtypeStruct(shape, dtype) for shape, dtype in outs],
        scratch_shapes=scratch,
        compiler_params=pltpu.CompilerParams(vmem_limit_bytes=VMEM_BYTES),
        cost_estimate=pl.CostEstimate(flops=flops, bytes_accessed=2**20, transcendentals=0),
    )(*args)


def project_kernel(
    tokens_ref, gains_ref, bias_ref, cosine_ref, sine_ref, reorder_ref, *refs
):
    piece_refs, (normed_ref, query_ref, key_value_ref) = refs[:-3], refs[-3:]
    inputs = tokens_ref[...].astype(F32)
    normed = (inputs * norm_scale(inputs) * gains_ref[0:1, :].astype(F32)).astype(BF16)
    normed = matmul(normed, reorder_ref[...]).astype(BF16)
    normed_ref[...] = normed
    projected = by_pieces(normed, piece_refs) + bias_ref[...].astype(F32)
    cosine, sine = cosine_ref[...], sine_ref[...]
    for head in range(QUERY_HEADS):
        rotated = rotate(projected[:, head_columns(head)], cosine, sine)
        query_ref[:, head_columns(head)] = rotated.astype(BF16)
    for head in range(2 * KEY_VALUE_HEADS):
        values = projected[:, head_columns(QUERY_HEADS + head)]
        if head < KEY_VALUE_HEADS:
            values = rotate(values, cosine, sine)
        key_value_ref[:, head_columns(head)] = values.astype(BF16)


def attend_kernel(piece_count, tokens_ref, gains_ref, reorder_ref, query_ref, rows_ref, keys_ref, *refs):
    key_value_refs, refs = refs[:piece_count], refs[piece_count:]
    weight_refs, refs = refs[:-6], refs[-6:]
    mixed_ref, log_ref, attended_ref, hidden_ref, normed_ref, all_ref = refs
    size = key_value_refs[0].shape[0]
    for k, ref in enumerate(key_value_refs):
        all_ref[k * size : (k + 1) * size, :] = ref[...]
    visible = keys_ref[...] <= rows_ref[...]
    scale = 1.0 / math.sqrt(HEAD_DIM)
    group = QUERY_HEADS // KEY_VALUE_HEADS
    attended = []
    log_ref[...] = jnp.zeros(log_ref.shape, F32)
    for head in range(QUERY_HEADS):
        keys = all_ref[:, head_columns(head // group)]
        values = all_ref[:, head_columns(KEY_VALUE_HEADS + head // group)]
        scores = matmul_nt(query_ref[:, head_columns(head)], keys) * scale
        scores = jnp.where(visible, scores, MASK_FILL)
        peak = jnp.max(scores, axis=-1, keepdims=True)
        weights = jnp.exp(scores - peak)
        total = jnp.sum(weights, axis=-1, keepdims=True)
        log_ref[:, head : head + 1] = peak + jnp.log(total)
        mixed = matmul((weights * (1.0 / total)).astype(BF16), values)
        mixed_ref[:, head_columns(head)] = mixed
        attended.append(mixed.astype(BF16))
    attended = jnp.concatenate(attended, axis=1)
    attended = matmul(attended, reorder_ref[...]).astype(BF16)
    attended_ref[...] = attended
    hidden = tokens_ref[...].astype(F32) + by_pieces(attended, weight_refs)
    hidden_ref[...] = hidden
    normed_ref[...] = (hidden * norm_scale(hidden) * gains_ref[1:2, :].astype(F32)).astype(BF16)


def attend_back_kernel(
    piece_count,
    grad_count,
    cotangent_ref,
    gains_ref,
    hidden_ref,
    reorder_ref,
    query_ref,
    rows_ref,
    keys_ref,
    cosine_ref,
    sine_ref,
    mixed_ref,
    log_ref,
    *refs,
):
    grad_refs, refs = refs[:grad_count], refs[grad_count:]
    key_value_refs, refs = refs[:piece_count], refs[piece_count:]
    outs = 4 + piece_count
    weight_refs, refs = refs[: -outs - 3], refs[-outs - 3 :]
    hidden_grad_ref, branch_ref, gain_ref, query_grad_ref = refs[:4]
    piece_refs, (all_ref, key_sum, value_sum) = refs[4:outs], refs[outs:]
    size = key_value_refs[0].shape[0]
    for k, ref in enumerate(key_value_refs):
        all_ref[k * size : (k + 1) * size, :] = ref[...]
    hidden = hidden_ref[...]
    grad_normed = sum(ref[...].astype(F32) for ref in grad_refs)
    grad, grad_gain = norm_back(
        hidden, norm_scale(hidden), gains_ref[1:2, :].astype(F32), grad_normed
    )
    gain_ref[...] = grad_gain
    grad = grad + cotangent_ref[...].astype(F32)
    hidden_grad_ref[...] = grad
    branch = grad.astype(BF16)
    branch_ref[...] = branch
    attended_grad = by_pieces_nt(branch, weight_refs).astype(BF16)
    attended_grad = matmul_nt(attended_grad, reorder_ref[...]).astype(BF16)
    visible = keys_ref[...] <= rows_ref[...]
    scale = 1.0 / math.sqrt(HEAD_DIM)
    group = QUERY_HEADS // KEY_VALUE_HEADS
    cosine, sine = cosine_ref[...], sine_ref[...]
    for head in range(QUERY_HEADS):
        kind = head // group
        keys = all_ref[:, head_columns(kind)]
        values = all_ref[:, head_columns(KEY_VALUE_HEADS + kind)]
        query = query_ref[:, head_columns(head)]
        own = attended_grad[:, head_columns(head)]
        scores = matmul_nt(query, keys) * scale
        soft = jnp.exp(jnp.where(visible, scores, MASK_FILL) - log_ref[:, head : head + 1])
        inner = jnp.sum(
            own.astype(F32) * mixed_ref[:, head_columns(head)], axis=-1, keepdims=True
        )
        score_grad = (soft * (matmul_nt(own, values) - inner)).astype(BF16)
        query_grad = matmul(score_grad, keys) * scale
        query_grad_ref[:, head_columns(head)] = rotate(query_grad, cosine, -sine).astype(BF16)
        key_part = matmul_tn(score_grad, query)
        value_part = matmul_tn(soft.astype(BF16), own)
        if head % group == 0:
            key_sum[...] = key_part
            value_sum[...] = value_part
        else:
            key_sum[...] += key_part
            value_sum[...] += value_part
        if head % group == group - 1:
            for k, ref in enumerate(piece_refs):
                rows = slice(k * size, (k + 1) * size)
                ref[:, head_columns(kind)] = (key_sum[rows, :] * scale).astype(BF16)
                ref[:, head_columns(KEY_VALUE_HEADS + kind)] = value_sum[rows, :].astype(BF16)


def weights_back_kernel(
    tokens_ref,
    gains_ref,
    reorder_ref,
    cosine_ref,
    sine_ref,
    normed_ref,
    attended_ref,
    branch_ref,
    hidden_grad_ref,
    query_grad_ref,
    pair_ref,
    other_ref,
    *refs,
):
    weight_refs, refs = refs[:-6], refs[-6:]
    own_ref, sent_ref, tokens_grad_ref, bias_ref, gain_ref, grad_ref = refs
    query_width = query_grad_ref.shape[1]
    grad_ref[:, :query_width] = query_grad_ref[...]
    key_value = pair_ref[...] + other_ref[...].astype(F32)
    cosine, sine = cosine_ref[...], sine_ref[...]
    for head in range(2 * KEY_VALUE_HEADS):
        values = key_value[:, head_columns(head)]
        if head < KEY_VALUE_HEADS:
            values = rotate(values, cosine, -sine)
        grad_ref[:, head_columns(QUERY_HEADS + head)] = values.astype(BF16)
    grad = grad_ref[...]
    bias_ref[...] = jnp.sum(grad.astype(F32), axis=0, keepdims=True)
    qkv_width = grad.shape[1]
    branch = branch_ref[...]
    size = own_ref.shape[1]
    for k in range(2 * CORES):
        out = sent_ref if k % CORES else own_ref
        rows = slice(k * size, (k + 1) * size)
        out[k // CORES, :, :qkv_width] = matmul_tn(normed_ref[:, rows], grad).astype(BF16)
        out[k // CORES, :, qkv_width:] = matmul_tn(attended_ref[:, rows], branch).astype(BF16)
    normed_grad = by_pieces_nt(grad, weight_refs)
    high = normed_grad.astype(BF16)
    low = (normed_grad - high.astype(F32)).astype(BF16)
    reorder = reorder_ref[...]
    normed_grad = matmul_nt(high, reorder) + matmul_nt(low, reorder)
    inputs = tokens_ref[...].astype(F32)
    grad, grad_gain = norm_back(
        inputs, norm_scale(inputs), gains_ref[0:1, :].astype(F32), normed_grad
    )
    gain_ref[...] = grad_gain
    tokens_grad_ref[...] = grad + hidden_grad_ref[...]


def vector_step(old_state, gradient):
    fresh_state = MOMENTUM * old_state + gradient
    inverse_rms = lax.rsqrt(
        jnp.mean(fresh_state * fresh_state, axis=-1, keepdims=True) + NORM_EPSILON
    )
    return (fresh_state, -VECTOR_STEP * fresh_state * inverse_rms)


def packed_height(width):
    count = width // TILE
    return count * (count + 1) // 2 * TILE


def packed_block(row, column, count):
    return pl.ds((row * count - row * (row - 1) // 2 + column - row) * TILE, TILE)


def block_rows(index):
    return slice(index * TILE, (index + 1) * TILE)


def gram_kernel(start_ref, packed_ref):
    count = start_ref.shape[1] // TILE
    for i in range(count):
        row = lax.dot_general(
            start_ref[:, block_rows(i)],
            start_ref[:, i * TILE :],
            (((0,), (0,)), ((), ())),
            preferred_element_type=F32,
        )
        for j in range(i, count):
            packed_ref[packed_block(i, j, count), :] = row[:, block_rows(j - i)].astype(
                packed_ref.dtype
            )


def gram_packed(start, dtype):
    rows, width = start.shape
    height = packed_height(width)
    return pl.pallas_call(
        gram_kernel,
        out_shape=jax.ShapeDtypeStruct((height, TILE), dtype),
        compiler_params=pltpu.CompilerParams(vmem_limit_bytes=VMEM_BYTES),
        cost_estimate=pl.CostEstimate(
            flops=rows * width * width,
            bytes_accessed=2 * rows * width + 4 * height * TILE,
            transcendentals=0,
        ),
    )(start)


def chain_kernel(packed_ref, start_ref, new_ref, low, poly, mixed, two):
    count = start_ref.shape[1] // TILE

    def put(ref, i, j, block):
        ref[block_rows(i), block_rows(j)] = block
        if i != j:
            ref[block_rows(j), block_rows(i)] = block.T

    def product(left, right):
        for i in range(count):
            row = jnp.dot(left[block_rows(i), :], right[:, i * TILE :], preferred_element_type=F32)
            for j in range(i, count):
                yield i, j, row[:, block_rows(j - i)]

    same = lax.broadcasted_iota(jnp.int32, (TILE, TILE), 0) == lax.broadcasted_iota(
        jnp.int32, (TILE, TILE), 1
    )
    trace = jnp.zeros((1, 1), F32)
    for i in range(count):
        block = packed_ref[packed_block(i, i, count), :].astype(F32)
        trace = trace + jnp.sum(jnp.where(same, block, 0.0), keepdims=True)
    factor = 1.0 / (jnp.sqrt(trace) + 1e-07)
    square = factor * factor

    def gram_one(i, j):
        return packed_ref[packed_block(i, j, count), :].astype(F32) * square

    for i in range(count):
        for j in range(i, count):
            put(low, i, j, gram_one(i, j).astype(BF16))
    for i, j, block in product(low, low):
        put(poly, i, j, (POLY_THREE * gram_one(i, j) + POLY_FIVE * block).astype(BF16))
    for i, j, block in product(low, poly):
        two[packed_block(i, j, count), :] = (POLY_ONE * POLY_ONE) * gram_one(i, j) + (
            2.0 * POLY_ONE
        ) * block
        put(mixed, i, j, block.astype(BF16))
    for i, j, block in product(poly, mixed):
        block = two[packed_block(i, j, count), :] + block
        two[packed_block(i, j, count), :] = block
        put(low, i, j, block.astype(BF16))
    start = start_ref[...]
    middle = jnp.dot(start, poly[...], preferred_element_type=F32)
    middle = (factor * (POLY_ONE * start.astype(F32) + middle)).astype(BF16)
    for i, j, block in product(low, low):
        block = POLY_THREE * two[packed_block(i, j, count), :] + POLY_FIVE * block
        put(mixed, i, j, block.astype(BF16))
    new = jnp.dot(middle, mixed[...], preferred_element_type=F32)
    new_ref[...] = (POLY_ONE * middle.astype(F32) + new).astype(BF16)


def orthogonalize(packed, start):
    rows, width = start.shape
    return pl.pallas_call(
        chain_kernel,
        out_shape=jax.ShapeDtypeStruct(start.shape, BF16),
        scratch_shapes=[
            pltpu.VMEM((width, width), BF16),
            pltpu.VMEM((width, width), BF16),
            pltpu.VMEM((width, width), BF16),
            pltpu.VMEM((packed_height(width), TILE), F32),
        ],
        compiler_params=pltpu.CompilerParams(vmem_limit_bytes=VMEM_BYTES),
        cost_estimate=pl.CostEstimate(
            flops=5 * width**3 + 4 * rows * width * width,
            bytes_accessed=4 * rows * width + 4 * packed_height(width) * TILE,
            transcendentals=0,
        ),
    )(packed, start)


def shards(
    tokens,
    cotangent,
    block_position,
    w_query,
    key_weight,
    value_weight,
    w_output,
    w_gate,
    w_up,
    w_down,
    projection_bias,
    norm_gains,
    momentum_query,
    key_momentum,
    value_momentum,
    momentum_output,
    momentum_gate,
    momentum_up,
    momentum_down,
    bias_momentum,
    momentum_gains,
):
    shard_rows = tokens.shape[1]
    width = tokens.shape[2]
    ctx_count = lax.axis_size("ctx")
    z_count = lax.axis_size("fsdp")
    grid = Grid(ctx_count, z_count)
    y_count, x_count = grid.y_count, grid.x_count
    plane = y_count * x_count
    place_y, place_x, place_c, place_z = grid.place()
    ctx_rank = lax.axis_index("ctx")
    all_count = ctx_count * z_count
    half_block = shard_rows // 2
    query_width = QUERY_HEADS * HEAD_DIM
    key_value_width = KEY_VALUE_HEADS * HEAD_DIM
    weight_rows = w_query.shape[0]
    ff_rows = w_gate.shape[0]

    def both_cores(chunks):
        parts = []
        for chunk in chunks:
            parts += [chunk, grid.shift(chunk, dc=1)]
        return parts

    qkv_width = query_width + 2 * key_value_width
    qkv_slots = grid.z_slots(jnp.concatenate([w_query, key_weight, value_weight], axis=1))
    qkv_chunks = grid.gather(qkv_slots)
    qkv_pieces = both_cores(qkv_chunks)
    output_slots = grid.z_slots(after(w_output, qkv_slots[-1]))
    output_chunks = grid.gather(after(output_slots, *qkv_chunks))
    output_pieces = both_cores(output_chunks)
    tokens = after(tokens, qkv_slots[-1])
    place_y, place_x, place_c, place_z = after(
        (place_y, place_x, place_c, place_z), qkv_slots[-1]
    )
    jz_parts, jy, jx, row = grid.gather_order(weight_rows)
    source_y = (place_y - jnp.asarray(jy)) % y_count
    source_x = (place_x - jnp.asarray(jx)) % x_count
    pieces = []
    for jz in jz_parts:
        source_z = (place_z - jnp.asarray(jz)) % z_count
        for jc in range(CORES):
            source_ctx = (source_y * x_count + source_x) * CORES + (place_c - jc) % CORES
            pieces.append((source_ctx * z_count + source_z) * weight_rows + jnp.asarray(row))
    relative_rows = jnp.concatenate(pieces)
    reorder = (jnp.arange(width, dtype=jnp.int32)[:, None] == relative_rows[None, :]).astype(BF16)

    own_tokens = tokens[0]
    grad_mid = cotangent[0]

    own_positions = (
        lax.dynamic_slice_in_dim(block_position, 2 * ctx_rank, 2)[:, None] * half_block
        + jnp.arange(half_block, dtype=jnp.int32)[None, :]
    ).reshape(shard_rows)
    cosine_lookup, sine_lookup = rope_tables(own_positions, HEAD_DIM)
    row_positions = own_positions[:, None]
    normed_relative, queries, key_value = compute(
        project_kernel,
        [
            ((shard_rows, width), BF16),
            ((shard_rows, query_width), BF16),
            ((shard_rows, 2 * key_value_width), BF16),
        ],
        [
            own_tokens,
            norm_gains,
            projection_bias[None, :],
            cosine_lookup,
            sine_lookup,
            reorder,
            *qkv_pieces,
        ],
        2 * shard_rows * width * qkv_width,
    )
    key_value_pair = jnp.concatenate([key_value, grid.shift(key_value, dc=1)])
    places = [(jy_, jx_) for jy_ in range(y_count) for jx_ in range(x_count)]
    key_value_pieces = [grid.shift(key_value_pair, dy=a, dx=b) for a, b in places]
    key_ctx = jnp.stack(
        [
            (((place_y - a) % y_count) * x_count + (place_x - b) % x_count) * CORES
            + (place_c - j) % CORES
            for a, b in places
            for j in range(CORES)
        ]
    )
    key_positions = (
        jnp.take(block_position.reshape(ctx_count, 2), key_ctx, axis=0)[:, :, None] * half_block
        + jnp.arange(half_block, dtype=jnp.int32)[None, None, :]
    ).reshape(1, shard_rows * ctx_count)
    seq_length = shard_rows * ctx_count

    shared = 2 * CORES
    ff_block = after(jnp.concatenate([w_gate, w_up, w_down]), qkv_slots[-1], output_slots[-1])
    ff_chip = jnp.concatenate([ff_block, grid.shift(ff_block, dpair=1)])
    ff_chip = after(ff_chip, key_value)
    ff_all = jnp.concatenate([ff_chip, grid.shift(ff_chip, dc=1)])
    ff_all = ff_all.reshape(shared, 3, ff_rows, width)
    gate_shared, up_shared, down_shared = (
        ff_all[:, k].reshape(shared * ff_rows, width) for k in range(3)
    )

    grad_chunks = grid.token_gather(after(grad_mid, output_chunks[-1]))

    mixed, log_total, attended_relative, hidden_one, normed_two = compute(
        functools.partial(attend_kernel, plane),
        [
            ((shard_rows, query_width), F32),
            ((shard_rows, HEAD_DIM), F32),
            ((shard_rows, query_width), BF16),
            ((shard_rows, width), F32),
            ((shard_rows, width), BF16),
        ],
        [
            own_tokens,
            norm_gains,
            reorder,
            queries,
            row_positions,
            key_positions,
            *key_value_pieces,
            *output_pieces,
        ],
        4 * shard_rows * width * width,
        [pltpu.VMEM((seq_length, 2 * key_value_width), BF16)],
    )

    normed_chunks = grid.token_gather(normed_two)
    out_parts, normed_grad_parts = [], []
    gate_sum = up_sum = down_sum = 0.0
    for normed_chunk, grad_chunk in zip(normed_chunks, grad_chunks):
        gate_values = matmul_nt(normed_chunk, gate_shared)
        up_values = matmul_nt(normed_chunk, up_shared)
        grad_hidden = matmul_nt(grad_chunk, down_shared)
        sigmoid_gate = jax.nn.sigmoid(gate_values)
        active = gate_values * sigmoid_gate
        hidden = (active * up_values).astype(BF16)
        up_low = (grad_hidden * active).astype(BF16)
        gate_low = (
            grad_hidden * up_values * (sigmoid_gate * (1.0 + gate_values * (1.0 - sigmoid_gate)))
        ).astype(BF16)
        normed_grad_parts.append(
            (matmul(gate_low, gate_shared) + matmul(up_low, up_shared)).astype(BF16)
        )
        gate_sum = gate_sum + matmul_tn(gate_low, normed_chunk)
        up_sum = up_sum + matmul_tn(up_low, normed_chunk)
        down_sum = down_sum + matmul_tn(hidden, grad_chunk)
        out_parts.append(matmul(hidden, down_shared).astype(BF16))

    def own_rows(total):
        chip_rows = 2 * ff_rows
        other = grid.shift(total[chip_rows:].astype(BF16), dc=1)
        chip_sum = total[:chip_rows] + other.astype(F32)
        piece = grid.shift(chip_sum[ff_rows:].astype(BF16), dpair=1)
        return chip_sum[:ff_rows] + piece.astype(F32)

    grad_gate, grad_up, grad_down = own_rows(gate_sum), own_rows(up_sum), own_rows(down_sum)
    moment_gate = MOMENTUM * momentum_gate + grad_gate
    moment_up = MOMENTUM * momentum_up + grad_up
    moment_down = MOMENTUM * momentum_down + grad_down

    normed_grad_sums = grid.token_reduce(normed_grad_parts)
    hidden_grad, grad_branch, grad_gain_two, query_grad, *key_value_grads = compute(
        functools.partial(attend_back_kernel, plane, len(normed_grad_sums)),
        [
            ((shard_rows, width), F32),
            ((shard_rows, width), BF16),
            ((1, width), F32),
            ((shard_rows, query_width), BF16),
        ]
        + [((CORES * shard_rows, 2 * key_value_width), BF16)] * plane,
        [
            grad_mid,
            norm_gains,
            hidden_one,
            reorder,
            queries,
            row_positions,
            key_positions,
            cosine_lookup,
            sine_lookup,
            mixed,
            log_total,
            *normed_grad_sums,
            *key_value_pieces,
            *output_pieces,
        ],
        4 * shard_rows * width * width,
        [
            pltpu.VMEM((seq_length, 2 * key_value_width), BF16),
            pltpu.VMEM((seq_length, HEAD_DIM), F32),
            pltpu.VMEM((seq_length, HEAD_DIM), F32),
        ],
    )
    pair_grad = sum(
        grid.shift(piece, dy=-a, dx=-b).astype(F32)
        for piece, (a, b) in zip(key_value_grads, places)
    )
    key_value_other = grid.shift(pair_grad[shard_rows:].astype(BF16), dc=1)

    weight_shape = (2, weight_rows * all_count // (2 * CORES), qkv_width + width)
    weight_own, weight_sent, grad_tokens, bias_term, grad_gain_one = compute(
        weights_back_kernel,
        [
            (weight_shape, BF16),
            (weight_shape, BF16),
            ((shard_rows, width), F32),
            ((1, qkv_width), F32),
            ((1, width), F32),
        ],
        [
            own_tokens,
            norm_gains,
            reorder,
            cosine_lookup,
            sine_lookup,
            normed_relative,
            attended_relative,
            grad_branch,
            hidden_grad,
            query_grad,
            pair_grad[:shard_rows],
            key_value_other,
            *qkv_pieces,
        ],
        4 * shard_rows * width * qkv_width,
        [pltpu.VMEM((shard_rows, qkv_width), BF16)],
    )
    other = grid.shift(weight_sent, dc=1)
    weight_sum = (weight_own.astype(F32) + other.astype(F32)).astype(BF16)
    attention_slots = grid.reduce_plane([weight_sum[j] for j in range(2)])
    attention_grads = grid.z_sum(attention_slots)
    grad_query = attention_grads[:, :query_width]
    grad_key = attention_grads[:, query_width : query_width + key_value_width]
    grad_value = attention_grads[:, query_width + key_value_width : qkv_width]
    grad_output = attention_grads[:, qkv_width:]

    vectors = grid.total(
        jnp.concatenate([bias_term, grad_gain_one, grad_gain_two], axis=1).reshape(-1, HEAD_DIM)
    ).reshape(-1)
    grad_bias = vectors[:qkv_width]
    grad_gains = vectors[qkv_width:].reshape(2, width)
    moment_bias, update_bias = vector_step(bias_momentum, grad_bias)
    moment_gains, update_gains = vector_step(momentum_gains, grad_gains)

    moment_query = MOMENTUM * momentum_query + grad_query
    moment_key = MOMENTUM * key_momentum + grad_key
    moment_value = MOMENTUM * value_momentum + grad_value
    moment_output = MOMENTUM * momentum_output + grad_output
    query_key = jnp.concatenate([moment_query, moment_key], axis=1).astype(BF16)
    output_value = jnp.concatenate([moment_output, moment_value], axis=1).astype(BF16)
    mine = jnp.where(place_c == 0, query_key, output_value)
    theirs = jnp.where(place_c == 0, output_value, query_key)
    pair_start = jnp.concatenate([mine, grid.shift(theirs, dc=1)])
    start_slots = grid.z_slots(pair_start)
    start_all = jnp.concatenate(grid.gather(start_slots))

    ff_start = jnp.stack([m.astype(BF16) for m in (moment_gate, moment_up, moment_down)])
    ff_start = after(ff_start, *attention_slots)
    ff_count = ff_start.shape[0]

    def weight_at(a, b):
        column = ((place_y + a) % y_count) * x_count + (place_x + b) % x_count
        return lax.dynamic_index_in_dim(
            ff_start, jnp.minimum(column, ff_count - 1), axis=0, keepdims=False
        )

    def has_weight(y, x):
        return y * x_count + x < ff_count

    current = jnp.concatenate(
        [grid.shift(weight_at(a, b), dy=a, dx=b, keep=has_weight) for a, b in places]
    )
    current = after(current, pair_start)
    gram_part = gram_packed(current, BF16)
    half_rows = gram_part.shape[0] // CORES
    kept = lax.dynamic_slice_in_dim(gram_part, place_c * half_rows, half_rows)
    sent = lax.dynamic_slice_in_dim(gram_part, (1 - place_c) * half_rows, half_rows)
    gram_half = (kept.astype(F32) + grid.shift(sent, dc=1).astype(F32)).astype(BF16)
    gram_half = after(gram_half, *start_slots)
    z_rows = half_rows // z_count
    gram_own = grid.z_sum(
        [
            lax.dynamic_slice_in_dim(gram_half, ((place_z - j) % z_count) * z_rows, z_rows)
            for j in range(z_count)
        ]
    ).astype(BF16)
    gram_half = jnp.zeros((half_rows, TILE), BF16)
    for j, piece in enumerate(grid.z_slots(gram_own)):
        gram_half = lax.dynamic_update_slice_in_dim(
            gram_half, piece, ((place_z - j) % z_count) * z_rows, axis=0
        )
    gram_other = grid.shift(gram_half, dc=1)
    gram = jnp.where(
        place_c == 0,
        jnp.concatenate([gram_half, gram_other]),
        jnp.concatenate([gram_other, gram_half]),
    )
    moved = orthogonalize(after(gram, start_all), current)
    back = jnp.stack(
        [
            grid.shift(moved[k * ff_rows : (k + 1) * ff_rows], dy=-a, dx=-b)
            for k, (a, b) in enumerate(places)
        ]
    )

    def ff_update(index):
        a = (index // x_count - place_y) % y_count
        b = (index % x_count - place_x) % x_count
        rows = lax.dynamic_index_in_dim(back, a * x_count + b, axis=0, keepdims=False)
        scale = -STEP_SCALE * math.sqrt(max(ff_rows * all_count, width))
        return scale * rows.astype(F32)

    update_gate, update_up, update_down = ff_update(0), ff_update(1), ff_update(2)

    start_all = after(start_all, moved)
    large, small = start_all[:, :width], start_all[:, width:]
    large_new = orthogonalize(gram_packed(large, F32), pair_start[:, :width])
    small_new = orthogonalize(gram_packed(small, F32), pair_start[:, width:])
    pair_new = jnp.concatenate([large_new, small_new], axis=1)
    mine_new = pair_new[:weight_rows]
    theirs_new = grid.shift(pair_new[weight_rows:], dc=1)
    query_key_new = jnp.where(place_c == 0, mine_new, theirs_new).astype(F32)
    output_value_new = jnp.where(place_c == 0, theirs_new, mine_new).astype(F32)
    scale = -STEP_SCALE * math.sqrt(max(weight_rows * all_count, width))
    kv_scale = -STEP_SCALE * math.sqrt(max(weight_rows * all_count, key_value_width))
    update_query = scale * query_key_new[:, :width]
    update_key = kv_scale * query_key_new[:, width:]
    update_output = scale * output_value_new[:, :width]
    update_value = kv_scale * output_value_new[:, width:]

    out_terms = grid.token_reduce([after(part, pair_grad) for part in out_parts])
    out_tokens = sum((term.astype(F32) for term in out_terms), hidden_one).astype(BF16)[None]
    return (
        out_tokens,
        grad_tokens[None],
        grad_query,
        grad_key,
        grad_value,
        grad_output,
        grad_gate,
        grad_up,
        grad_down,
        moment_query,
        moment_key,
        moment_value,
        moment_output,
        moment_gate,
        moment_up,
        moment_down,
        update_query,
        update_key,
        update_value,
        update_output,
        update_gate,
        update_up,
        update_down,
        grad_bias,
        moment_bias,
        update_bias,
        grad_gains,
        moment_gains,
        update_gains,
    )


def solution(mesh):
    tokens = P("fsdp", "ctx", None)
    rows = P(("ctx", "fsdp"), None)
    return jax.shard_map(
        shards,
        mesh=mesh,
        in_specs=(tokens, tokens, P()) + (rows,) * 7 + (P(), P()) + (rows,) * 7 + (P(), P()),
        out_specs=(tokens, tokens) + (rows,) * 21 + (P(),) * 6,
        check_vma=False,
    )
```

time: 1110 us -> 787 us (0.71)
  matrix products: 279 us -> 49 us
  Pallas kernels: 0 us -> 128 us
  starting transfers between devices: 195 us -> 126 us
  blocking collectives: 65.8 us -> 0 us
  local copies, waits for them, and re-layouts: 99.2 us -> 50.8 us
  waiting for transfers between devices: 389 us -> 343 us
    dot_general x31 -> x6, matrix products: 191 us -> 18.3 us  [matmul(): return jnp.dot(left, right, preferred_element_type=F32)]
    pallas_call x0 -> x10, Pallas kernels: none -> 128 us  [the longest x3 59.5 us: orthogonalize(): pl.pallas_call(chain_kernel, out_shape=jax.ShapeDtypeStruct(start.shape,...]
    ppermute x139 -> x91, waiting for transfers between devices: 351 us -> 229 us  [shift(): return lax.ppermute(value, 'ctx', pairs)]
    ppermute x27 -> x31, waiting for transfers between devices: 38.7 us -> 113 us  [the longest x26 111 us: shift(): return lax.ppermute(value, 'fsdp', pairs)]
    psum x1 -> x0, blocking collectives: 65.8 us -> none  [shards(): lax.psum(jnp.concatenate([jnp.sum(qkv_grad_low, axis=0, dtype=F32), grad_...]
    ppermute x139 -> x91, starting transfers between devices: 143 us -> 82.6 us  [shift(): return lax.ppermute(value, 'ctx', pairs)]
    unnamed x316 -> x191, local copies, waits for them, and re-layouts: 71.5 us -> 25.8 us
    dot_general x8 -> x6, matrix products: 39.7 us -> 16.5 us  [matmul_tn(): lax.dot_general(left, right, (((0,), (0,)), ((), ())), preferred_element_...]
  transfers between devices with their start and end apart: 166 -> 122, of which waited for: 91 -> 60; matrix products, arithmetic and copies ran while one was open for 30% -> 16% of each run, Pallas kernels for 0% -> 4%
where the time goes in v2:
time: 787 us; the launch traced here: 773 us
  waiting for transfers between devices  343 us (44%)
  Pallas kernels  128 us (16%)
  starting transfers between devices  126 us (16%)
  other arithmetic  72.3 us (9%)
  local copies, waits for them, and re-layouts  50.8 us (6%)
  matrix products  49 us (6%)
    ppermute x91, waiting for transfers between devices, shift(): return lax.ppermute(value, 'ctx', pairs)  229 us
    ppermute x26, waiting for transfers between devices, shift(): return lax.ppermute(value, 'fsdp', pairs)  111 us
    ppermute x91, starting transfers between devices, shift(): return lax.ppermute(value, 'ctx', pairs)  82.6 us
    pallas_call x3, Pallas kernels, orthogonalize(): pl.pallas_call(chain_kernel, out_shape=jax.ShapeDtypeStruct(start.shape,...  59.5 us
    pallas_call x4, Pallas kernels, compute(): pl.pallas_call(kernel, out_shape=[jax.ShapeDtypeStruct(shape, dtype) for...  50.1 us
    ppermute x26, starting transfers between devices, shift(): return lax.ppermute(value, 'fsdp', pairs)  39.4 us
    unnamed x191, local copies, waits for them, and re-layouts  25.8 us
    pallas_call x3, Pallas kernels, gram_packed(): pl.pallas_call(gram_kernel, out_shape=jax.ShapeDtypeStruct((height, TILE)...  18.8 us
  transfers between devices with their start and end apart: 122, of which 60 were waited for; matrix products, arithmetic and copies ran while one was open for 16% of the time, Pallas kernels for 4%

profile of v2, /device:TPU:0, one launch (start us, length us, event | category | flops | bytes accessed | tf_op | source)
XLA Modules:
  0.0 772.8 jit_solution(7344052618341788051)
XLA Ops:
  42.2 11.4 %collective-permute-done.10 = bf16[48,2048]{1,0:T(8,128)(2,1)S(1)} collective-permute-done((bf16[48,2048]{1,0:T(8,128)(2,1)S(1)}, bf16[48,2048]{1,0:T(8,128)(2,1)S(1)}, u32[]{:S(2)}, u32[]{:S(2)}) %collective-permute-start.10) | collective-permute-done | bytes 196640 | tf_op jit(solution)/shard_map/ppermute | solution.py:86
  127.5 8.1 %collective-permute-done.37 = bf16[128,1536]{1,0:T(8,128)(2,1)S(1)} collective-permute-done((bf16[128,1536]{1,0:T(8,128)(2,1)S(1)}, bf16[128,1536]{1,0:T(8,128)(2,1)S(1)}, u32[]{:S(2)}, u32[]{:S(2)}) %collective-permute-start.37) | collective-permute-done | bytes 393248 | tf_op jit(solution)/shard_map/ppermute | solution.py:86
  177.8 12.9 %shard_map.474 = (f32[128,1536]{1,0:T(8,128)}, f32[128,128]{1,0:T(8,128)}, bf16[128,1536]{1,0:T(8,128)(2,1)}, f32[128,1536]{1,0:T(8,128)}, bf16[128,1536]{1,0:T(8,128)(2,1)}) custom-call(bf16[128,1536]{1,0:T(8,128)(2,1)} %bitcast.132, bf16[2,1536]{1,0:T(2,128)(2,1)} %gains_ref.7, bf16[1536,1536]{1,0:T(8,128)(2,1)} %fusion.reorder_ref, ...), custom_call_target="tpu_custom_call" | custom-call | flops 1207959552 | bytes 1048576 | tf_op jit(solution)/shard_map/pallas_call | solution.py:227
  220.3 9.3 %collective-permute-done.51 = bf16[128,1536]{1,0:T(8,128)(2,1)S(1)} collective-permute-done((bf16[128,1536]{1,0:T(8,128)(2,1)S(1)}, bf16[128,1536]{1,0:T(8,128)(2,1)S(1)}, u32[]{:S(2)}, u32[]{:S(2)}) %collective-permute-start.51) | collective-permute-done | bytes 393248 | tf_op jit(solution)/shard_map/ppermute | solution.py:86
  229.8 9.8 %pad_maximum_fusion = bf16[3360,1536]{1,0:T(8,128)(2,1)S(1)} fusion(bf16[1680,1536]{1,0:T(8,128)(2,1)} %collective-permute-done.35, bf16[1680,1536]{1,0:T(8,128)(2,1)S(1)} %pad_maximum_fusion.1), kind=kLoop, calls=%fused_computation.2 | loop fusion | flops 20643840 | bytes 20643840 | tf_op jit(solution)/shard_map/concatenate | solution.py:645
  286.1 12.7 %collective-permute-done.58.refs_1_ = bf16[128,1536]{1,0:T(8,128)(2,1)} collective-permute-done((bf16[128,1536]{1,0:T(8,128)(2,1)S(1)}, bf16[128,1536]{1,0:T(8,128)(2,1)}, u32[]{:S(2)}, u32[]{:S(2)}) %collective-permute-start.58) | collective-permute-done | bytes 393248 | tf_op jit(solution)/shard_map/ppermute | solution.py:73
  298.7 15.7 %shard_map.475 = (f32[128,1536]{1,0:T(8,128)}, bf16[128,1536]{1,0:T(8,128)(2,1)}, f32[1,1536]{1,0:T(1,128)}, bf16[128,1536]{1,0:T(8,128)(2,1)}, bf16[256,512]{1,...) custom-call(bf16[128,1536]{1,0:T(8,128)(2,1)} %bitcast.142, ...), custom_call_target="tpu_custom_call" | custom-call | flops 1207959552 | bytes 1048576 | tf_op jit(solution)/shard_map/pallas_call | solution.py:227
  334.9 14.3 %shard_map.476 = (bf16[2,384,3584]{2,1,0:T(8,128)(2,1)}, bf16[2,384,3584]{2,1,0:T(8,128)(2,1)}, f32[128,1536]{1,0:T(8,128)}, f32[1,2048]{1,0:T(1,128)}, f32[1,1536]{1,0:T(1,128)}) custom-call(bf16[128,1536]{1,0:T(8,128)(2,1)} %bitcast.133, bf16[2,1536]{1,0:T(2,128)(2,1)} %gains_ref.7, bf16[1536,1536]{1,0:T(8,128)(2,1)} %fusion.reorder_ref, ...), custom_call_target="tpu_custom_call" | custom-call | flops 1610612736 | bytes 1048576 | tf_op jit(solution)/shard_map/pallas_call | solution.py:227
  384.2 7.5 collective-permute-done.66
  436.2 10.1 %collective-permute-done.78 = bf16[96,3584]{1,0:T(8,128)(2,1)S(1)} collective-permute-done((bf16[96,3584]{1,0:T(8,128)(2,1)S(1)}, bf16[96,3584]{1,0:T(8,128)(2,1)S(1)}, u32[]{:S(2)}, u32[]{:S(2)}) %collective-permute-start.78) | collective-permute-done | bytes 688160 | tf_op jit(solution)/shard_map/ppermute | solution.py:86
  449.0 8.2 %collective-permute-done.87 = bf16[280,1536]{1,0:T(8,128)(2,1)S(1)} collective-permute-done((bf16[280,1536]{1,0:T(8,128)(2,1)S(1)}, bf16[280,1536]{1,0:T(8,128)(2,1)S(1)}, u32[]{:S(2)}, u32[]{:S(2)}) %collective-permute-start.87) | collective-permute-done | bytes 860192 | tf_op jit(solution)/shard_map/ppermute | solution.py:73
  468.6 9.2 %collective-permute-done.85 = bf16[280,1536]{1,0:T(8,128)(2,1)S(1)} collective-permute-done((bf16[280,1536]{1,0:T(8,128)(2,1)S(1)}, bf16[280,1536]{1,0:T(8,128)(2,1)S(1)}, u32[]{:S(2)}, u32[]{:S(2)}) %collective-permute-start.85) | collective-permute-done | bytes 860192 | tf_op jit(solution)/shard_map/ppermute | solution.py:73
  483.0 16.1 %collective-permute-done.80 = bf16[48,3584]{1,0:T(8,128)(2,1)S(1)} collective-permute-done((bf16[48,3584]{1,0:T(8,128)(2,1)S(1)}, bf16[48,3584]{1,0:T(8,128)(2,1)S(1)}, u32[]{:S(2)}, u32[]{:S(2)}) %collective-permute-start.80) | collective-permute-done | bytes 344096 | tf_op jit(solution)/shard_map/ppermute | solution.py:73
  513.7 9.8 %collective-permute-done.102 = bf16[280,1536]{1,0:T(8,128)(2,1)S(1)} collective-permute-done((bf16[280,1536]{1,0:T(8,128)(2,1)S(1)}, bf16[280,1536]{1,0:T(8,128)(2,1)S(1)}, u32[]{:S(2)}, u32[]{:S(2)}) %collective-permute-start.102) | collective-permute-done | bytes 860192 | tf_op jit(solution)/shard_map/ppermute | solution.py:86
  523.5 16.2 %collective-permute-done.103 = bf16[280,1536]{1,0:T(8,128)(2,1)S(1)} collective-permute-done((bf16[280,1536]{1,0:T(8,128)(2,1)S(1)}, bf16[280,1536]{1,0:T(8,128)(2,1)S(1)}, u32[]{:S(2)}, u32[]{:S(2)}) %collective-permute-start.103) | collective-permute-done | bytes 860192 | tf_op jit(solution)/shard_map/ppermute | solution.py:86
  564.1 21.4 %collective-permute-done.94 = bf16[96,1792]{1,0:T(8,128)(2,1)S(1)} collective-permute-done((bf16[96,1792]{1,0:T(8,128)(2,1)S(1)}, bf16[96,1792]{1,0:T(8,128)(2,1)S(1)}, u32[]{:S(2)}, u32[]{:S(2)}) %collective-permute-start.94) | collective-permute-done | bytes 344096 | tf_op jit(solution)/shard_map/ppermute | solution.py:86
  597.7 23.7 %collective-permute-done.107 = bf16[672,256]{1,0:T(8,128)(2,1)S(1)} collective-permute-done((bf16[672,256]{1,0:T(8,128)(2,1)S(1)}, bf16[672,256]{1,0:T(8,128)(2,1)S(1)}, u32[]{:S(2)}, u32[]{:S(2)}) %collective-permute-start.107) | collective-permute-done | bytes 344096 | tf_op jit(solution)/shard_map/ppermute | solution.py:73
  625.9 8.9 %collective-permute-done.109 = bf16[672,256]{1,0:T(8,128)(2,1)S(1)} collective-permute-done((bf16[672,256]{1,0:T(8,128)(2,1)S(1)}, bf16[672,256]{1,0:T(8,128)(2,1)S(1)}, u32[]{:S(2)}, u32[]{:S(2)}) %collective-permute-start.109) | collective-permute-done | bytes 344096 | tf_op jit(solution)/shard_map/ppermute | solution.py:73
  634.7 12.6 %collective-permute-done.110 = bf16[672,256]{1,0:T(8,128)(2,1)S(1)} collective-permute-done((bf16[672,256]{1,0:T(8,128)(2,1)S(1)}, bf16[672,256]{1,0:T(8,128)(2,1)S(1)}, u32[]{:S(2)}, u32[]{:S(2)}) %collective-permute-start.110) | collective-permute-done | bytes 344096 | tf_op jit(solution)/shard_map/ppermute | solution.py:73
  653.0 33.5 %shard_map.478 = bf16[1120,1536]{1,0:T(8,128)(2,1)} custom-call(bf16[5376,256]{1,0:T(8,128)(2,1)} %maximum_select_fusion.packed_ref, bf16[1120,1536]{1,0:T(8,128)(2,1)} %pad_maximum_fusion.2.start_ref), custom_call_target="tpu_custom_call" | custom-call | flops 28689039360 | bytes 12386304 | tf_op jit(solution)/shard_map/pallas_call | solution.py:511
  690.2 9.2 %shard_map.479.packed_ref = f32[5376,256]{1,0:T(8,128)} custom-call(bf16[1536,1536]{1,0:T(8,128)(2,1)} %slice.445.start_ref), custom_call_target="tpu_custom_call" | custom-call | flops 3623878656 | bytes 10223616 | tf_op jit(solution)/shard_map/pallas_call | solution.py:446
  701.7 23.4 %shard_map.480 = bf16[96,1536]{1,0:T(8,128)(2,1)} custom-call(f32[5376,256]{1,0:T(8,128)} %shard_map.479.packed_ref, bf16[96,1536]{1,0:T(8,128)(2,1)} %fusion.12.start_ref), custom_call_target="tpu_custom_call" | custom-call | flops 19025362944 | bytes 6094848 | tf_op jit(solution)/shard_map/pallas_call | solution.py:511
  735.5 15.6 %collective-permute-done.114 = bf16[280,1536]{1,0:T(8,128)(2,1)S(1)} collective-permute-done((bf16[280,1536]{1,0:T(8,128)(2,1)S(1)}, bf16[280,1536]{1,0:T(8,128)(2,1)S(1)}, u32[]{:S(2)}, u32[]{:S(2)}) %collective-permute-start.114) | collective-permute-done | bytes 860192 | tf_op jit(solution)/shard_map/ppermute | solution.py:86
  751.2 18.2 %collective-permute-done.115 = bf16[280,1536]{1,0:T(8,128)(2,1)S(1)} collective-permute-done((bf16[280,1536]{1,0:T(8,128)(2,1)S(1)}, bf16[280,1536]{1,0:T(8,128)(2,1)S(1)}, u32[]{:S(2)}, u32[]{:S(2)}) %collective-permute-start.115) | collective-permute-done | bytes 860192 | tf_op jit(solution)/shard_map/ppermute | solution.py:86
  (598 shorter events, 431.4 us)
Async XLA Ops:
  23.2 51.3 %collective-permute-start.17 = (bf16[48,1536]{1,0:T(8,128)(2,1)}, bf16[48,1536]{1,0:T(8,128)(2,1)S(1)}, u32[]{:S(2)}, u32[]{:S(2)}) collective-permute-start(bf16[48,1536]{1,0:T(8,128)(2,1)} %param.32), channel_id=1, source_target_pairs={{0,1},{1,2},{2,3},{3,0},{4,5},{5,6},{6,7},{7,4},{8,9},{9,10},{10,1... | collective-permute-start | bytes 442376 | tf_op jit(solution)/shard_map/ppermute | solution.py:73
  33.4 41.1 %collective-permute-start.18 = (bf16[48,1536]{1,0:T(8,128)(2,1)}, bf16[48,1536]{1,0:T(8,128)(2,1)S(1)}, u32[]{:S(2)}, u32[]{:S(2)}) collective-permute-start(bf16[48,1536]{1,0:T(8,128)(2,1)} %param.32), channel_id=1, source_target_pairs={{0,2},{1,3},{2,0},{3,1},{4,6},{5,7},{6,4},{7,5},{8,10},{9,11},{10,... | collective-permute-start | bytes 442376 | tf_op jit(solution)/shard_map/ppermute | solution.py:73
  53.6 109.8 %collective-permute-start.34 = (bf16[840,1536]{1,0:T(8,128)(2,1)S(1)}, bf16[840,1536]{1,0:T(8,128)(2,1)}, u32[]{:S(2)}, u32[]{:S(2)}) collective-permute-start(bf16[840,1536]{1,0:T(8,128)(2,1)S(1)} %pad_maximum_fusion.4), channel_id=1, source_target_pairs={{0,1},{1,0},{2,3},{3,2},{4,5},{5,4},{6,7},{7,6},{8,9},{9,8},{10,11... | collective-permute-start | bytes 7741448 | tf_op jit(solution)/shard_map/ppermute | solution.py:73
  67.4 82.4 %collective-permute-start.12 = (bf16[384,2048]{1,0:T(8,128)(2,1)S(1)}, bf16[384,2048]{1,0:T(8,128)(2,1)S(1)}, u32[]{:S(2)}, u32[]{:S(2)}) collective-permute-start(bf16[384,2048]{1,0:T(8,128)(2,1)S(1)} %constant_dynamic-update-slice_fusion.11.refs_2_), channel_id=1, source_target_pairs={{0,4},{4,0},{8,12},{12,8},{16,20},{20,16},{24,28},{28,24},{1,5},{5... | collective-permute-start | bytes 4718600 | tf_op jit(solution)/shard_map/ppermute | solution.py:86
  74.5 75.3 %collective-permute-start.6 = (bf16[384,2048]{1,0:T(8,128)(2,1)}, bf16[384,2048]{1,0:T(8,128)(2,1)S(1)}, u32[]{:S(2)}, u32[]{:S(2)}) collective-permute-start(bf16[384,2048]{1,0:T(8,128)(2,1)} %constant_dynamic-update-slice_fusion.3.refs_0_), channel_id=1, source_target_pairs={{0,4},{4,0},{8,12},{12,8},{16,20},{20,16},{24,28},{28,24},{1,5},{5... | collective-permute-start | bytes 4718600 | tf_op jit(solution)/shard_map/ppermute | solution.py:86
  167.0 62.8 %collective-permute-start.35 = (bf16[1680,1536]{1,0:T(8,128)(2,1)S(1)}, bf16[1680,1536]{1,0:T(8,128)(2,1)}, u32[]{:S(2)}, u32[]{:S(2)}) collective-permute-start(bf16[1680,1536]{1,0:T(8,128)(2,1)S(1)} %pad_maximum_fusion.1), channel_id=1, source_target_pairs={{0,4},{4,0},{8,12},{12,8},{16,20},{20,16},{24,28},{28,24},{1,5},{5... | collective-permute-start | bytes 15482888 | tf_op jit(solution)/shard_map/ppermute | solution.py:86
  356.0 38.1 %collective-permute-start.88 = (bf16[560,1536]{1,0:T(8,128)(2,1)}, bf16[560,1536]{1,0:T(8,128)(2,1)}, u32[]{:S(2)}, u32[]{:S(2)}) collective-permute-start(bf16[560,1536]{1,0:T(8,128)(2,1)} %slice.654), channel_id=1, source_target_pairs={{0,4},{4,0},{8,12},{12,8},{16,20},{20,16},{24,28},{28,24},{1,5},{5... | collective-permute-start | bytes 5160968 | tf_op jit(solution)/shard_map/ppermute | solution.py:86
  360.5 36.4 %collective-permute-start.86 = (bf16[560,1536]{1,0:T(8,128)(2,1)}, bf16[560,1536]{1,0:T(8,128)(2,1)}, u32[]{:S(2)}, u32[]{:S(2)}) collective-permute-start(bf16[560,1536]{1,0:T(8,128)(2,1)} %slice.655), channel_id=1, source_target_pairs={{0,4},{4,0},{8,12},{12,8},{16,20},{20,16},{24,28},{28,24},{1,5},{5... | collective-permute-start | bytes 5160968 | tf_op jit(solution)/shard_map/ppermute | solution.py:86
  376.5 33.2 %collective-permute-start.72 = (bf16[2,384,3584]{2,1,0:T(8,128)(2,1)}, bf16[2,384,3584]{2,1,0:T(8,128)(2,1)}, u32[]{:S(2)}, u32[]{:S(2)}) collective-permute-start(bf16[2,384,3584]{2,1,0:T(8,128)(2,1)} %get-tuple-element.102), channel_id=1, source_target_pairs={{0,4},{4,0},{8,12},{12,8},{16,20},{20,16},{24,28},{28,24},{1,5},{5... | collective-permute-start | bytes 16515080 | tf_op jit(solution)/shard_map/ppermute | solution.py:86
  434.1 43.7 %collective-permute-start.85 = (bf16[280,1536]{1,0:T(8,128)(2,1)S(1)}, bf16[280,1536]{1,0:T(8,128)(2,1)S(1)}, u32[]{:S(2)}, u32[]{:S(2)}) collective-permute-start(bf16[280,1536]{1,0:T(8,128)(2,1)S(1)} %copy-done.34), channel_id=1, source_target_pairs={{0,1},{1,0},{2,3},{3,2},{4,5},{5,4},{6,7},{7,6},{8,9},{9,8},{10,11... | collective-permute-start | bytes 2580488 | tf_op jit(solution)/shard_map/ppermute | solution.py:73
  435.3 73.3 %collective-permute-start.70 = (bf16[128,1536]{1,0:T(8,128)(2,1)S(1)}, bf16[128,1536]{1,0:T(8,128)(2,1)S(1)}, u32[]{:S(2)}, u32[]{:S(2)}) collective-permute-start(bf16[128,1536]{1,0:T(8,128)(2,1)S(1)} %pad_maximum_fusion.25), channel_id=1, source_target_pairs={{0,2},{1,3},{2,0},{3,1},{4,6},{5,7},{6,4},{7,5},{8,10},{9,11},{10,... | collective-permute-start | bytes 1179656 | tf_op jit(solution)/shard_map/ppermute | solution.py:73
  503.2 36.5 %collective-permute-start.103 = (bf16[280,1536]{1,0:T(8,128)(2,1)S(1)}, bf16[280,1536]{1,0:T(8,128)(2,1)S(1)}, u32[]{:S(2)}, u32[]{:S(2)}) collective-permute-start(bf16[280,1536]{1,0:T(8,128)(2,1)S(1)} %get-tuple-element.171), channel_id=1, source_target_pairs={{0,16},{4,20},{16,0},{20,4},{24,8},{28,12},{1,17},{5,21},{17,1},{2... | collective-permute-start | bytes 2580488 | tf_op jit(solution)/shard_map/ppermute | solution.py:86
  505.2 36.3 %collective-permute-start.104 = (bf16[280,1536]{1,0:T(8,128)(2,1)S(1)}, bf16[280,1536]{1,0:T(8,128)(2,1)S(1)}, u32[]{:S(2)}, u32[]{:S(2)}) collective-permute-start(bf16[280,1536]{1,0:T(8,128)(2,1)S(1)} %get-tuple-element.170), channel_id=1, source_target_pairs={{8,16},{12,20},{16,8},{20,12},{24,0},{28,4},{9,17},{13,21},{17,9},... | collective-permute-start | bytes 2580488 | tf_op jit(solution)/shard_map/ppermute | solution.py:86
  510.0 45.3 %collective-permute-start.93 = (bf16[96,1792]{1,0:T(8,128)(2,1)S(1)}, bf16[96,1792]{1,0:T(8,128)(2,1)S(1)}, u32[]{:S(2)}, u32[]{:S(2)}) collective-permute-start(bf16[96,1792]{1,0:T(8,128)(2,1)S(1)} %pad_maximum_fusion.11), channel_id=1, source_target_pairs={{0,1},{1,2},{2,3},{3,0},{4,5},{5,6},{6,7},{7,4},{8,9},{9,10},{10,1... | collective-permute-start | bytes 1032200 | tf_op jit(solution)/shard_map/ppermute | solution.py:73
  511.0 44.0 %collective-permute-start.96 = (bf16[96,1792]{1,0:T(8,128)(2,1)S(1)}, bf16[96,1792]{1,0:T(8,128)(2,1)S(1)}, u32[]{:S(2)}, u32[]{:S(2)}) collective-permute-start(bf16[96,1792]{1,0:T(8,128)(2,1)S(1)} %pad_maximum_fusion.11), channel_id=1, source_target_pairs={{0,2},{1,3},{2,0},{3,1},{4,6},{5,7},{6,4},{7,5},{8,10},{9,11},{10,... | collective-permute-start | bytes 1032200 | tf_op jit(solution)/shard_map/ppermute | solution.py:73
  552.1 33.7 %collective-permute-start.105 = (bf16[2688,256]{1,0:T(8,128)(2,1)S(1)}, bf16[2688,256]{1,0:T(8,128)(2,1)S(1)}, u32[]{:S(2)}, u32[]{:S(2)}) collective-permute-start(bf16[2688,256]{1,0:T(8,128)(2,1)S(1)} %constant_dynamic-slice_fusion.3), channel_id=1, source_target_pairs={{0,4},{4,0},{8,12},{12,8},{16,20},{20,16},{24,28},{28,24},{1,5},{5... | collective-permute-start | bytes 4128776 | tf_op jit(solution)/shard_map/ppermute | solution.py:86
  552.9 38.8 %collective-permute-start.92 = (bf16[192,1792]{1,0:T(8,128)(2,1)S(1)}, bf16[192,1792]{1,0:T(8,128)(2,1)S(1)}, u32[]{:S(2)}, u32[]{:S(2)}) collective-permute-start(bf16[192,1792]{1,0:T(8,128)(2,1)S(1)} %pad_maximum_fusion.7), channel_id=1, source_target_pairs={{0,16},{4,20},{8,24},{12,28},{16,0},{20,4},{24,8},{28,12},{1,17},{... | collective-permute-start | bytes 2064392 | tf_op jit(solution)/shard_map/ppermute | solution.py:86
  555.0 30.8 %collective-permute-start.97 = (bf16[96,1792]{1,0:T(8,128)(2,1)S(1)}, bf16[96,1792]{1,0:T(8,128)(2,1)S(1)}, u32[]{:S(2)}, u32[]{:S(2)}) collective-permute-start(bf16[96,1792]{1,0:T(8,128)(2,1)S(1)} %collective-permute-done.96), channel_id=1, source_target_pairs={{0,8},{4,12},{8,0},{12,4},{16,24},{20,28},{24,16},{28,20},{1,9},{5... | collective-permute-start | bytes 1032200 | tf_op jit(solution)/shard_map/ppermute | solution.py:86
  563.8 83.9 %collective-permute-start.101 = (bf16[192,1792]{1,0:T(8,128)(2,1)S(1)}, bf16[192,1792]{1,0:T(8,128)(2,1)S(1)}, u32[]{:S(2)}, u32[]{:S(2)}) collective-permute-start(bf16[192,1792]{1,0:T(8,128)(2,1)S(1)} %pad_maximum_fusion.10), channel_id=1, source_target_pairs={{0,8},{4,12},{8,0},{12,4},{16,24},{20,28},{24,16},{28,20},{1,9},{5... | collective-permute-start | bytes 2064392 | tf_op jit(solution)/shard_map/ppermute | solution.py:86
  585.5 36.5 %collective-permute-start.95 = (bf16[192,1792]{1,0:T(8,128)(2,1)S(1)}, bf16[192,1792]{1,0:T(8,128)(2,1)S(1)}, u32[]{:S(2)}, u32[]{:S(2)}) collective-permute-start(bf16[192,1792]{1,0:T(8,128)(2,1)S(1)} %pad_maximum_fusion.8), channel_id=1, source_target_pairs={{0,8},{4,12},{8,0},{12,4},{16,24},{20,28},{24,16},{28,20},{1,9},{5... | collective-permute-start | bytes 2064392 | tf_op jit(solution)/shard_map/ppermute | solution.py:86
  586.4 35.0 %collective-permute-start.107 = (bf16[672,256]{1,0:T(8,128)(2,1)S(1)}, bf16[672,256]{1,0:T(8,128)(2,1)S(1)}, u32[]{:S(2)}, u32[]{:S(2)}) collective-permute-start(bf16[672,256]{1,0:T(8,128)(2,1)S(1)} %get-tuple-element.191), channel_id=1, source_target_pairs={{0,2},{1,3},{2,0},{3,1},{4,6},{5,7},{6,4},{7,5},{8,10},{9,11},{10,... | collective-permute-start | bytes 1032200 | tf_op jit(solution)/shard_map/ppermute | solution.py:73
  597.4 50.2 %collective-permute-start.98 = (bf16[192,1792]{1,0:T(8,128)(2,1)S(1)}, bf16[192,1792]{1,0:T(8,128)(2,1)S(1)}, u32[]{:S(2)}, u32[]{:S(2)}) collective-permute-start(bf16[192,1792]{1,0:T(8,128)(2,1)S(1)} %pad_maximum_fusion.9), channel_id=1, source_target_pairs={{0,16},{4,20},{8,24},{12,28},{16,0},{20,4},{24,8},{28,12},{1,17},{... | collective-permute-start | bytes 2064392 | tf_op jit(solution)/shard_map/ppermute | solution.py:86
  729.8 39.5 %collective-permute-start.115 = (bf16[280,1536]{1,0:T(8,128)(2,1)S(1)}, bf16[280,1536]{1,0:T(8,128)(2,1)S(1)}, u32[]{:S(2)}, u32[]{:S(2)}) collective-permute-start(bf16[280,1536]{1,0:T(8,128)(2,1)S(1)} %get-tuple-element.167), channel_id=1, source_target_pairs={{0,16},{4,20},{8,24},{12,28},{16,0},{20,4},{24,8},{28,12},{1,17},{... | collective-permute-start | bytes 2580488 | tf_op jit(solution)/shard_map/ppermute | solution.py:86
  730.5 38.8 %collective-permute-start.116 = (bf16[280,1536]{1,0:T(8,128)(2,1)S(1)}, bf16[280,1536]{1,0:T(8,128)(2,1)S(1)}, u32[]{:S(2)}, u32[]{:S(2)}) collective-permute-start(bf16[280,1536]{1,0:T(8,128)(2,1)S(1)} %get-tuple-element.166), channel_id=1, source_target_pairs={{0,24},{4,28},{8,16},{12,20},{16,8},{20,12},{24,0},{28,4},{1,25},{... | collective-permute-start | bytes 2580488 | tf_op jit(solution)/shard_map/ppermute | solution.py:86
  (169 other events, 2082.3 us)

commit v3 on v2

--- a/solution.py
+++ b/solution.py
@@ -85,15 +85,20 @@
                         )
         return lax.ppermute(value, "ctx", pairs)
 
-    def plane_gather(self, block):
+    def gather_first(self, block):
         half = block.shape[0] // 2
         first, second = block[:half], block[half:]
-        first = jnp.concatenate(
-            [first] + [self.shift(first, dx=j) for j in range(1, self.x_count)]
+        return (
+            [first] + [self.shift(first, dx=j) for j in range(1, self.x_count)],
+            [second] + [self.shift(second, dy=j) for j in range(1, self.y_count)],
         )
-        second = jnp.concatenate(
-            [second] + [self.shift(second, dy=j) for j in range(1, self.y_count)]
-        )
+
+    def plane_gather(self, block, *others):
+        halves = self.gather_first(block)
+        return self.gather_second(*(after(halves, *others) if others else halves))
+
+    def gather_second(self, first, second):
+        first, second = jnp.concatenate(first), jnp.concatenate(second)
         return jnp.concatenate(
             [first]
             + [self.shift(first, dy=j) for j in range(1, self.y_count)]
@@ -114,7 +119,12 @@
                     jy.append(y), jx.append(x), row.append(r)
         return np.array(jy), np.array(jx), np.array(row)
 
-    def z_slots(self, block):
+    def z_slots(self, block, ring=False):
+        if ring:
+            slots = [block]
+            for _ in range(1, self.z_count):
+                slots.append(self.shift(slots[-1], dz=1))
+            return slots
         return [block] + [self.shift(block, dz=j) for j in range(1, self.z_count)]
 
     def gather(self, slots):
@@ -130,19 +140,28 @@
         jz = [k + row // rows for k in range(0, self.z_count, size)]
         return jz, jy, jx, row % rows
 
+    def step(self, rows, count, axis):
+        size = rows.shape[0] // count
+        total = rows[:size].astype(F32)
+        for j in range(1, count):
+            piece = rows[j * size : (j + 1) * size].astype(BF16)
+            total = total + self.shift(piece, **{axis: -j}).astype(F32)
+        return total
+
+    def reduce_first(self, part):
+        half = part.shape[0] // 2
+        return (
+            self.step(part[:half], self.y_count, "dy"),
+            self.step(part[half:], self.x_count, "dx"),
+        )
+
+    def reduce_second(self, first, second):
+        return jnp.concatenate(
+            [self.step(first, self.x_count, "dx"), self.step(second, self.y_count, "dy")]
+        )
+
     def plane_reduce(self, part):
-        def step(rows, count, axis):
-            size = rows.shape[0] // count
-            total = rows[:size].astype(F32)
-            for j in range(1, count):
-                piece = rows[j * size : (j + 1) * size].astype(BF16)
-                total = total + self.shift(piece, **{axis: -j}).astype(F32)
-            return total
-
-        half = part.shape[0] // 2
-        first = step(step(part[:half], self.y_count, "dy"), self.x_count, "dx")
-        second = step(step(part[half:], self.x_count, "dx"), self.y_count, "dy")
-        return jnp.concatenate([first, second])
+        return self.reduce_second(*self.reduce_first(part))
 
     def z_sum(self, parts):
         total = parts[0].astype(F32)
@@ -150,25 +169,29 @@
             total = total + self.shift(parts[j].astype(BF16), dz=-j).astype(F32)
         return total
 
-    def reduce_plane(self, parts):
+    def by_slot(self, totals):
         slots = []
-        for part in parts:
-            total = self.plane_reduce(part)
-            size = self.z_count // len(parts)
+        for total in totals:
+            size = self.z_count // len(totals)
             rows = total.shape[0] // size
             slots += [total[k * rows : (k + 1) * rows] for k in range(size)]
         return slots
 
-    def token_gather(self, block):
-        slots = [block] + [self.shift(block, dhigh=j) for j in range(1, self.z_count // 2)]
-        return [self.plane_gather(slot) for slot in slots]
-
-    def token_reduce(self, parts):
-        terms = [self.plane_reduce(parts[0])]
-        for j in range(1, len(parts)):
-            piece = self.plane_reduce(parts[j]).astype(BF16)
-            terms.append(self.shift(piece, dhigh=-j))
-        return terms
+    def token_gather(self, block, *others):
+        slots = [block] + [
+            self.shift(block, dhigh=j) for j in range(1, self.z_count // 2)
+        ]
+        if others:
+            slots[1:] = after(slots[1:], *others)
+        return [self.plane_gather(slots[0], *others)] + [
+            self.plane_gather(slot) for slot in slots[1:]
+        ]
+
+    def token_reduce(self, halves):
+        sums = [self.reduce_second(*half) for half in halves]
+        return sums[:1] + [
+            self.shift(sums[j].astype(BF16), dhigh=-j) for j in range(1, len(sums))
+        ]
 
     def total(self, value):
         for axis, count in (("ctx", self.y_count * self.x_count * CORES), ("fsdp", self.z_count)):
@@ -576,8 +599,12 @@
     qkv_chunks = grid.gather(qkv_slots)
     qkv_pieces = both_cores(qkv_chunks)
     output_slots = grid.z_slots(after(w_output, qkv_slots[-1]))
-    output_chunks = grid.gather(after(output_slots, *qkv_chunks))
-    output_pieces = both_cores(output_chunks)
+    output_first = output_slots[-1]
+    output_slots = after(output_slots, *qkv_chunks)
+    size = z_count // 2
+    output_halves = [
+        grid.gather_first(jnp.concatenate(output_slots[k : k + size])) for k in range(0, z_count, size)
+    ]
     tokens = after(tokens, qkv_slots[-1])
     place_y, place_x, place_c, place_z = after(
         (place_y, place_x, place_c, place_z), qkv_slots[-1]
@@ -597,6 +624,10 @@
     own_tokens = tokens[0]
     grad_mid = cotangent[0]
 
+    shared = 2 * CORES
+    ff_weights = after((w_gate, w_up, w_down), qkv_slots[-1], output_first)
+    ff_pairs = [grid.shift(weight, dpair=1) for weight in ff_weights]
+
     own_positions = (
         lax.dynamic_slice_in_dim(block_position, 2 * ctx_rank, 2)[:, None] * half_block
         + jnp.arange(half_block, dtype=jnp.int32)[None, :]
@@ -611,7 +642,7 @@
             ((shard_rows, 2 * key_value_width), BF16),
         ],
         [
-            own_tokens,
+            after(after(own_tokens, output_halves), ff_pairs[0]),
             norm_gains,
             projection_bias[None, :],
             cosine_lookup,
@@ -624,6 +655,13 @@
     key_value_pair = jnp.concatenate([key_value, grid.shift(key_value, dc=1)])
     places = [(jy_, jx_) for jy_ in range(y_count) for jx_ in range(x_count)]
     key_value_pieces = [grid.shift(key_value_pair, dy=a, dx=b) for a, b in places]
+    output_chunks = [grid.gather_second(*half) for half in output_halves]
+    output_pieces = both_cores(output_chunks)
+    ff_chips = [jnp.concatenate(pair) for pair in zip(ff_weights, ff_pairs)]
+    ff_others = [grid.shift(chip, dc=1) for chip in ff_chips]
+    gate_shared, up_shared, down_shared = (
+        jnp.concatenate(pair) for pair in zip(ff_chips, ff_others)
+    )
     key_ctx = jnp.stack(
         [
             (((place_y - a) % y_count) * x_count + (place_x - b) % x_count) * CORES
@@ -637,18 +675,6 @@
         + jnp.arange(half_block, dtype=jnp.int32)[None, None, :]
     ).reshape(1, shard_rows * ctx_count)
     seq_length = shard_rows * ctx_count
-
-    shared = 2 * CORES
-    ff_block = after(jnp.concatenate([w_gate, w_up, w_down]), qkv_slots[-1], output_slots[-1])
-    ff_chip = jnp.concatenate([ff_block, grid.shift(ff_block, dpair=1)])
-    ff_chip = after(ff_chip, key_value)
-    ff_all = jnp.concatenate([ff_chip, grid.shift(ff_chip, dc=1)])
-    ff_all = ff_all.reshape(shared, 3, ff_rows, width)
-    gate_shared, up_shared, down_shared = (
-        ff_all[:, k].reshape(shared * ff_rows, width) for k in range(3)
-    )
-
-    grad_chunks = grid.token_gather(after(grad_mid, output_chunks[-1]))
 
     mixed, log_total, attended_relative, hidden_one, normed_two = compute(
         functools.partial(attend_kernel, plane),
@@ -660,7 +686,7 @@
             ((shard_rows, width), BF16),
         ],
         [
-            own_tokens,
+            after(own_tokens, gate_shared, up_shared, down_shared),
             norm_gains,
             reorder,
             queries,
@@ -671,6 +697,10 @@
         ],
         4 * shard_rows * width * width,
         [pltpu.VMEM((seq_length, 2 * key_value_width), BF16)],
+    )
+
+    grad_chunks = grid.token_gather(
+        after(grad_mid, *key_value_pieces, output_chunks[-1]), normed_two
     )
 
     normed_chunks = grid.token_gather(normed_two)
@@ -695,19 +725,38 @@
         down_sum = down_sum + matmul_tn(hidden, grad_chunk)
         out_parts.append(matmul(hidden, down_shared).astype(BF16))
 
-    def own_rows(total):
-        chip_rows = 2 * ff_rows
-        other = grid.shift(total[chip_rows:].astype(BF16), dc=1)
-        chip_sum = total[:chip_rows] + other.astype(F32)
+    def chip_rows(total):
+        other = grid.shift(total[2 * ff_rows :].astype(BF16), dc=1)
+        return total[: 2 * ff_rows] + other.astype(F32)
+
+    def own_rows(chip_sum):
         piece = grid.shift(chip_sum[ff_rows:].astype(BF16), dpair=1)
         return chip_sum[:ff_rows] + piece.astype(F32)
 
-    grad_gate, grad_up, grad_down = own_rows(gate_sum), own_rows(up_sum), own_rows(down_sum)
+    chip_sums = [chip_rows(total) for total in (gate_sum, up_sum, down_sum)]
+    grad_gate, grad_up, grad_down = [own_rows(chip_sum) for chip_sum in chip_sums]
     moment_gate = MOMENTUM * momentum_gate + grad_gate
     moment_up = MOMENTUM * momentum_up + grad_up
     moment_down = MOMENTUM * momentum_down + grad_down
 
-    normed_grad_sums = grid.token_reduce(normed_grad_parts)
+    ff_start = jnp.stack([m.astype(BF16) for m in (moment_gate, moment_up, moment_down)])
+
+    ff_count = ff_start.shape[0]
+
+    def weight_at(a, b):
+        column = ((place_y + a) % y_count) * x_count + (place_x + b) % x_count
+        return lax.dynamic_index_in_dim(
+            ff_start, jnp.minimum(column, ff_count - 1), axis=0, keepdims=False
+        )
+
+    def has_weight(y, x):
+        return y * x_count + x < ff_count
+
+    shipped = [
+        grid.shift(weight_at(a, b), dy=a, dx=b, keep=has_weight) for a, b in places
+    ]
+
+    normed_grad_sums = grid.token_reduce([grid.reduce_first(part) for part in normed_grad_parts])
     hidden_grad, grad_branch, grad_gain_two, query_grad, *key_value_grads = compute(
         functools.partial(attend_back_kernel, plane, len(normed_grad_sums)),
         [
@@ -720,7 +769,7 @@
         [
             grad_mid,
             norm_gains,
-            hidden_one,
+            after(hidden_one, *chip_sums),
             reorder,
             queries,
             row_positions,
@@ -740,6 +789,7 @@
             pltpu.VMEM((seq_length, HEAD_DIM), F32),
         ],
     )
+    key_value_grads = after(key_value_grads, grad_gate)
     pair_grad = sum(
         grid.shift(piece, dy=-a, dx=-b).astype(F32)
         for piece, (a, b) in zip(key_value_grads, places)
@@ -775,21 +825,15 @@
         [pltpu.VMEM((shard_rows, qkv_width), BF16)],
     )
     other = grid.shift(weight_sent, dc=1)
+    other = after(other, ff_start)
     weight_sum = (weight_own.astype(F32) + other.astype(F32)).astype(BF16)
-    attention_slots = grid.reduce_plane([weight_sum[j] for j in range(2)])
+    attention_halves = [grid.reduce_first(weight_sum[j]) for j in range(2)]
+    attention_slots = grid.by_slot([grid.reduce_second(*halves) for halves in attention_halves])
     attention_grads = grid.z_sum(attention_slots)
     grad_query = attention_grads[:, :query_width]
     grad_key = attention_grads[:, query_width : query_width + key_value_width]
     grad_value = attention_grads[:, query_width + key_value_width : qkv_width]
     grad_output = attention_grads[:, qkv_width:]
-
-    vectors = grid.total(
-        jnp.concatenate([bias_term, grad_gain_one, grad_gain_two], axis=1).reshape(-1, HEAD_DIM)
-    ).reshape(-1)
-    grad_bias = vectors[:qkv_width]
-    grad_gains = vectors[qkv_width:].reshape(2, width)
-    moment_bias, update_bias = vector_step(bias_momentum, grad_bias)
-    moment_gains, update_gains = vector_step(momentum_gains, grad_gains)
 
     moment_query = MOMENTUM * momentum_query + grad_query
     moment_key = MOMENTUM * key_momentum + grad_key
@@ -800,32 +844,16 @@
     mine = jnp.where(place_c == 0, query_key, output_value)
     theirs = jnp.where(place_c == 0, output_value, query_key)
     pair_start = jnp.concatenate([mine, grid.shift(theirs, dc=1)])
-    start_slots = grid.z_slots(pair_start)
+    start_slots = grid.z_slots(pair_start, ring=True)
     start_all = jnp.concatenate(grid.gather(start_slots))
 
-    ff_start = jnp.stack([m.astype(BF16) for m in (moment_gate, moment_up, moment_down)])
-    ff_start = after(ff_start, *attention_slots)
-    ff_count = ff_start.shape[0]
-
-    def weight_at(a, b):
-        column = ((place_y + a) % y_count) * x_count + (place_x + b) % x_count
-        return lax.dynamic_index_in_dim(
-            ff_start, jnp.minimum(column, ff_count - 1), axis=0, keepdims=False
-        )
-
-    def has_weight(y, x):
-        return y * x_count + x < ff_count
-
-    current = jnp.concatenate(
-        [grid.shift(weight_at(a, b), dy=a, dx=b, keep=has_weight) for a, b in places]
-    )
-    current = after(current, pair_start)
+    current = jnp.concatenate(shipped)
     gram_part = gram_packed(current, BF16)
     half_rows = gram_part.shape[0] // CORES
     kept = lax.dynamic_slice_in_dim(gram_part, place_c * half_rows, half_rows)
     sent = lax.dynamic_slice_in_dim(gram_part, (1 - place_c) * half_rows, half_rows)
     gram_half = (kept.astype(F32) + grid.shift(sent, dc=1).astype(F32)).astype(BF16)
-    gram_half = after(gram_half, *start_slots)
+    gram_half = after(gram_half, weight_sum)
     z_rows = half_rows // z_count
     gram_own = grid.z_sum(
         [
@@ -833,24 +861,25 @@
             for j in range(z_count)
         ]
     ).astype(BF16)
+    gram_own = after(gram_own, *attention_halves)
     gram_half = jnp.zeros((half_rows, TILE), BF16)
-    for j, piece in enumerate(grid.z_slots(gram_own)):
+    for j, piece in enumerate(grid.z_slots(gram_own, ring=True)):
         gram_half = lax.dynamic_update_slice_in_dim(
             gram_half, piece, ((place_z - j) % z_count) * z_rows, axis=0
         )
+    gram_half = after(gram_half, *attention_slots)
     gram_other = grid.shift(gram_half, dc=1)
     gram = jnp.where(
         place_c == 0,
         jnp.concatenate([gram_half, gram_other]),
         jnp.concatenate([gram_other, gram_half]),
     )
-    moved = orthogonalize(after(gram, start_all), current)
-    back = jnp.stack(
-        [
-            grid.shift(moved[k * ff_rows : (k + 1) * ff_rows], dy=-a, dx=-b)
-            for k, (a, b) in enumerate(places)
-        ]
-    )
+    moved = orthogonalize(after(gram, *start_slots), current)
+    back_pieces = [
+        grid.shift(moved[k * ff_rows : (k + 1) * ff_rows], dy=-a, dx=-b)
+        for k, (a, b) in enumerate(places)
+    ]
+    back = jnp.stack(back_pieces)
 
     def ff_update(index):
         a = (index // x_count - place_y) % y_count
@@ -877,7 +906,18 @@
     update_output = scale * output_value_new[:, :width]
     update_value = kv_scale * output_value_new[:, width:]
 
-    out_terms = grid.token_reduce([after(part, pair_grad) for part in out_parts])
+    vectors = grid.total(
+        jnp.concatenate([bias_term, grad_gain_one, grad_gain_two], axis=1).reshape(-1, HEAD_DIM)
+    ).reshape(-1)
+    grad_bias = vectors[:qkv_width]
+    grad_gains = vectors[qkv_width:].reshape(2, width)
+    moment_bias, update_bias = vector_step(bias_momentum, grad_bias)
+    moment_gains, update_gains = vector_step(momentum_gains, grad_gains)
+
+    out_terms = grid.token_reduce(
+        [grid.reduce_first(after(part, gram_own)) for part in out_parts]
+    )
+    out_terms[1:] = after(out_terms[1:], moved)
     out_tokens = sum((term.astype(F32) for term in out_terms), hidden_one).astype(BF16)[None]
     return (
         out_tokens,

time: 787 us -> 721 us (0.916)
  waiting for transfers between devices: 343 us -> 283 us
    ppermute x91 -> x93, waiting for transfers between devices: 229 us -> 152 us  [shift(): return lax.ppermute(value, 'ctx', pairs)]
    ppermute x5, waiting for transfers between devices: 2.69 us -> 34.7 us  [total(): lax.ppermute(value, axis, [(k, k ^ step) for k in range(count)])]
    ppermute x26 -> x28, waiting for transfers between devices: 111 us -> 95.6 us  [shift(): return lax.ppermute(value, 'fsdp', pairs)]
    ppermute x26 -> x28, starting transfers between devices: 39.4 us -> 30.9 us  [shift(): return lax.ppermute(value, 'fsdp', pairs)]
    unnamed x191 -> x169, local copies, waits for them, and re-layouts: 25.8 us -> 19 us
    ppermute x91 -> x93, starting transfers between devices: 82.6 us -> 83.9 us  [shift(): return lax.ppermute(value, 'ctx', pairs)]
  transfers between devices with their start and end apart: 122 -> 126, of which waited for: 60 -> 48; matrix products, arithmetic and copies ran while one was open for 16% -> 21% of each run, Pallas kernels for 4% -> 18%
where the time goes in v3:
time: 721 us; the launch traced here: 710 us
  waiting for transfers between devices  283 us (39%)
  Pallas kernels  129 us (18%)
  starting transfers between devices  123 us (17%)
  other arithmetic  74.3 us (10%)
  local copies, waits for them, and re-layouts  52.2 us (7%)
  matrix products  44.8 us (6%)
    ppermute x93, waiting for transfers between devices, shift(): return lax.ppermute(value, 'ctx', pairs)  152 us
    ppermute x28, waiting for transfers between devices, shift(): return lax.ppermute(value, 'fsdp', pairs)  95.6 us
    ppermute x93, starting transfers between devices, shift(): return lax.ppermute(value, 'ctx', pairs)  83.9 us
    pallas_call x3, Pallas kernels, orthogonalize(): pl.pallas_call(chain_kernel, out_shape=jax.ShapeDtypeStruct(start.shape,...  59.5 us
    pallas_call x4, Pallas kernels, compute(): pl.pallas_call(kernel, out_shape=[jax.ShapeDtypeStruct(shape, dtype) for...  50.2 us
    ppermute x5, waiting for transfers between devices, total(): lax.ppermute(value, axis, [(k, k ^ step) for k in range(count)])  34.7 us
    ppermute x28, starting transfers between devices, shift(): return lax.ppermute(value, 'fsdp', pairs)  30.9 us
    unnamed x169, local copies, waits for them, and re-layouts  19 us
  transfers between devices with their start and end apart: 126, of which 48 were waited for; matrix products, arithmetic and copies ran while one was open for 21% of the time, Pallas kernels for 18%

profile of v3, /device:TPU:0, one launch (start us, length us, event | category | flops | bytes accessed | tf_op | source)
XLA Modules:
  0.0 709.7 jit_solution(5088304434316066173)
XLA Ops:
  42.1 8.2 %collective-permute-done.18 = bf16[48,2048]{1,0:T(8,128)(2,1)S(1)} collective-permute-done((bf16[48,2048]{1,0:T(8,128)(2,1)S(1)}, bf16[48,2048]{1,0:T(8,128)(2,1)S(1)}, u32[]{:S(2)}, u32[]{:S(2)}) %collective-permute-start.18) | collective-permute-done | bytes 196640 | tf_op jit(solution)/shard_map/ppermute | solution.py:86
  63.8 6.6 collective-permute-done.14
  97.0 7.1 %collective-permute-done.6 = bf16[280,1536]{1,0:T(8,128)(2,1)S(1)} collective-permute-done((bf16[280,1536]{1,0:T(8,128)(2,1)S(1)}, bf16[280,1536]{1,0:T(8,128)(2,1)S(1)}, u32[]{:S(2)}, u32[]{:S(2)}) %collective-permute-start.6) | collective-permute-done | bytes 860192 | tf_op jit(solution)/shard_map/ppermute | solution.py:73
  110.2 7.3 %shard_map.473 = (bf16[128,1536]{1,0:T(8,128)(2,1)}, bf16[128,1536]{1,0:T(8,128)(2,1)}, bf16[128,512]{1,0:T(8,128)(2,1)}) custom-call(bf16[128,1536]{1,0:T(8,128)(2,1)} %bitcast.116, bf16[2,1536]{1,0:T(2,128)(2,1)} %gains_ref.7, bf16[1,2048]{1,0:T(2,128)(2,1)} %broadcast_in_dim.14.bias_ref, f32[128,128]{1,0:T(8,128)} %get-tuple-element.257.cosine_ref, ...), custom_call_target="tpu_custom_call" | custom-call | flops 805306368 | bytes 1048576 | tf_op jit(solution)/shard_map/pallas_call | solution.py:250
  149.0 13.0 %shard_map.474 = (f32[128,1536]{1,0:T(8,128)}, f32[128,128]{1,0:T(8,128)}, bf16[128,1536]{1,0:T(8,128)(2,1)}, f32[128,1536]{1,0:T(8,128)}, bf16[128,1536]{1,0:T(8,128)(2,1)}) custom-call(bf16[128,1536]{1,0:T(8,128)(2,1)} %bitcast.117, bf16[2,1536]{1,0:T(2,128)(2,1)} %gains_ref.7, bf16[1536,1536]{1,0:T(8,128)(2,1)} %fusion.reorder_ref, ...), custom_call_target="tpu_custom_call" | custom-call | flops 1207959552 | bytes 1048576 | tf_op jit(solution)/shard_map/pallas_call | solution.py:250
  183.6 9.0 %collective-permute-done.45 = bf16[64,1536]{1,0:T(8,128)(2,1)S(1)} collective-permute-done((bf16[64,1536]{1,0:T(8,128)(2,1)S(1)}, bf16[64,1536]{1,0:T(8,128)(2,1)S(1)}, u32[]{:S(2)}, u32[]{:S(2)}) %collective-permute-start.45) | collective-permute-done | bytes 196640 | tf_op jit(solution)/shard_map/ppermute | solution.py:86
  278.5 10.3 %collective-permute-done.72.refs_1_ = bf16[128,1536]{1,0:T(8,128)(2,1)} collective-permute-done((bf16[128,1536]{1,0:T(8,128)(2,1)S(1)}, bf16[128,1536]{1,0:T(8,128)(2,1)}, u32[]{:S(2)}, u32[]{:S(2)}) %collective-permute-start.72) | collective-permute-done | bytes 393248 | tf_op jit(solution)/shard_map/ppermute | solution.py:73
  288.8 16.0 %shard_map.476 = (f32[128,1536]{1,0:T(8,128)}, bf16[128,1536]{1,0:T(8,128)(2,1)}, f32[1,1536]{1,0:T(1,128)}, bf16[128,1536]{1,0:T(8,128)(2,1)}, bf16[256,512]{1,...) custom-call(bf16[128,1536]{1,0:T(8,128)(2,1)} %bitcast.18.cotangent_ref, ...), custom_call_target="tpu_custom_call" | custom-call | flops 1207959552 | bytes 1048576 | tf_op jit(solution)/shard_map/pallas_call | solution.py:250
  330.6 14.0 %shard_map.477 = (bf16[2,384,3584]{2,1,0:T(8,128)(2,1)}, bf16[2,384,3584]{2,1,0:T(8,128)(2,1)}, f32[128,1536]{1,0:T(8,128)}, f32[1,2048]{1,0:T(1,128)}, f32[1,1536]{1,0:T(1,128)}) custom-call(bf16[128,1536]{1,0:T(8,128)(2,1)} %bitcast.118, bf16[2,1536]{1,0:T(2,128)(2,1)} %gains_ref.7, bf16[1536,1536]{1,0:T(8,128)(2,1)} %fusion.reorder_ref, ...), custom_call_target="tpu_custom_call" | custom-call | flops 1610612736 | bytes 1048576 | tf_op jit(solution)/shard_map/pallas_call | solution.py:250
  361.9 30.7 %collective-permute-done.122 = f32[40,128]{1,0:T(8,128)S(1)} collective-permute-done((f32[40,128]{1,0:T(8,128)S(1)}, f32[40,128]{1,0:T(8,128)S(1)}, u32[]{:S(2)}, u32[]{:S(2)}) %collective-permute-start.122) | collective-permute-done | bytes 20512 | tf_op jit(solution)/shard_map/ppermute | solution.py:200
  408.0 7.4 %shard_map.475 = bf16[5376,256]{1,0:T(8,128)(2,1)} custom-call(bf16[1120,1536]{1,0:T(8,128)(2,1)} %pad_maximum_fusion.start_ref), custom_call_target="tpu_custom_call" | custom-call | flops 2642411520 | bytes 8945664 | tf_op jit(solution)/shard_map/pallas_call | solution.py:469
  435.4 7.0 collective-permute-done.78
  442.4 13.8 %collective-permute-done.79 = bf16[672,256]{1,0:T(8,128)(2,1)S(1)} collective-permute-done((bf16[672,256]{1,0:T(8,128)(2,1)S(1)}, bf16[672,256]{1,0:T(8,128)(2,1)S(1)}, u32[]{:S(2)}, u32[]{:S(2)}) %collective-permute-start.79) | collective-permute-done | bytes 344096 | tf_op jit(solution)/shard_map/ppermute | solution.py:73
  457.1 10.7 %collective-permute-done.80 = bf16[672,256]{1,0:T(8,128)(2,1)S(1)} collective-permute-done((bf16[672,256]{1,0:T(8,128)(2,1)S(1)}, bf16[672,256]{1,0:T(8,128)(2,1)S(1)}, u32[]{:S(2)}, u32[]{:S(2)}) %collective-permute-start.80) | collective-permute-done | bytes 344096 | tf_op jit(solution)/shard_map/ppermute | solution.py:73
  473.5 6.3 collective-permute-done.98
  488.3 7.3 %collective-permute-done.85 = bf16[128,1536]{1,0:T(8,128)(2,1)S(1)} collective-permute-done((bf16[128,1536]{1,0:T(8,128)(2,1)S(1)}, bf16[128,1536]{1,0:T(8,128)(2,1)S(1)}, u32[]{:S(2)}, u32[]{:S(2)}) %collective-permute-start.85) | collective-permute-done | bytes 393248 | tf_op jit(solution)/shard_map/ppermute | solution.py:86
  526.6 14.6 %collective-permute-done.103 = bf16[48,3584]{1,0:T(8,128)(2,1)S(1)} collective-permute-done((bf16[48,3584]{1,0:T(8,128)(2,1)S(1)}, bf16[48,3584]{1,0:T(8,128)(2,1)S(1)}, u32[]{:S(2)}, u32[]{:S(2)}) %collective-permute-start.103) | collective-permute-done | bytes 344096 | tf_op jit(solution)/shard_map/ppermute | solution.py:73
  547.8 15.4 %collective-permute-done.106 = bf16[96,1792]{1,0:T(8,128)(2,1)S(1)} collective-permute-done((bf16[96,1792]{1,0:T(8,128)(2,1)S(1)}, bf16[96,1792]{1,0:T(8,128)(2,1)S(1)}, u32[]{:S(2)}, u32[]{:S(2)}) %collective-permute-start.106) | collective-permute-done | bytes 344096 | tf_op jit(solution)/shard_map/ppermute | solution.py:73
  565.5 9.1 %collective-permute-done.107 = bf16[96,1792]{1,0:T(8,128)(2,1)S(1)} collective-permute-done((bf16[96,1792]{1,0:T(8,128)(2,1)S(1)}, bf16[96,1792]{1,0:T(8,128)(2,1)S(1)}, u32[]{:S(2)}, u32[]{:S(2)}) %collective-permute-start.107) | collective-permute-done | bytes 344096 | tf_op jit(solution)/shard_map/ppermute | solution.py:73
  576.2 7.2 %collective-permute-done.113 = bf16[96,1792]{1,0:T(8,128)(2,1)S(1)} collective-permute-done((bf16[96,1792]{1,0:T(8,128)(2,1)S(1)}, bf16[96,1792]{1,0:T(8,128)(2,1)S(1)}, u32[]{:S(2)}, u32[]{:S(2)}) %collective-permute-start.113) | collective-permute-done | bytes 344096 | tf_op jit(solution)/shard_map/ppermute | solution.py:86
  590.1 20.5 %collective-permute-done.115 = bf16[96,1792]{1,0:T(8,128)(2,1)S(1)} collective-permute-done((bf16[96,1792]{1,0:T(8,128)(2,1)S(1)}, bf16[96,1792]{1,0:T(8,128)(2,1)S(1)}, u32[]{:S(2)}, u32[]{:S(2)}) %collective-permute-start.115) | collective-permute-done | bytes 344096 | tf_op jit(solution)/shard_map/ppermute | solution.py:86
  615.5 33.5 %shard_map.478 = bf16[1120,1536]{1,0:T(8,128)(2,1)} custom-call(bf16[5376,256]{1,0:T(8,128)(2,1)} %maximum_select_fusion.packed_ref, bf16[1120,1536]{1,0:T(8,128)(2,1)} %pad_maximum_fusion.start_ref), custom_call_target="tpu_custom_call" | custom-call | flops 28689039360 | bytes 12386304 | tf_op jit(solution)/shard_map/pallas_call | solution.py:534
  662.1 9.2 %shard_map.479.packed_ref = f32[5376,256]{1,0:T(8,128)} custom-call(bf16[1536,1536]{1,0:T(8,128)(2,1)} %slice.433.start_ref), custom_call_target="tpu_custom_call" | custom-call | flops 3623878656 | bytes 10223616 | tf_op jit(solution)/shard_map/pallas_call | solution.py:469
  673.6 23.3 %shard_map.480 = bf16[96,1536]{1,0:T(8,128)(2,1)} custom-call(f32[5376,256]{1,0:T(8,128)} %shard_map.479.packed_ref, bf16[96,1536]{1,0:T(8,128)(2,1)} %fusion.12.start_ref), custom_call_target="tpu_custom_call" | custom-call | flops 19025362944 | bytes 6094848 | tf_op jit(solution)/shard_map/pallas_call | solution.py:534
  (584 shorter events, 398.1 us)
Async XLA Ops:
  21.1 49.9 %collective-permute-start.8 = (bf16[48,1536]{1,0:T(8,128)(2,1)}, bf16[48,1536]{1,0:T(8,128)(2,1)S(1)}, u32[]{:S(2)}, u32[]{:S(2)}) collective-permute-start(bf16[48,1536]{1,0:T(8,128)(2,1)} %param.32), channel_id=1, source_target_pairs={{0,1},{1,2},{2,3},{3,0},{4,5},{5,6},{6,7},{7,4},{8,9},{9,10},{10,1... | collective-permute-start | bytes 442376 | tf_op jit(solution)/shard_map/ppermute | solution.py:73
  32.6 38.4 %collective-permute-start.9 = (bf16[48,1536]{1,0:T(8,128)(2,1)S(1)}, bf16[48,1536]{1,0:T(8,128)(2,1)S(1)}, u32[]{:S(2)}, u32[]{:S(2)}) collective-permute-start(bf16[48,1536]{1,0:T(8,128)(2,1)S(1)} %copy-done.29), channel_id=1, source_target_pairs={{0,2},{1,3},{2,0},{3,1},{4,6},{5,7},{6,4},{7,5},{8,10},{9,11},{10,... | collective-permute-start | bytes 442376 | tf_op jit(solution)/shard_map/ppermute | solution.py:73
  50.3 39.0 %collective-permute-start.2 = (bf16[280,1536]{1,0:T(8,128)(2,1)}, bf16[280,1536]{1,0:T(8,128)(2,1)S(1)}, u32[]{:S(2)}, u32[]{:S(2)}) collective-permute-start(bf16[280,1536]{1,0:T(8,128)(2,1)} %param.33), channel_id=1, source_target_pairs={{0,1},{1,0},{2,3},{3,2},{4,5},{5,4},{6,7},{7,6},{8,9},{9,8},{10,11... | collective-permute-start | bytes 2580488 | tf_op jit(solution)/shard_map/ppermute | solution.py:73
  138.8 35.4 %collective-permute-start.44 = (bf16[128,1536]{1,0:T(8,128)(2,1)}, bf16[128,1536]{1,0:T(8,128)(2,1)}, u32[]{:S(2)}, u32[]{:S(2)}) collective-permute-start(bf16[128,1536]{1,0:T(8,128)(2,1)} %bitcast.18.cotangent_ref), channel_id=1, source_target_pairs={{0,2},{1,3},{2,0},{3,1},{4,6},{5,7},{6,4},{7,5},{8,10},{9,11},{10,... | collective-permute-start | bytes 1179656 | tf_op jit(solution)/shard_map/ppermute | solution.py:73
  167.3 35.4 %collective-permute-start.43 = (bf16[128,1536]{1,0:T(8,128)(2,1)S(1)}, bf16[128,1536]{1,0:T(8,128)(2,1)S(1)}, u32[]{:S(2)}, u32[]{:S(2)}) collective-permute-start(bf16[128,1536]{1,0:T(8,128)(2,1)S(1)} %pad_maximum_fusion.19), channel_id=1, source_target_pairs={{0,8},{4,12},{8,0},{12,4},{16,24},{20,28},{24,16},{28,20},{1,9},{5... | collective-permute-start | bytes 1179656 | tf_op jit(solution)/shard_map/ppermute | solution.py:86
  173.2 36.4 %collective-permute-start.39 = (bf16[128,1536]{1,0:T(8,128)(2,1)S(1)}, bf16[128,1536]{1,0:T(8,128)(2,1)S(1)}, u32[]{:S(2)}, u32[]{:S(2)}) collective-permute-start(bf16[128,1536]{1,0:T(8,128)(2,1)S(1)} %pad_maximum_fusion.17), channel_id=1, source_target_pairs={{0,8},{4,12},{8,0},{12,4},{16,24},{20,28},{24,16},{28,20},{1,9},{5... | collective-permute-start | bytes 1179656 | tf_op jit(solution)/shard_map/ppermute | solution.py:86
  174.2 34.5 %collective-permute-start.37 = (bf16[128,1536]{1,0:T(8,128)(2,1)S(1)}, bf16[128,1536]{1,0:T(8,128)(2,1)S(1)}, u32[]{:S(2)}, u32[]{:S(2)}) collective-permute-start(bf16[128,1536]{1,0:T(8,128)(2,1)S(1)} %pad_maximum_fusion.16), channel_id=1, source_target_pairs={{0,16},{4,20},{8,24},{12,28},{16,0},{20,4},{24,8},{28,12},{1,17},{... | collective-permute-start | bytes 1179656 | tf_op jit(solution)/shard_map/ppermute | solution.py:86
  277.9 47.3 %collective-permute-start.57 = (bf16[280,1536]{1,0:T(8,128)(2,1)}, bf16[280,1536]{1,0:T(8,128)(2,1)}, u32[]{:S(2)}, u32[]{:S(2)}) collective-permute-start(bf16[280,1536]{1,0:T(8,128)(2,1)} %slice.639), channel_id=1, source_target_pairs={{0,1},{1,0},{2,3},{3,2},{4,5},{5,4},{6,7},{7,6},{8,9},{9,8},{10,11... | collective-permute-start | bytes 2580488 | tf_op jit(solution)/shard_map/ppermute | solution.py:73
  344.6 81.3 %collective-permute-start.77 = (bf16[2,384,3584]{2,1,0:T(8,128)(2,1)}, bf16[2,384,3584]{2,1,0:T(8,128)(2,1)}, u32[]{:S(2)}, u32[]{:S(2)}) collective-permute-start(bf16[2,384,3584]{2,1,0:T(8,128)(2,1)} %get-tuple-element.129), channel_id=1, source_target_pairs={{0,4},{4,0},{8,12},{12,8},{16,20},{20,16},{24,28},{28,24},{1,5},{5... | collective-permute-start | bytes 16515080 | tf_op jit(solution)/shard_map/ppermute | solution.py:86
  350.5 54.3 %collective-permute-start.60 = (bf16[280,1536]{1,0:T(8,128)(2,1)}, bf16[280,1536]{1,0:T(8,128)(2,1)}, u32[]{:S(2)}, u32[]{:S(2)}) collective-permute-start(bf16[280,1536]{1,0:T(8,128)(2,1)} %get-tuple-element.199), channel_id=1, source_target_pairs={{0,8},{4,12},{8,0},{12,4},{24,16},{28,20},{1,9},{5,13},{9,1},{13,5... | collective-permute-start | bytes 2580488 | tf_op jit(solution)/shard_map/ppermute | solution.py:86
  353.2 51.6 %collective-permute-start.61 = (bf16[280,1536]{1,0:T(8,128)(2,1)}, bf16[280,1536]{1,0:T(8,128)(2,1)}, u32[]{:S(2)}, u32[]{:S(2)}) collective-permute-start(bf16[280,1536]{1,0:T(8,128)(2,1)} %get-tuple-element.198), channel_id=1, source_target_pairs={{0,16},{4,20},{16,0},{20,4},{24,8},{28,12},{1,17},{5,21},{17,1},{2... | collective-permute-start | bytes 2580488 | tf_op jit(solution)/shard_map/ppermute | solution.py:86
  355.2 49.6 %collective-permute-start.62 = (bf16[280,1536]{1,0:T(8,128)(2,1)S(1)}, bf16[280,1536]{1,0:T(8,128)(2,1)}, u32[]{:S(2)}, u32[]{:S(2)}) collective-permute-start(bf16[280,1536]{1,0:T(8,128)(2,1)S(1)} %get-tuple-element.197), channel_id=1, source_target_pairs={{8,16},{12,20},{16,8},{20,12},{24,0},{28,4},{9,17},{13,21},{17,9},... | collective-permute-start | bytes 2580488 | tf_op jit(solution)/shard_map/ppermute | solution.py:86
  357.8 34.8 %collective-permute-start.122 = (f32[40,128]{1,0:T(8,128)S(1)}, f32[40,128]{1,0:T(8,128)S(1)}, u32[]{:S(2)}, u32[]{:S(2)}) collective-permute-start(f32[40,128]{1,0:T(8,128)S(1)} %add.690), channel_id=1, source_target_pairs={{0,8},{4,12},{8,0},{12,4},{16,24},{20,28},{24,16},{28,20},{1,9},{5... | collective-permute-start | bytes 61448 | tf_op jit(solution)/shard_map/ppermute | solution.py:200
  433.3 34.6 %collective-permute-start.81 = (bf16[96,3584]{1,0:T(8,128)(2,1)S(1)}, bf16[96,3584]{1,0:T(8,128)(2,1)S(1)}, u32[]{:S(2)}, u32[]{:S(2)}) collective-permute-start(bf16[96,3584]{1,0:T(8,128)(2,1)S(1)} %get-tuple-element.182), channel_id=1, source_target_pairs={{0,16},{4,20},{8,24},{12,28},{16,0},{20,4},{24,8},{28,12},{1,17},{... | collective-permute-start | bytes 2064392 | tf_op jit(solution)/shard_map/ppermute | solution.py:86
  471.1 51.8 %collective-permute-start.97 = (bf16[48,3584]{1,0:T(8,128)(2,1)S(1)}, bf16[48,3584]{1,0:T(8,128)(2,1)S(1)}, u32[]{:S(2)}, u32[]{:S(2)}) collective-permute-start(bf16[48,3584]{1,0:T(8,128)(2,1)S(1)} %slice.644), channel_id=1, source_target_pairs={{0,8},{4,12},{8,0},{12,4},{16,24},{20,28},{24,16},{28,20},{1,9},{5... | collective-permute-start | bytes 1032200 | tf_op jit(solution)/shard_map/ppermute | solution.py:86
  496.7 44.5 %collective-permute-start.103 = (bf16[48,3584]{1,0:T(8,128)(2,1)S(1)}, bf16[48,3584]{1,0:T(8,128)(2,1)S(1)}, u32[]{:S(2)}, u32[]{:S(2)}) collective-permute-start(bf16[48,3584]{1,0:T(8,128)(2,1)S(1)} %slice_add_fusion.7), channel_id=1, source_target_pairs={{0,2},{1,3},{2,0},{3,1},{4,6},{5,7},{6,4},{7,5},{8,10},{9,11},{10,... | collective-permute-start | bytes 1032200 | tf_op jit(solution)/shard_map/ppermute | solution.py:73
  501.8 39.4 %collective-permute-start.104 = (bf16[48,3584]{1,0:T(8,128)(2,1)S(1)}, bf16[48,3584]{1,0:T(8,128)(2,1)S(1)}, u32[]{:S(2)}, u32[]{:S(2)}) collective-permute-start(bf16[48,3584]{1,0:T(8,128)(2,1)S(1)} %slice_add_fusion.6), channel_id=1, source_target_pairs={{0,1},{1,2},{2,3},{3,0},{4,5},{5,6},{6,7},{7,4},{8,9},{9,10},{10,1... | collective-permute-start | bytes 1032200 | tf_op jit(solution)/shard_map/ppermute | solution.py:73
  524.3 130.0 %collective-permute-start.93 = (bf16[128,1536]{1,0:T(8,128)(2,1)}, bf16[128,1536]{1,0:T(8,128)(2,1)S(1)}, u32[]{:S(2)}, u32[]{:S(2)}) collective-permute-start(bf16[128,1536]{1,0:T(8,128)(2,1)} %pad_maximum_fusion.25), channel_id=1, source_target_pairs={{0,2},{1,3},{2,0},{3,1},{4,6},{5,7},{6,4},{7,5},{8,10},{9,11},{10,... | collective-permute-start | bytes 1179656 | tf_op jit(solution)/shard_map/ppermute | solution.py:73
  563.2 49.9 %collective-permute-start.101 = (bf16[2688,256]{1,0:T(8,128)(2,1)S(1)}, bf16[2688,256]{1,0:T(8,128)(2,1)S(1)}, u32[]{:S(2)}, u32[]{:S(2)}) collective-permute-start(bf16[2688,256]{1,0:T(8,128)(2,1)S(1)} %constant_dynamic-update-slice_fusion.77), channel_id=1, source_target_pairs={{0,4},{4,0},{8,12},{12,8},{16,20},{20,16},{24,28},{28,24},{1,5},{5... | collective-permute-start | bytes 4128776 | tf_op jit(solution)/shard_map/ppermute | solution.py:86
  586.5 69.7 %collective-permute-start.114 = (bf16[192,1792]{1,0:T(8,128)(2,1)}, bf16[192,1792]{1,0:T(8,128)(2,1)}, u32[]{:S(2)}, u32[]{:S(2)}) collective-permute-start(bf16[192,1792]{1,0:T(8,128)(2,1)} %pad_maximum_fusion.9), channel_id=1, source_target_pairs={{0,16},{4,20},{8,24},{12,28},{16,0},{20,4},{24,8},{28,12},{1,17},{... | collective-permute-start | bytes 2064392 | tf_op jit(solution)/shard_map/ppermute | solution.py:86
  611.5 45.9 %collective-permute-start.116 = (bf16[192,1792]{1,0:T(8,128)(2,1)}, bf16[192,1792]{1,0:T(8,128)(2,1)}, u32[]{:S(2)}, u32[]{:S(2)}) collective-permute-start(bf16[192,1792]{1,0:T(8,128)(2,1)} %pad_maximum_fusion.10), channel_id=1, source_target_pairs={{0,8},{4,12},{8,0},{12,4},{16,24},{20,28},{24,16},{28,20},{1,9},{5... | collective-permute-start | bytes 2064392 | tf_op jit(solution)/shard_map/ppermute | solution.py:86
  652.7 52.1 %collective-permute-start.118 = (bf16[280,1536]{1,0:T(8,128)(2,1)}, bf16[280,1536]{1,0:T(8,128)(2,1)}, u32[]{:S(2)}, u32[]{:S(2)}) collective-permute-start(bf16[280,1536]{1,0:T(8,128)(2,1)} %get-tuple-element.195), channel_id=1, source_target_pairs={{0,8},{4,12},{8,0},{12,4},{16,24},{20,28},{24,16},{28,20},{1,9},{5... | collective-permute-start | bytes 2580488 | tf_op jit(solution)/shard_map/ppermute | solution.py:86
  653.2 51.5 %collective-permute-start.119 = (bf16[280,1536]{1,0:T(8,128)(2,1)}, bf16[280,1536]{1,0:T(8,128)(2,1)}, u32[]{:S(2)}, u32[]{:S(2)}) collective-permute-start(bf16[280,1536]{1,0:T(8,128)(2,1)} %get-tuple-element.194), channel_id=1, source_target_pairs={{0,16},{4,20},{8,24},{12,28},{16,0},{20,4},{24,8},{28,12},{1,17},{... | collective-permute-start | bytes 2580488 | tf_op jit(solution)/shard_map/ppermute | solution.py:86
  654.3 50.5 %collective-permute-start.120 = (bf16[280,1536]{1,0:T(8,128)(2,1)}, bf16[280,1536]{1,0:T(8,128)(2,1)}, u32[]{:S(2)}, u32[]{:S(2)}) collective-permute-start(bf16[280,1536]{1,0:T(8,128)(2,1)} %get-tuple-element.193), channel_id=1, source_target_pairs={{0,24},{4,28},{8,16},{12,20},{16,8},{20,12},{24,0},{28,4},{1,25},{... | collective-permute-start | bytes 2580488 | tf_op jit(solution)/shard_map/ppermute | solution.py:86
  (159 other events, 2107.4 us)
